TPU v7x, 32 devices: a whole 2x2x4 slice. The times are simulated.
32 devices in a mesh: groups: 2 (over y), latent: 8 (over z, x), hidden: 2 (over core).
Axes of the slice: x: 2, y: 2, z: 4, core: 2. Of those that a mesh axis runs over, the one named last changes fastest.
Arguments:
- input_codes: int32 [288, 2304], P('groups', ('latent', 'hidden')), parts along dimension 0, may hold values from -128 to 127
- cotangent_codes: int32 [288, 2304], P('groups', ('latent', 'hidden')), parts along dimension 0, may hold values from -128 to 127
- dictionary: bfloat16 [8192, 2304], P(('latent', 'hidden')), as said below
- encoder_bias: float32 [8192], P(('latent', 'hidden')), may hold values from -12 to 0, as said below
- decoder_bias: float32 [2304], replicated, may hold values from -1.2 to 1.2
- norm_gain: float32 [2304], replicated, may hold values from 0.1 to 1.9
- gate_weight: bfloat16 [8192, 2304], P(('latent', 'hidden')), may hold values from -0.1875 to 0.1875
- up_weight: bfloat16 [8192, 2304], P(('latent', 'hidden')), may hold values from -0.1875 to 0.1875
- down_weight: bfloat16 [8192, 2304], P(('latent', 'hidden')), may hold values from -0.09375 to 0.09375
Outputs:
- block_output: bfloat16 [288, 2304], P('groups', ('latent', 'hidden')), parts along dimension 0
- dictionary_grad: bfloat16 [8192, 4608], P(('latent', 'hidden'), 'groups'), parts along dimension 1
There are 2 independent parts, one for each index of `groups`. A program takes and returns all parts, laid end to end along the dimension named above; an argument that names none is the same for every part. Nothing has to cross between parts.
Inputs may be any that keep to these rules, and one draw needn't show every extreme that they name: `dictionary`: every entry is a whole multiple of 2^-10, at most 119 such units in magnitude. `encoder_bias`: every entry is a whole multiple of 2^-16.
All inputs are finite; a program needn't handle non-finite values.
Results may differ from a plain program's by a relative error of at most 0.0072.
Values may be sent and summed in bfloat16 or wider, within the bound.
No kernel may reach another device: no remote copies, remote signals or barrier semaphores. Data moves between devices by JAX's collectives and lax.ppermute only.
A program may use at most 64 MiB of HBM per device.

v0:
```python
import functools
import math

import jax
import jax.numpy as jnp
from jax import lax
from jax.experimental import pallas as pl
from jax.experimental.pallas import tpu as pltpu
from jax.sharding import PartitionSpec as P

CODE_STEP = 2.0 ** (-6)
NORM_EPSILON = 1e-06
GELU_ROOT = 0.7978845608028654
GELU_CUBIC = 0.044715
ACROSS = (((1,), (1,)), ((), ()))
DOWNWARD = (((0,), (0,)), ((), ()))
LANES = 128
ROW_TILE = 16
DIRECT_LIMIT = 16
VMEM_BYTES = 24 * 1024 * 1024
VMEM_BRING = 53 * 1024 * 1024
F32 = jnp.float32
BF16 = jnp.bfloat16


def gelu_parts(values):
    argument = GELU_ROOT * (values + GELU_CUBIC * values * values * values)
    tanh_value = jnp.tanh(argument)
    result = 0.5 * values * (1.0 + tanh_value)
    derivative = 0.5 * (1.0 + tanh_value) + 0.5 * values * (
        1.0 - tanh_value * tanh_value
    ) * GELU_ROOT * (1.0 + 3.0 * GELU_CUBIC * values * values)
    return (result, derivative)


def up_to(value, unit):
    return -(-value // unit) * unit


def chips_fit(chips):
    return 8 <= chips <= DIRECT_LIMIT and chips & (chips - 1) == 0


class Plan:
    def __init__(self, chips, cores, rows, own):
        self.chips, self.cores, self.rows, self.own = chips, cores, rows, own
        self.width = own * chips * cores
        self.half = self.width // cores
        self.tiles = self.half // LANES
        self.chunk = up_to(-(-self.tiles * rows // chips), ROW_TILE)
        self.flat = self.chunk * chips
        self.tail = own - LANES
        if self.tail > 0:
            self.fold_rows = min(
                size
                for size in range(ROW_TILE, rows + ROW_TILE, ROW_TILE)
                if -(-rows // size) * self.tail <= LANES
            )
            self.packed = rows + self.fold_rows
        self.columns = list(range(0, chips, 2))
        self.doubling = [1 << k for k in reversed(range(1, (chips - 1).bit_length()))]
        self.doubled = [0]
        for bit in self.doubling:
            self.doubled = self.doubled + [place ^ bit for place in self.doubled]

    def side_blocks(self, refs):
        me = lax.axis_index("latent")
        stack_ref, *crossed_refs = refs
        for place, column in enumerate(self.columns):
            yield me ^ column, stack_ref[place]
        places = iter(self.columns)
        for ref in crossed_refs:
            for place in range(ref.shape[0]):
                yield me ^ next(places) ^ 1, ref[place]

    def pieces(self):
        for tile in range(self.tiles):
            row = 0
            while row < self.rows:
                chip, place = divmod(tile * self.rows + row, self.chunk)
                count = min(self.rows - row, self.chunk - place)
                yield tile, chip, place, row, count
                row += count

    def fits(self):
        return (
            self.cores == 2
            and chips_fit(self.chips)
            and self.rows % ROW_TILE == 0
            and self.half % LANES == 0
            and 0 < self.tail < LANES
            and self.packed == self.chunk
        )


HBM = pl.BlockSpec(memory_space=pltpu.HBM)
ONCHIP = pl.BlockSpec(memory_space=pltpu.VMEM)


def shaped(*dims, dtype=F32):
    return jax.ShapeDtypeStruct(dims, dtype)


HBM = pl.BlockSpec(memory_space=pltpu.HBM)
ONCHIP = pl.BlockSpec(memory_space=pltpu.VMEM)


def shaped(*dims, dtype=F32):
    return jax.ShapeDtypeStruct(dims, dtype)


def call(body, out_shapes, operands, scratch=(), out_specs=None, flops=0, moved=0):
    return pl.pallas_call(
        body,
        out_shape=out_shapes,
        in_specs=[ONCHIP] * len(operands),
        out_specs=jax.tree.map(lambda _: ONCHIP, out_shapes) if out_specs is None else out_specs,
        scratch_shapes=list(scratch),
        compiler_params=pltpu.CompilerParams(vmem_limit_bytes=VMEM_BYTES),
        cost_estimate=pl.CostEstimate(flops=flops, bytes_accessed=moved, transcendentals=0),
    )(*operands)


def padded_bytes(array):
    *lead, rows, columns = array.shape
    item = jnp.dtype(array.dtype).itemsize
    return math.prod(lead) * up_to(rows, ROW_TILE) * up_to(columns, LANES) * item


def copies(sources, targets, sems):
    started = []
    for index, (source, target) in enumerate(zip(sources, targets)):
        one = pltpu.make_async_copy(source, target, sems.at[index])
        one.start()
        started.append(one)
    return started


def pack_block(plan, block):
    tail = block[:, LANES:]
    folded = []
    for start in range(0, plan.rows, plan.fold_rows):
        piece = tail[start : min(start + plan.fold_rows, plan.rows), :]
        short = plan.fold_rows - piece.shape[0]
        if short:
            piece = jnp.concatenate([piece, jnp.zeros((short, plan.tail), block.dtype)], axis=0)
        folded.append(piece)
    fill = LANES - len(folded) * plan.tail
    if fill:
        folded.append(jnp.zeros((plan.fold_rows, fill), block.dtype))
    return block[:, :LANES], jnp.concatenate(folded, axis=1)


def unpack_block(plan, packed):
    pieces = []
    for fold, start in enumerate(range(0, plan.rows, plan.fold_rows)):
        count = min(plan.fold_rows, plan.rows - start)
        pieces.append(
            packed[plan.rows : plan.rows + count, fold * plan.tail : (fold + 1) * plan.tail]
        )
    return jnp.concatenate([packed[: plan.rows, :], jnp.concatenate(pieces, axis=0)], axis=1)


def pack_values_body(plan, values_ref, *block_refs):
    for index, block_ref in enumerate(block_refs):
        main, tail = pack_block(plan, values_ref[index].astype(F32))
        block_ref[0, : plan.rows, :] = main.astype(BF16)
        block_ref[0, plan.rows :, :] = tail.astype(BF16)


def pack_values(plan, values):
    return call(
        functools.partial(pack_values_body, plan),
        [shaped(1, plan.packed, LANES, dtype=BF16)] * values.shape[0],
        (values,),
        moved=values.size * 6,
    )


def assemble(plan, own_refs, other_refs, both, full_ref):
    core = lax.axis_index("hidden")
    for side, refs in ((core, own_refs), (1 - core, other_refs)):
        for chip, block in plan.side_blocks(refs):
            both[side, chip] = block
    for chip in range(plan.chips):
        for side in range(plan.cores):
            column = (chip * plan.cores + side) * plan.own
            full_ref[:, column : column + plan.own] = unpack_block(plan, both[side, chip])


def both_scratch(plan, dtype=BF16):
    return pltpu.VMEM((plan.cores, plan.chips, plan.packed, LANES), dtype)


def chunk_scratch(plan):
    return pltpu.VMEM((plan.chips, plan.chunk, LANES), F32)


def side_shapes(plan, dtype=F32):
    return [shaped(len(plan.columns), plan.chunk, LANES, dtype=dtype)] * 2


def half_product(plan, pairs, side, kept_ref, sent_ref, target, gain_ref=None, bias_ref=None):
    span = pl.ds(pl.multiple_of(side * plan.half, LANES), plan.half)
    total = None
    for left, right_ref in pairs:
        term = jnp.dot(left, right_ref[:, span], preferred_element_type=F32)
        total = term if total is None else total + term
    if bias_ref is not None:
        total = total + bias_ref[:, span] * jnp.where(lax.axis_index("latent") == 0, 1.0, 0.0)
    if gain_ref is not None:
        total = total * gain_ref[:, span]
    for tile, chip, place, row, count in plan.pieces():
        target[chip, place : place + count, :] = total[
            row : row + count, tile * LANES : (tile + 1) * LANES
        ]
    used = plan.tiles * plan.rows
    while used < plan.flat:
        chip, place = divmod(used, plan.chunk)
        target[chip, place:, :] = jnp.zeros((plan.chunk - place, LANES), F32)
        used += plan.chunk - place
    me = lax.axis_index("latent")
    for place, column in enumerate(plan.columns):
        kept_ref[place] = target[me ^ column]
        sent_ref[place] = target[me ^ column ^ 1]


def bring_encoder_body(dict_hbm, vectors_hbm, dict_ref, bias_ref, decoder_ref, gain_ref, sems):
    sources, targets = [dict_hbm], [dict_ref]
    start = 0
    for target in (bias_ref, decoder_ref, gain_ref):
        sources.append(vectors_hbm.at[:, start : start + target.shape[1]])
        targets.append(target)
        start += target.shape[1]
    for copy in copies(sources, targets, sems):
        copy.wait()


def bring_encoder(plan, dictionary, vectors):
    outputs = [
        shaped(*dictionary.shape, dtype=BF16),
        shaped(1, dictionary.shape[0]),
        shaped(1, plan.width),
        shaped(1, plan.width),
    ]
    return pl.pallas_call(
        bring_encoder_body,
        out_shape=outputs,
        in_specs=[HBM] * 2,
        out_specs=[ONCHIP] * len(outputs),
        scratch_shapes=[pltpu.SemaphoreType.DMA((len(outputs),))],
        compiler_params=pltpu.CompilerParams(
            vmem_limit_bytes=VMEM_BRING - sum(map(padded_bytes, outputs))
        ),
        cost_estimate=pl.CostEstimate(
            flops=0, bytes_accessed=dictionary.size * 4, transcendentals=0
        ),
    )(dictionary, vectors)


def encode_body(plan, *refs):
    own, other, (dict_ref, bias_ref, gain_ref) = refs[:2], refs[2:4], refs[4:7]
    inputs_ref, latents_ref, kept_ref, sent_ref, both, target = refs[7:]
    assemble(plan, own, other, both, inputs_ref)
    preact = (
        lax.dot_general(inputs_ref[...], dict_ref[...], ACROSS, preferred_element_type=F32)
        + bias_ref[...]
    )
    latents = jnp.maximum(preact, 0.0).astype(BF16)
    latents_ref[...] = latents
    theirs = 1 - lax.axis_index("hidden")
    half_product(plan, [(latents, dict_ref)], theirs, kept_ref, sent_ref, target, gain_ref)


def encode(plan, own, other, dictionary, encoder_bias, gain):
    latents = dictionary.shape[0]
    return call(
        functools.partial(encode_body, plan),
        [
            shaped(plan.rows, plan.width, dtype=BF16),
            shaped(plan.rows, latents, dtype=BF16),
            *side_shapes(plan),
        ],
        (*own, *other, dictionary, encoder_bias, gain),
        [both_scratch(plan), chunk_scratch(plan)],
        flops=3 * plan.rows * plan.width * latents,
        moved=dictionary.size * 2,
    )


def decode_own_body(plan, latents_ref, dict_ref, decoder_ref, gain_ref, kept_ref, sent_ref, target):
    pairs = [(latents_ref[...], dict_ref)]
    mine = lax.axis_index("hidden")
    half_product(plan, pairs, mine, kept_ref, sent_ref, target, gain_ref, decoder_ref)


def decode_own(plan, latents, dictionary, decoder_bias, gain):
    return call(
        functools.partial(decode_own_body, plan),
        side_shapes(plan),
        (latents, dictionary, decoder_bias, gain),
        [chunk_scratch(plan)],
        flops=plan.rows * plan.width * dictionary.shape[0],
        moved=dictionary.size,
    )


def back_project_body(plan, *refs):
    own, other, (down_ref, grad_ref, both, full) = refs[:2], refs[2:4], refs[4:]
    assemble(plan, own, other, both, full)
    grad_ref[...] = lax.dot_general(
        full[...], down_ref[...], ACROSS, preferred_element_type=F32
    )


def back_project(plan, own, other, down_weight):
    units = down_weight.shape[0]
    return call(
        functools.partial(back_project_body, plan),
        shaped(plan.rows, units),
        (*own, *other, down_weight),
        [both_scratch(plan), pltpu.VMEM((plan.rows, plan.width), BF16)],
        flops=2 * plan.rows * plan.width * units,
        moved=down_weight.size * 2,
    )


def join_half(plan, source, first, full_ref):
    for tile, chip, place, row, count in plan.pieces():
        column = pl.multiple_of(first + tile * LANES, LANES)
        full_ref[row : row + count, pl.ds(column, LANES)] = source[
            chip, place : place + count, :
        ]


def half_terms(plan, half, side, gate_ref, up_ref, gain_ref):
    span = pl.ds(pl.multiple_of(side * plan.half, LANES), plan.half)
    rebuilt = half.astype(F32) / gain_ref[:, span]
    squares = jnp.sum(rebuilt * rebuilt, axis=1, keepdims=True)
    gate = lax.dot_general(half, gate_ref[:, span], ACROSS, preferred_element_type=F32)
    up = lax.dot_general(half, up_ref[:, span], ACROSS, preferred_element_type=F32)
    return squares, gate, up


def mlp_first_body(plan, own_ref, gate_ref, up_ref, gain_ref, half_ref, squares_ref, gate_part_ref, up_part_ref):
    join_half(plan, own_ref, 0, half_ref)
    squares_ref[...], gate_part_ref[...], up_part_ref[...] = half_terms(
        plan, half_ref[...], lax.axis_index("hidden"), gate_ref, up_ref, gain_ref
    )


def mlp_first(plan, own, gate_weight, up_weight, gain):
    units = gate_weight.shape[0]
    return call(
        functools.partial(mlp_first_body, plan),
        [
            shaped(plan.rows, plan.half, dtype=BF16),
            shaped(plan.rows, 1),
            shaped(plan.rows, units),
            shaped(plan.rows, units),
        ],
        (own, gate_weight, up_weight, gain),
        flops=2 * plan.rows * plan.width * units,
        moved=gate_weight.size * 4,
    )


def mlp_body(plan, other_ref, gate_ref, up_ref, gain_ref, grad_ref, half_ref, squares_ref, gate_part_ref, up_part_ref, scaled_ref, inverse_ref, hidden_ref, gate_grad_ref, up_grad_ref, kept_ref, sent_ref, target):
    core = lax.axis_index("hidden")
    join_half(plan, other_ref, (1 - core) * plan.half, scaled_ref)
    other_span = pl.ds(pl.multiple_of((1 - core) * plan.half, LANES), plan.half)
    own_span = pl.ds(pl.multiple_of(core * plan.half, LANES), plan.half)
    scaled_ref[:, own_span] = half_ref[...]
    squares, gate, up = half_terms(
        plan, scaled_ref[:, other_span], 1 - core, gate_ref, up_ref, gain_ref
    )
    inverse = lax.rsqrt((squares + squares_ref[...]) / plan.width + NORM_EPSILON)
    inverse_ref[...] = inverse
    gate_proj = inverse * (gate + gate_part_ref[...])
    up_proj = inverse * (up + up_part_ref[...])
    gelu_value, gelu_slope = gelu_parts(gate_proj)
    hidden_ref[...] = (gelu_value * up_proj).astype(BF16)
    hidden_grad = grad_ref[...]
    gate_grad = (hidden_grad * up_proj * gelu_slope).astype(BF16)
    up_grad = (hidden_grad * gelu_value).astype(BF16)
    gate_grad_ref[...] = gate_grad
    up_grad_ref[...] = up_grad
    pairs = [(gate_grad, gate_ref), (up_grad, up_ref)]
    half_product(plan, pairs, 1 - core, kept_ref, sent_ref, target)


def mlp(plan, other, gate_weight, up_weight, gain, hidden_grad, first):
    units = gate_weight.shape[0]
    return call(
        functools.partial(mlp_body, plan),
        [
            shaped(plan.rows, plan.width, dtype=BF16),
            shaped(plan.rows, 1),
            shaped(plan.rows, units, dtype=BF16),
            shaped(plan.rows, units, dtype=BF16),
            shaped(plan.rows, units, dtype=BF16),
            *side_shapes(plan),
        ],
        (other, gate_weight, up_weight, gain, hidden_grad, *first),
        [chunk_scratch(plan)],
        flops=6 * plan.rows * plan.width * units,
        moved=gate_weight.size * 4,
    )


def mlp_own_body(plan, gate_grad_ref, up_grad_ref, gate_ref, up_ref, kept_ref, sent_ref, target):
    pairs = [(gate_grad_ref[...], gate_ref), (up_grad_ref[...], up_ref)]
    half_product(plan, pairs, lax.axis_index("hidden"), kept_ref, sent_ref, target)


def mlp_own(plan, gate_grad, up_grad, gate_weight, up_weight):
    return call(
        functools.partial(mlp_own_body, plan),
        side_shapes(plan),
        (gate_grad, up_grad, gate_weight, up_weight),
        [chunk_scratch(plan)],
        flops=2 * plan.rows * plan.width * gate_weight.shape[0],
        moved=gate_weight.size * 2,
    )


def project_body(plan, hidden_ref, down_ref, mine_ref, theirs_ref, both):
    core = lax.axis_index("hidden")
    terms = jnp.dot(hidden_ref[...], down_ref[...], preferred_element_type=F32).astype(BF16)
    for chip in range(plan.chips):
        for side in range(plan.cores):
            start = (chip * plan.cores + side) * plan.own
            main, tail = pack_block(plan, terms[:, start : start + plan.own])
            both[side, chip, : plan.rows, :] = main
            both[side, chip, plan.rows :, :] = tail
    mine_ref[...] = both[core]
    theirs_ref[...] = both[1 - core]


def project(plan, hidden, down_weight):
    units = down_weight.shape[0]
    shape = (plan.chips, plan.packed, LANES)
    return call(
        functools.partial(project_body, plan),
        [shaped(*shape, dtype=BF16)] * 2,
        (hidden, down_weight),
        [both_scratch(plan)],
        flops=2 * plan.rows * plan.width * units,
        moved=down_weight.size * 2,
    )


def add_pair_body(plan, first_ref, mine_ref, theirs_ref, kept_ref, sent_ref):
    me = lax.axis_index("latent")
    sent_ref[0] = first_ref[0]
    for place, column in enumerate(plan.columns):
        kept, sent = me ^ column, me ^ column ^ 1
        kept_ref[place] = mine_ref[kept].astype(F32) + theirs_ref[kept].astype(F32)
        sent_ref[1 + place] = (
            mine_ref[sent].astype(F32) + theirs_ref[sent].astype(F32)
        ).astype(BF16)


def add_pair(plan, first, mine, theirs):
    count, dims = len(plan.columns), mine.shape[1:]
    return call(
        functools.partial(add_pair_body, plan),
        [shaped(count, *dims), shaped(1 + count, *dims, dtype=BF16)],
        (first, mine, theirs),
        moved=mine.size * 10,
    )


def add_sent_body(mine_ref, theirs_ref, first_ref, rest_ref):
    total = (mine_ref[...] + theirs_ref[...]).astype(BF16)
    first_ref[...] = total[:1]
    rest_ref[...] = total[1:]


def add_sent(plan, mine, theirs):
    count, *dims = mine.shape
    return call(
        add_sent_body,
        [shaped(1, *dims, dtype=BF16), shaped(count - 1, *dims, dtype=BF16)],
        (mine, theirs),
        moved=mine.size * 10,
    )


def add_across_body(mine_ref, theirs_ref, got_ref, *sent_refs):
    for place, out_ref in enumerate(sent_refs):
        total = mine_ref[1 + place] + theirs_ref[1 + place] + got_ref[place].astype(F32)
        out_ref[0] = total.astype(BF16)


def add_across(plan, mine, theirs, got):
    return call(
        add_across_body,
        [shaped(1, *mine.shape[1:], dtype=BF16)] * got.shape[0],
        (mine, theirs, got),
        moved=mine.size * 10,
    )


def column_total(mine_ref, theirs_ref, *refs):
    total = mine_ref[0] + theirs_ref[0]
    for ref in refs:
        total = total + ref[0].astype(F32)
    return total.astype(BF16)


def add_column_body(*refs):
    *sources, block_ref, more_ref = refs
    block_ref[0] = column_total(*sources)
    more_ref[...] = sources[-1][1:]


def add_column(plan, mine, theirs, got, first):
    dims = mine.shape[1:]
    return call(
        add_column_body,
        [shaped(1, *dims, dtype=BF16), shaped(first.shape[0] - 1, *dims, dtype=BF16)],
        (mine, theirs, *reversed(got), first),
        moved=mine.size * 8,
    )


def add_with_output_body(plan, count, *refs):
    total = column_total(*refs[:count])
    first_ref, kept_ref, block_ref, own_ref = refs[count - 1 : count + 3]
    block_ref[0] = total
    own_ref[0] = kept_ref[0] + first_ref[1].astype(F32)
    for place, both_ref in enumerate(refs[count + 3 :], 1):
        both_ref[0, : plan.chunk, :] = total
        both_ref[0, plan.chunk :, :] = (
            kept_ref[place] + first_ref[1 + place].astype(F32)
        ).astype(BF16)


def add_with_output(plan, mine, theirs, got, first, kept):
    both = shaped(1, plan.chunk + plan.packed, LANES, dtype=BF16)
    block, out_own, *messages = call(
        functools.partial(add_with_output_body, plan, 3 + len(got)),
        [shaped(1, plan.chunk, LANES, dtype=BF16), shaped(1, plan.packed, LANES)]
        + [both] * (len(plan.columns) - 1),
        (mine, theirs, *reversed(got), first, kept),
        moved=mine.size * 12,
    )
    return block, out_own, messages


def stack_body(places, *refs):
    count = len(places)
    stack_ref, *rest_refs = refs[count:]
    rows = stack_ref.shape[1]
    for place, ref in zip(places, refs):
        stack_ref[place] = ref[0, :rows, :]
        for rest_ref in rest_refs:
            if place:
                rest_ref[place - 1] = ref[0, :rows, :]


def stack_up(plan, block, got, with_rest=False):
    dims = block.shape[1:]
    operands = [block, *got]
    places = list(range(len(operands)))
    if with_rest:
        operands, places = operands[::-1], places[::-1]
    outs = [shaped(1 + len(got), *dims, dtype=BF16), shaped(len(got), *dims, dtype=BF16)]
    return call(
        functools.partial(stack_body, places),
        outs if with_rest else outs[0],
        operands,
        moved=block.size * 16,
    )


def join_body(*refs):
    *sources, joined_ref = refs
    start = 0
    for ref in sources:
        joined_ref[start : start + ref.shape[0]] = ref[...]
        start += ref.shape[0]


def join(plan, *stacks):
    count = sum(one.shape[0] for one in stacks)
    return call(
        join_body,
        shaped(count, *stacks[0].shape[1:], dtype=BF16),
        stacks,
        moved=count * stacks[0].size,
    )


def double(plan, stack, bit):
    return join(plan, stack, partner_swap(stack, bit))


def add_message_body(plan, first_ref, here_ref, there_ref, stack_ref, message_ref):
    message_ref[0] = first_ref[0]
    half = here_ref.shape[0]
    for index, column in enumerate(plan.doubled):
        block = here_ref[index] if index < half else there_ref[index - half]
        place = plan.columns.index(column)
        stack_ref[place] = block
        message_ref[1 + place] = block


def add_message(plan, first, here, there):
    count, dims = len(plan.columns), first.shape[1:]
    return call(
        functools.partial(add_message_body, plan),
        [shaped(count, *dims, dtype=BF16), shaped(1 + count, *dims, dtype=BF16)],
        (first, here, there),
        moved=first.size * 40,
    )


def line_up_body(plan, *refs):
    for chip, block in plan.side_blocks(refs[:-1]):
        refs[-1][chip] = block


def line_up(plan, stack, *crossed):
    return call(
        functools.partial(line_up_body, plan),
        shaped(plan.chips, *stack.shape[1:], dtype=BF16),
        (stack, *crossed),
        moved=stack.size * 8,
    )


def finish_output_body(plan, own_ref, *refs):
    total = own_ref[0]
    for ref in refs[:-1]:
        total = total + ref[0, plan.chunk :, :].astype(F32)
    refs[-1][...] = unpack_block(plan, total).astype(BF16)


def finish_output(plan, own, messages):
    return call(
        functools.partial(finish_output_body, plan),
        shaped(plan.rows, plan.own, dtype=BF16),
        (own, *reversed(messages)),
        moved=own.size * 8,
    )


def prepare_body(plan, scaled_ref, inputs_ref, gain_ref, inverse_ref, factor_ref, slope_ref, base_ref):
    gain = gain_ref[...]
    inverse = inverse_ref[...]
    rebuilt = scaled_ref[...].astype(F32) / gain
    factor_ref[...] = inverse * gain
    slope_ref[...] = rebuilt * (inverse * inverse * inverse / plan.width)
    base_ref[...] = rebuilt - inputs_ref[...].astype(F32)


def prepare(plan, scaled, inputs, gain, inverse):
    return call(
        functools.partial(prepare_body, plan),
        [shaped(plan.rows, plan.width)] * 3,
        (scaled, inputs, gain, inverse),
        moved=scaled.size * 16,
    )


def dictionary_body(plan, pieces, own_ref, other_ref, scaled_ref, factor_ref, slope_ref, base_ref, inputs_ref, latents_ref, dict_ref, out_hbm, full, out_ref, out_sems):
    core = lax.axis_index("hidden")
    join_half(plan, own_ref, core * plan.half, full)
    join_half(plan, other_ref, (1 - core) * plan.half, full)
    grad = full[...].astype(F32)
    inner_row = jnp.sum(grad * scaled_ref[...].astype(F32), axis=1, keepdims=True)
    inputs = inputs_ref[...]
    rebuilt_grad = (
        grad * factor_ref[...] - inner_row * slope_ref[...] + base_ref[...]
    ).astype(BF16)
    latents = latents_ref[...]
    latent_grad = lax.dot_general(
        rebuilt_grad, dict_ref[...], ACROSS, preferred_element_type=F32
    )
    preact_grad = jnp.where(latents.astype(F32) > 0.0, latent_grad, 0.0).astype(BF16)
    left = jnp.concatenate([latents, preact_grad], axis=0)
    right = jnp.concatenate([rebuilt_grad, inputs], axis=0)
    size = plan.width // pieces
    writes = []
    for piece in range(pieces):
        span = slice(piece * size, (piece + 1) * size)
        out_ref[:, span] = lax.dot_general(
            left, right[:, span], DOWNWARD, preferred_element_type=F32
        ).astype(BF16)
        one = pltpu.make_async_copy(
            out_ref.at[:, span], out_hbm.at[:, span], out_sems.at[piece]
        )
        one.start()
        writes.append(one)
    for one in writes:
        one.wait()


def dictionary_step(plan, own, other, scaled, prepared, inputs, latents, dictionary):
    units = dictionary.shape[0]
    pieces = plan.tiles
    return call(
        functools.partial(dictionary_body, plan, pieces),
        shaped(*dictionary.shape, dtype=BF16),
        (own, other, scaled, *prepared, inputs, latents, dictionary),
        [
            pltpu.VMEM((plan.rows, plan.width), BF16),
            pltpu.VMEM(dictionary.shape, BF16),
            pltpu.SemaphoreType.DMA((pieces,)),
        ],
        out_specs=HBM,
        flops=6 * plan.rows * plan.width * units,
        moved=dictionary.size * 4,
    )


def swap(value):
    size = lax.axis_size("hidden")
    return lax.ppermute(value, "hidden", [(i, (i + 1) % size) for i in range(size)])


def partner_swap(value, bits):
    size = lax.axis_size("latent")
    return lax.ppermute(value, "latent", [(i, i ^ bits) for i in range(size)])


def cross(value):
    return partner_swap(value, 1)


def to_column(plan, blocks):
    pairs = list(zip(blocks, plan.columns[1:]))
    got = [partner_swap(one, column) for one, column in reversed(pairs)]
    return got[::-1]


def to_all_columns(plan, block):
    return [partner_swap(block, column) for column in plan.columns[1:]]


def tie(*values):
    return lax.optimization_barrier(values)


def per_device(
    input_codes,
    cotangent_codes,
    dictionary,
    encoder_bias,
    decoder_bias,
    norm_gain,
    gate_weight,
    up_weight,
    down_weight,
):
    plan = Plan(
        lax.axis_size("latent"), lax.axis_size("hidden"), input_codes.shape[0], input_codes.shape[1]
    )
    if not plan.fits():
        return per_device_plain(
            input_codes,
            cotangent_codes,
            dictionary,
            encoder_bias,
            decoder_bias,
            norm_gain,
            gate_weight,
            up_weight,
            down_weight,
        )
    vectors = jnp.concatenate([encoder_bias, decoder_bias, norm_gain]).reshape(1, -1)
    codes = jnp.stack([input_codes, cotangent_codes])
    values = (codes.astype(F32) * CODE_STEP).astype(BF16)
    block, cotangent = pack_values(plan, values)
    stack = stack_up(plan, block, to_all_columns(plan, block))
    stack, vectors, late_dictionary, cotangent = tie(stack, vectors, dictionary, cotangent)
    stack_other, crossed = swap(stack), cross(stack)
    encoder = bring_encoder(plan, late_dictionary, vectors)
    cotangent = double(plan, cotangent, plan.doubling[0])
    stack_other, crossed, encoder, cotangent = tie(stack_other, crossed, encoder, cotangent)
    brought, bias, decoder, gain = encoder
    inputs, latents, kept, sent = encode(
        plan, (stack, crossed), (stack_other, swap(crossed)), brought, bias, gain
    )
    sent, kept = swap(sent), swap(kept)
    own_kept, own_sent = decode_own(plan, latents, brought, decoder, gain)
    sent_first, sent_rest = add_sent(plan, own_sent, sent)
    sent_rest, cotangent = tie(sent_rest, cotangent)
    for bit in plan.doubling[1:-1]:
        cotangent = double(plan, cotangent, bit)
    there = partner_swap(cotangent, plan.doubling[-1])
    sent = add_across(plan, own_kept, kept, cross(sent_rest))
    sent, sent_first, cotangent, there = tie(sent, sent_first, cotangent, there)
    cotangent, sent_first = add_message(plan, sent_first, cotangent, there)
    got, first = to_column(plan, sent), cross(sent_first)
    block, crossed = add_column(plan, own_kept, kept, got, first)
    cotangent_own = (cotangent, crossed)
    hidden_grad = back_project(
        plan, cotangent_own, [swap(one) for one in cotangent_own], down_weight
    )
    stack = stack_up(plan, block, to_all_columns(plan, block))
    stack_other, crossed = swap(stack), cross(stack)
    stack_other, crossed, hidden_grad = tie(stack_other, crossed, hidden_grad)
    terms = mlp_first(plan, line_up(plan, stack, crossed), gate_weight, up_weight, gain)
    scaled_other = line_up(plan, stack_other, swap(crossed))
    scaled, inverse, hidden, gate_grad, up_grad, kept, sent = mlp(
        plan, scaled_other, gate_weight, up_weight, gain, hidden_grad, terms
    )
    sent, kept = swap(sent), swap(kept)
    own_kept, own_sent = mlp_own(plan, gate_grad, up_grad, gate_weight, up_weight)
    out_mine, out_theirs = project(plan, hidden, down_weight)
    sent_first, sent_rest = add_sent(plan, own_sent, sent)
    sent_first, sent_rest, out_mine, out_theirs = tie(sent_first, sent_rest, out_mine, out_theirs)
    crossed = cross(sent_rest)
    out_kept, sent_first = add_pair(plan, sent_first, out_mine, swap(out_theirs))
    sent = add_across(plan, own_kept, kept, crossed)
    sent, sent_first, out_kept = tie(sent, sent_first, out_kept)
    got = to_column(plan, sent)
    first = cross(sent_first)
    block, out_own, messages = add_with_output(plan, own_kept, kept, got, first, out_kept)
    got = list(tie(*to_column(plan, messages)))
    stack = stack_up(plan, block, got)
    stack, scaled_late, inputs_late = tie(stack, scaled, inputs)
    crossed, stack_other = cross(stack), swap(stack)
    prepared = prepare(plan, scaled_late, inputs_late, gain, inverse)
    block_output = finish_output(plan, out_own, got)
    grad_own = line_up(plan, stack, crossed)
    grad_other = line_up(plan, stack_other, swap(crossed))
    dictionary_grad = dictionary_step(
        plan, grad_own, grad_other, scaled, prepared, inputs, latents, brought
    )
    return (block_output, dictionary_grad)


def per_device_plain(
    input_codes,
    cotangent_codes,
    dictionary,
    encoder_bias,
    decoder_bias,
    norm_gain,
    gate_weight,
    up_weight,
    down_weight,
):
    own_width = input_codes.shape[1]
    model_width = own_width * lax.axis_size(("latent", "hidden"))
    cotangent_local = (cotangent_codes.astype(jnp.float32) * CODE_STEP).astype(jnp.bfloat16)
    inputs_local = (input_codes.astype(jnp.float32) * CODE_STEP).astype(jnp.bfloat16)
    inputs = lax.all_gather(inputs_local, ("latent", "hidden"), axis=1, tiled=True)
    preact = (
        lax.dot_general(inputs, dictionary, ACROSS, preferred_element_type=jnp.float32)
        + encoder_bias
    )
    latents = jnp.maximum(preact, 0.0).astype(jnp.bfloat16)
    partial_value = jnp.dot(latents, dictionary, preferred_element_type=jnp.float32)
    rebuilt = lax.psum(partial_value, ("latent", "hidden")) + decoder_bias
    inverse = lax.rsqrt(
        jnp.sum(rebuilt * rebuilt, axis=1, keepdims=True) / model_width + NORM_EPSILON
    )
    normed = (rebuilt * inverse * norm_gain).astype(jnp.bfloat16)
    target = inputs.astype(jnp.float32)
    gate_proj = lax.dot_general(normed, gate_weight, ACROSS, preferred_element_type=jnp.float32)
    up_proj = lax.dot_general(normed, up_weight, ACROSS, preferred_element_type=jnp.float32)
    gelu_value, gelu_slope = gelu_parts(gate_proj)
    hidden = (gelu_value * up_proj).astype(jnp.bfloat16)
    output_terms = jnp.dot(hidden, down_weight, preferred_element_type=jnp.float32)
    block_output = lax.psum_scatter(
        output_terms, ("latent", "hidden"), scatter_dimension=1, tiled=True
    ).astype(jnp.bfloat16)
    hidden_grad = lax.dot_general(
        lax.all_gather(cotangent_local, ("latent", "hidden"), axis=1, tiled=True),
        down_weight,
        ACROSS,
        preferred_element_type=jnp.float32,
    )
    gate_grad = (hidden_grad * up_proj * gelu_slope).astype(jnp.bfloat16)
    up_grad = (hidden_grad * gelu_value).astype(jnp.bfloat16)
    partial_grad = jnp.dot(gate_grad, gate_weight, preferred_element_type=jnp.float32) + jnp.dot(
        up_grad, up_weight, preferred_element_type=jnp.float32
    )
    scaled = lax.psum(partial_grad, ("latent", "hidden")) * norm_gain
    inner_row = jnp.sum(scaled * rebuilt, axis=1, keepdims=True)
    inverse_cube = inverse * inverse * inverse
    rebuilt_grad = (
        inverse * scaled - inverse_cube * rebuilt * (inner_row / model_width) + (rebuilt - target)
    ).astype(jnp.bfloat16)
    latent_grad = lax.dot_general(
        rebuilt_grad, dictionary, ACROSS, preferred_element_type=jnp.float32
    )
    preact_grad = jnp.where(preact > 0.0, latent_grad, 0.0).astype(jnp.bfloat16)
    dictionary_grad = lax.dot_general(
        latents, rebuilt_grad, DOWNWARD, preferred_element_type=jnp.float32
    ) + lax.dot_general(preact_grad, inputs, DOWNWARD, preferred_element_type=jnp.float32)
    return (block_output, dictionary_grad.astype(jnp.bfloat16))


def solution(mesh):
    in_specs = (
        P("groups", ("latent", "hidden")),
        P("groups", ("latent", "hidden")),
        P(("latent", "hidden"), None),
        P(("latent", "hidden")),
        P(),
        P(),
        P(("latent", "hidden"), None),
        P(("latent", "hidden"), None),
        P(("latent", "hidden"), None),
    )
    out_specs = (P("groups", ("latent", "hidden")), P(("latent", "hidden"), "groups"))
    return jax.shard_map(
        per_device, mesh=mesh, in_specs=in_specs, out_specs=out_specs, check_vma=False
    )
```

profile of v0, /device:TPU:0, one launch (start us, length us, event | category | flops | bytes accessed | tf_op | source)
XLA Modules:
  0.0 91.3 jit_solution(3419806569219977158)
XLA Ops:
  1.7 5.1 %collective-permute-start.2 = (bf16[1,176,128]{2,1,0:T(8,128)(2,1)S(1)}, bf16[1,176,128]{2,1,0:T(8,128)(2,1)S(1)}, u32[]{:S(2)}, u32[]{:S(2)}) collective-permute-start(bf16[1,176,128]{2,1,0:T(8,128)(2,1)S(1)} %get-tuple-element.90.refs_0_), channel_id=1, source_target_pairs={{0,12},{2,14},{4,8},{6,10},{8,4},{10,6},{12,0},{14,2},{1,13},{3,15... | collective-permute-start | bytes 135176 | tf_op jit(solution)/shard_map/ppermute | solution.py:726
  8.9 2.9 %collective-permute-done.1.refs_2_ = bf16[1,176,128]{2,1,0:T(8,128)(2,1)S(1)} collective-permute-done((bf16[1,176,128]{2,1,0:T(8,128)(2,1)S(1)}, bf16[1,176,128]{2,1,0:T(8,128)(2,1)S(1)}, u32[]{:S(2)}, u32[]{:S(2)}) %collective-permute-start.1) | collective-permute-done | bytes 45088 | tf_op jit(solution)/shard_map/ppermute | solution.py:726
  11.8 1.6 %collective-permute-start.4 = (bf16[4,176,128]{2,1,0:T(8,128)(2,1)S(1)}, bf16[4,176,128]{2,1,0:T(8,128)(2,1)S(1)}, u32[]{:S(2)}, u32[]{:S(2)}) collective-permute-start(bf16[4,176,128]{2,1,0:T(8,128)(2,1)S(1)} %shard_map.105.refs_0_), channel_id=1, source_target_pairs={{0,2},{2,0},{4,6},{6,4},{8,10},{10,8},{12,14},{14,12},{1,3},{3,1},... | collective-permute-start | bytes 540680 | tf_op jit(solution)/shard_map/ppermute | solution.py:726
  13.4 2.0 %collective-permute-start.5 = (bf16[1,176,128]{2,1,0:T(8,128)(2,1)S(1)}, bf16[1,176,128]{2,1,0:T(8,128)(2,1)S(1)}, u32[]{:S(2)}, u32[]{:S(2)}) collective-permute-start(bf16[1,176,128]{2,1,0:T(8,128)(2,1)S(1)} %get-tuple-element.99.refs_0_), channel_id=1, source_target_pairs={{0,8},{2,10},{4,12},{6,14},{8,0},{10,2},{12,4},{14,6},{1,9},{3,11}... | collective-permute-start | bytes 135176 | tf_op jit(solution)/shard_map/ppermute | solution.py:726
  15.4 1.7 %shard_map.106 = (bf16[512,2304]{1,0:T(8,128)(2,1)S(1)}, f32[1,512]{1,0:T(1,128)S(1)}, f32[1,2304]{1,0:T(1,128)S(1)}, f32[1,2304]{1,0:T(1,128)S(1)}) custom-call(bf16[512,2304]{1,0:T(8,128)(2,1)} %dict_hbm, f32[1,5120]{1,0:T(1,128)S(1)} %bitcast.3), custom_call_target="tpu_custom_call" | custom-call | bytes 4718592 | tf_op jit(solution)/shard_map/pallas_call | solution.py:246
  17.1 2.0 %collective-permute-done.5.refs_1_ = bf16[1,176,128]{2,1,0:T(8,128)(2,1)S(1)} collective-permute-done((bf16[1,176,128]{2,1,0:T(8,128)(2,1)S(1)}, bf16[1,176,128]{2,1,0:T(8,128)(2,1)S(1)}, u32[]{:S(2)}, u32[]{:S(2)}) %collective-permute-start.5) | collective-permute-done | bytes 45088 | tf_op jit(solution)/shard_map/ppermute | solution.py:726
  19.3 1.3 %collective-permute-done.6.refs_3_ = bf16[4,176,128]{2,1,0:T(8,128)(2,1)S(1)} collective-permute-done((bf16[4,176,128]{2,1,0:T(8,128)(2,1)S(1)}, bf16[4,176,128]{2,1,0:T(8,128)(2,1)S(1)}, u32[]{:S(2)}, u32[]{:S(2)}) %collective-permute-start.6) | collective-permute-done | bytes 180256 | tf_op jit(solution)/shard_map/ppermute | solution.py:721
  20.6 1.7 %shard_map.108 = (bf16[144,2304]{1,0:T(8,128)(2,1)S(1)}, bf16[144,512]{1,0:T(8,128)(2,1)S(1)}, f32[4,176,128]{2,1,0:T(8,128)S(1)}, f32[4,176,128]{2,1,0:T(8,128)S(1)}) custom-call(bf16[4,176,128]{2,1,0:T(8,128)(2,1)S(1)} %shard_map.105.refs_0_, bf16[4,176,128]{2,1,0:T(8,128)(2,1)S(1)} %collective-permute-done.4.refs_1_, ...), custom_call_target="tpu_custom_call" | custom-call | flops 509607936 | bytes 2359296 | tf_op jit(solution)/shard_map/pallas_call | solution.py:113
  24.7 5.1 %collective-permute-done.9.got_ref = bf16[3,176,128]{2,1,0:T(8,128)(2,1)S(1)} collective-permute-done((bf16[3,176,128]{2,1,0:T(8,128)(2,1)S(1)}, bf16[3,176,128]{2,1,0:T(8,128)(2,1)S(1)}, u32[]{:S(2)}, u32[]{:S(2)}) %collective-permute-start.9) | collective-permute-done | bytes 135200 | tf_op jit(solution)/shard_map/ppermute | solution.py:726
  32.4 2.8 %collective-permute-start.13 = (bf16[1,176,128]{2,1,0:T(8,128)(2,1)S(1)}, bf16[1,176,128]{2,1,0:T(8,128)(2,1)S(1)}, u32[]{:S(2)}, u32[]{:S(2)}) collective-permute-start(bf16[1,176,128]{2,1,0:T(8,128)(2,1)S(1)} %get-tuple-element.121), channel_id=1, source_target_pairs={{0,4},{2,6},{4,0},{6,2},{8,12},{10,14},{12,8},{14,10},{1,5},{3,7},... | collective-permute-start | bytes 135176 | tf_op jit(solution)/shard_map/ppermute | solution.py:726
  35.2 1.5 %collective-permute-done.11.refs_2_ = bf16[1,176,128]{2,1,0:T(8,128)(2,1)S(1)} collective-permute-done((bf16[1,176,128]{2,1,0:T(8,128)(2,1)S(1)}, bf16[1,176,128]{2,1,0:T(8,128)(2,1)S(1)}, u32[]{:S(2)}, u32[]{:S(2)}) %collective-permute-start.11) | collective-permute-done | bytes 45088 | tf_op jit(solution)/shard_map/ppermute | solution.py:726
  37.8 2.0 %collective-permute-start.17 = (bf16[1,176,128]{2,1,0:T(8,128)(2,1)S(1)}, bf16[1,176,128]{2,1,0:T(8,128)(2,1)S(1)}, u32[]{:S(2)}, u32[]{:S(2)}) collective-permute-start(bf16[1,176,128]{2,1,0:T(8,128)(2,1)S(1)} %get-tuple-element.126.refs_0_), channel_id=1, source_target_pairs={{0,12},{2,14},{4,8},{6,10},{8,4},{10,6},{12,0},{14,2},{1,13},{3,15... | collective-permute-start | bytes 135176 | tf_op jit(solution)/shard_map/ppermute | solution.py:726
  40.9 1.4 %collective-permute-start.15 = (bf16[1,176,128]{2,1,0:T(8,128)(2,1)S(1)}, bf16[1,176,128]{2,1,0:T(8,128)(2,1)S(1)}, u32[]{:S(2)}, u32[]{:S(2)}) collective-permute-start(bf16[1,176,128]{2,1,0:T(8,128)(2,1)S(1)} %get-tuple-element.126.refs_0_), channel_id=1, source_target_pairs={{0,4},{2,6},{4,0},{6,2},{8,12},{10,14},{12,8},{14,10},{1,5},{3,7},... | collective-permute-start | bytes 135176 | tf_op jit(solution)/shard_map/ppermute | solution.py:726
  45.2 1.3 %collective-permute-start.19 = (bf16[4,176,128]{2,1,0:T(8,128)(2,1)S(1)}, bf16[4,176,128]{2,1,0:T(8,128)(2,1)S(1)}, u32[]{:S(2)}, u32[]{:S(2)}) collective-permute-start(bf16[4,176,128]{2,1,0:T(8,128)(2,1)S(1)} %shard_map.114.refs_0_), channel_id=1, source_target_pairs={{0,2},{2,0},{4,6},{6,4},{8,10},{10,8},{12,14},{14,12},{1,3},{3,1},... | collective-permute-start | bytes 540680 | tf_op jit(solution)/shard_map/ppermute | solution.py:726
  47.8 3.0 %collective-permute-done.19.refs_1_ = bf16[4,176,128]{2,1,0:T(8,128)(2,1)S(1)} collective-permute-done((bf16[4,176,128]{2,1,0:T(8,128)(2,1)S(1)}, bf16[4,176,128]{2,1,0:T(8,128)(2,1)S(1)}, u32[]{:S(2)}, u32[]{:S(2)}) %collective-permute-start.19) | collective-permute-done | bytes 180256 | tf_op jit(solution)/shard_map/ppermute | solution.py:726
  52.2 1.6 %shard_map.119 = (bf16[144,2304]{1,0:T(8,128)(2,1)S(1)}, f32[144,1]{1,0:T(8,128)S(1)}, bf16[144,512]{1,0:T(8,128)(2,1)S(1)}, bf16[144,512]{1,0:T(8,128)(2,1)S(1)...) custom-call(bf16[8,176,128]{2,1,0:T(8,128)(2,1)S(1)} %shard_map.116.other_ref, ...), custom_call_target="tpu_custom_call" | custom-call | flops 1019215872 | bytes 4718592 | tf_op jit(solution)/shard_map/pallas_call | solution.py:113
  57.6 4.6 %collective-permute-done.25.got_ref = bf16[3,176,128]{2,1,0:T(8,128)(2,1)S(1)} collective-permute-done((bf16[3,176,128]{2,1,0:T(8,128)(2,1)S(1)}, bf16[3,176,128]{2,1,0:T(8,128)(2,1)S(1)}, u32[]{:S(2)}, u32[]{:S(2)}) %collective-permute-start.25) | collective-permute-done | bytes 135200 | tf_op jit(solution)/shard_map/ppermute | solution.py:726
  63.7 1.9 %collective-permute-start.27 = (bf16[1,176,128]{2,1,0:T(8,128)(2,1)S(1)}, bf16[1,176,128]{2,1,0:T(8,128)(2,1)S(1)}, u32[]{:S(2)}, u32[]{:S(2)}) collective-permute-start(bf16[1,176,128]{2,1,0:T(8,128)(2,1)S(1)} %get-tuple-element.156), channel_id=1, source_target_pairs={{0,12},{2,14},{4,8},{6,10},{8,4},{10,6},{12,0},{14,2},{1,13},{3,15... | collective-permute-start | bytes 135176 | tf_op jit(solution)/shard_map/ppermute | solution.py:726
  66.2 1.9 %collective-permute-start.29 = (bf16[1,176,128]{2,1,0:T(8,128)(2,1)S(1)}, bf16[1,176,128]{2,1,0:T(8,128)(2,1)S(1)}, u32[]{:S(2)}, u32[]{:S(2)}) collective-permute-start(bf16[1,176,128]{2,1,0:T(8,128)(2,1)S(1)} %get-tuple-element.158), channel_id=1, source_target_pairs={{0,4},{2,6},{4,0},{6,2},{8,12},{10,14},{12,8},{14,10},{1,5},{3,7},... | collective-permute-start | bytes 135176 | tf_op jit(solution)/shard_map/ppermute | solution.py:726
  68.1 1.8 %collective-permute-done.27.refs_2_ = bf16[1,176,128]{2,1,0:T(8,128)(2,1)S(1)} collective-permute-done((bf16[1,176,128]{2,1,0:T(8,128)(2,1)S(1)}, bf16[1,176,128]{2,1,0:T(8,128)(2,1)S(1)}, u32[]{:S(2)}, u32[]{:S(2)}) %collective-permute-start.27) | collective-permute-done | bytes 45088 | tf_op jit(solution)/shard_map/ppermute | solution.py:726
  73.4 2.0 %collective-permute-start.33 = (bf16[1,352,128]{2,1,0:T(8,128)(2,1)S(1)}, bf16[1,352,128]{2,1,0:T(8,128)(2,1)S(1)}, u32[]{:S(2)}, u32[]{:S(2)}) collective-permute-start(bf16[1,352,128]{2,1,0:T(8,128)(2,1)S(1)} %get-tuple-element.164), channel_id=1, source_target_pairs={{0,12},{2,14},{4,8},{6,10},{8,4},{10,6},{12,0},{14,2},{1,13},{3,15... | collective-permute-start | bytes 270344 | tf_op jit(solution)/shard_map/ppermute | solution.py:726
  75.6 4.9 %collective-permute-done.32.refs_1_.refs_2_ = bf16[1,352,128]{2,1,0:T(8,128)(2,1)S(1)} collective-permute-done((bf16[1,352,128]{2,1,0:T(8,128)(2,1)S(1)}, bf16[1,352,128]{2,1,0:T(8,128)(2,1)S(1)}, u32[]{:S(2)}, u32[]{:S(2)}) %collective-permute-start.32) | collective-permute-done | bytes 90144 | tf_op jit(solution)/shard_map/ppermute | solution.py:726
  81.4 4.7 %collective-permute-done.34.refs_1_ = bf16[4,176,128]{2,1,0:T(8,128)(2,1)S(1)} collective-permute-done((bf16[4,176,128]{2,1,0:T(8,128)(2,1)S(1)}, bf16[4,176,128]{2,1,0:T(8,128)(2,1)S(1)}, u32[]{:S(2)}, u32[]{:S(2)}) %collective-permute-start.34) | collective-permute-done | bytes 180256 | tf_op jit(solution)/shard_map/ppermute | solution.py:726
  87.6 3.7 %shard_map.131 = bf16[512,2304]{1,0:T(8,128)(2,1)} custom-call(bf16[8,176,128]{2,1,0:T(8,128)(2,1)S(1)} %shard_map.128.own_ref, bf16[8,176,128]{2,1,0:T(8,128)(2,1)S(1)} %shard_map.129.other_ref, bf16[144,2304]{1,0:T(8,128)(2,1)S(1)} %get-tuple-element.172.scaled_ref, f32[144,2304]{1,0:T(8,128)S(1)} %get-tuple-element.175.factor_ref, ...), custom_call_target="tpu_custom_call" | custom-call | flops 1019215872 | bytes 4718592 | tf_op jit(solution)/shard_map/pallas_call | solution.py:113
  (86 shorter events, 28.1 us)
Async XLA Ops:
  1.7 7.2 %collective-permute-start.2 = (bf16[1,176,128]{2,1,0:T(8,128)(2,1)S(1)}, bf16[1,176,128]{2,1,0:T(8,128)(2,1)S(1)}, u32[]{:S(2)}, u32[]{:S(2)}) collective-permute-start(bf16[1,176,128]{2,1,0:T(8,128)(2,1)S(1)} %get-tuple-element.90.refs_0_), channel_id=1, source_target_pairs={{0,12},{2,14},{4,8},{6,10},{8,4},{10,6},{12,0},{14,2},{1,13},{3,15... | collective-permute-start | bytes 135176 | tf_op jit(solution)/shard_map/ppermute | solution.py:726
  6.9 4.9 %collective-permute-start.1 = (bf16[1,176,128]{2,1,0:T(8,128)(2,1)S(1)}, bf16[1,176,128]{2,1,0:T(8,128)(2,1)S(1)}, u32[]{:S(2)}, u32[]{:S(2)}) collective-permute-start(bf16[1,176,128]{2,1,0:T(8,128)(2,1)S(1)} %get-tuple-element.90.refs_0_), channel_id=1, source_target_pairs={{0,8},{2,10},{4,12},{6,14},{8,0},{10,2},{12,4},{14,6},{1,9},{3,11}... | collective-permute-start | bytes 135176 | tf_op jit(solution)/shard_map/ppermute | solution.py:726
  6.9 4.9 %collective-permute-start = (bf16[1,176,128]{2,1,0:T(8,128)(2,1)S(1)}, bf16[1,176,128]{2,1,0:T(8,128)(2,1)S(1)}, u32[]{:S(2)}, u32[]{:S(2)}) collective-permute-start(bf16[1,176,128]{2,1,0:T(8,128)(2,1)S(1)} %get-tuple-element.90.refs_0_), channel_id=1, source_target_pairs={{0,4},{2,6},{4,0},{6,2},{8,12},{10,14},{12,8},{14,10},{1,5},{3,7},... | collective-permute-start | bytes 135176 | tf_op jit(solution)/shard_map/ppermute | solution.py:726
  11.8 7.3 %collective-permute-start.4 = (bf16[4,176,128]{2,1,0:T(8,128)(2,1)S(1)}, bf16[4,176,128]{2,1,0:T(8,128)(2,1)S(1)}, u32[]{:S(2)}, u32[]{:S(2)}) collective-permute-start(bf16[4,176,128]{2,1,0:T(8,128)(2,1)S(1)} %shard_map.105.refs_0_), channel_id=1, source_target_pairs={{0,2},{2,0},{4,6},{6,4},{8,10},{10,8},{12,14},{14,12},{1,3},{3,1},... | collective-permute-start | bytes 540680 | tf_op jit(solution)/shard_map/ppermute | solution.py:726
  13.4 5.8 %collective-permute-start.3 = (bf16[4,176,128]{2,1,0:T(8,128)(2,1)S(1)}, bf16[4,176,128]{2,1,0:T(8,128)(2,1)S(1)}, u32[]{:S(2)}, u32[]{:S(2)}) collective-permute-start(bf16[4,176,128]{2,1,0:T(8,128)(2,1)S(1)} %shard_map.105.refs_0_), channel_id=1, source_target_pairs={{0,1},{1,0},{2,3},{3,2},{4,5},{5,4},{6,7},{7,6},{8,9},{9,8},{10,11... | collective-permute-start | bytes 540680 | tf_op jit(solution)/shard_map/ppermute | solution.py:721
  13.4 5.7 %collective-permute-start.5 = (bf16[1,176,128]{2,1,0:T(8,128)(2,1)S(1)}, bf16[1,176,128]{2,1,0:T(8,128)(2,1)S(1)}, u32[]{:S(2)}, u32[]{:S(2)}) collective-permute-start(bf16[1,176,128]{2,1,0:T(8,128)(2,1)S(1)} %get-tuple-element.99.refs_0_), channel_id=1, source_target_pairs={{0,8},{2,10},{4,12},{6,14},{8,0},{10,2},{12,4},{14,6},{1,9},{3,11}... | collective-permute-start | bytes 135176 | tf_op jit(solution)/shard_map/ppermute | solution.py:726
  24.1 5.7 %collective-permute-start.9 = (bf16[3,176,128]{2,1,0:T(8,128)(2,1)S(1)}, bf16[3,176,128]{2,1,0:T(8,128)(2,1)S(1)}, u32[]{:S(2)}, u32[]{:S(2)}) collective-permute-start(bf16[3,176,128]{2,1,0:T(8,128)(2,1)S(1)} %get-tuple-element.113), channel_id=1, source_target_pairs={{0,2},{2,0},{4,6},{6,4},{8,10},{10,8},{12,14},{14,12},{1,3},{3,1},... | collective-permute-start | bytes 405512 | tf_op jit(solution)/shard_map/ppermute | solution.py:726
  24.7 5.2 %collective-permute-start.10 = (bf16[2,176,128]{2,1,0:T(8,128)(2,1)S(1)}, bf16[2,176,128]{2,1,0:T(8,128)(2,1)S(1)}, u32[]{:S(2)}, u32[]{:S(2)}) collective-permute-start(bf16[2,176,128]{2,1,0:T(8,128)(2,1)S(1)} %shard_map.107.here_ref), channel_id=1, source_target_pairs={{0,4},{2,6},{4,0},{6,2},{8,12},{10,14},{12,8},{14,10},{1,5},{3,7},... | collective-permute-start | bytes 270344 | tf_op jit(solution)/shard_map/ppermute | solution.py:726
  29.9 7.8 %collective-permute-start.14 = (bf16[5,176,128]{2,1,0:T(8,128)(2,1)S(1)}, bf16[5,176,128]{2,1,0:T(8,128)(2,1)S(1)}, u32[]{:S(2)}, u32[]{:S(2)}) collective-permute-start(bf16[5,176,128]{2,1,0:T(8,128)(2,1)S(1)} %get-tuple-element.125), channel_id=1, source_target_pairs={{0,2},{2,0},{4,6},{6,4},{8,10},{10,8},{12,14},{14,12},{1,3},{3,1},... | collective-permute-start | bytes 675848 | tf_op jit(solution)/shard_map/ppermute | solution.py:726
  30.8 5.9 %collective-permute-start.11 = (bf16[1,176,128]{2,1,0:T(8,128)(2,1)S(1)}, bf16[1,176,128]{2,1,0:T(8,128)(2,1)S(1)}, u32[]{:S(2)}, u32[]{:S(2)}) collective-permute-start(bf16[1,176,128]{2,1,0:T(8,128)(2,1)S(1)} %get-tuple-element.119), channel_id=1, source_target_pairs={{0,12},{2,14},{4,8},{6,10},{8,4},{10,6},{12,0},{14,2},{1,13},{3,15... | collective-permute-start | bytes 135176 | tf_op jit(solution)/shard_map/ppermute | solution.py:726
  31.9 5.8 %collective-permute-start.12 = (bf16[1,176,128]{2,1,0:T(8,128)(2,1)S(1)}, bf16[1,176,128]{2,1,0:T(8,128)(2,1)S(1)}, u32[]{:S(2)}, u32[]{:S(2)}) collective-permute-start(bf16[1,176,128]{2,1,0:T(8,128)(2,1)S(1)} %get-tuple-element.120), channel_id=1, source_target_pairs={{0,8},{2,10},{4,12},{6,14},{8,0},{10,2},{12,4},{14,6},{1,9},{3,11}... | collective-permute-start | bytes 135176 | tf_op jit(solution)/shard_map/ppermute | solution.py:726
  32.4 5.3 %collective-permute-start.13 = (bf16[1,176,128]{2,1,0:T(8,128)(2,1)S(1)}, bf16[1,176,128]{2,1,0:T(8,128)(2,1)S(1)}, u32[]{:S(2)}, u32[]{:S(2)}) collective-permute-start(bf16[1,176,128]{2,1,0:T(8,128)(2,1)S(1)} %get-tuple-element.121), channel_id=1, source_target_pairs={{0,4},{2,6},{4,0},{6,2},{8,12},{10,14},{12,8},{14,10},{1,5},{3,7},... | collective-permute-start | bytes 135176 | tf_op jit(solution)/shard_map/ppermute | solution.py:726
  37.8 5.9 %collective-permute-start.17 = (bf16[1,176,128]{2,1,0:T(8,128)(2,1)S(1)}, bf16[1,176,128]{2,1,0:T(8,128)(2,1)S(1)}, u32[]{:S(2)}, u32[]{:S(2)}) collective-permute-start(bf16[1,176,128]{2,1,0:T(8,128)(2,1)S(1)} %get-tuple-element.126.refs_0_), channel_id=1, source_target_pairs={{0,12},{2,14},{4,8},{6,10},{8,4},{10,6},{12,0},{14,2},{1,13},{3,15... | collective-permute-start | bytes 135176 | tf_op jit(solution)/shard_map/ppermute | solution.py:726
  39.7 5.0 %collective-permute-start.16 = (bf16[1,176,128]{2,1,0:T(8,128)(2,1)S(1)}, bf16[1,176,128]{2,1,0:T(8,128)(2,1)S(1)}, u32[]{:S(2)}, u32[]{:S(2)}) collective-permute-start(bf16[1,176,128]{2,1,0:T(8,128)(2,1)S(1)} %get-tuple-element.126.refs_0_), channel_id=1, source_target_pairs={{0,8},{2,10},{4,12},{6,14},{8,0},{10,2},{12,4},{14,6},{1,9},{3,11}... | collective-permute-start | bytes 135176 | tf_op jit(solution)/shard_map/ppermute | solution.py:726
  45.2 5.6 %collective-permute-start.19 = (bf16[4,176,128]{2,1,0:T(8,128)(2,1)S(1)}, bf16[4,176,128]{2,1,0:T(8,128)(2,1)S(1)}, u32[]{:S(2)}, u32[]{:S(2)}) collective-permute-start(bf16[4,176,128]{2,1,0:T(8,128)(2,1)S(1)} %shard_map.114.refs_0_), channel_id=1, source_target_pairs={{0,2},{2,0},{4,6},{6,4},{8,10},{10,8},{12,14},{14,12},{1,3},{3,1},... | collective-permute-start | bytes 540680 | tf_op jit(solution)/shard_map/ppermute | solution.py:726
  56.1 6.1 %collective-permute-start.26 = (bf16[8,176,128]{2,1,0:T(8,128)(2,1)S(1)}, bf16[8,176,128]{2,1,0:T(8,128)(2,1)S(1)}, u32[]{:S(2)}, u32[]{:S(2)}) collective-permute-start(bf16[8,176,128]{2,1,0:T(8,128)(2,1)S(1)} %get-tuple-element.153), channel_id=1, source_target_pairs={{0,1},{1,0},{2,3},{3,2},{4,5},{5,4},{6,7},{7,6},{8,9},{9,8},{10,11... | collective-permute-start | bytes 1081352 | tf_op jit(solution)/shard_map/ppermute | solution.py:721
  56.4 5.8 %collective-permute-start.25 = (bf16[3,176,128]{2,1,0:T(8,128)(2,1)S(1)}, bf16[3,176,128]{2,1,0:T(8,128)(2,1)S(1)}, u32[]{:S(2)}, u32[]{:S(2)}) collective-permute-start(bf16[3,176,128]{2,1,0:T(8,128)(2,1)S(1)} %get-tuple-element.147), channel_id=1, source_target_pairs={{0,2},{2,0},{4,6},{6,4},{8,10},{10,8},{12,14},{14,12},{1,3},{3,1},... | collective-permute-start | bytes 405512 | tf_op jit(solution)/shard_map/ppermute | solution.py:726
  62.4 8.5 %collective-permute-start.30 = (bf16[5,176,128]{2,1,0:T(8,128)(2,1)S(1)}, bf16[5,176,128]{2,1,0:T(8,128)(2,1)S(1)}, u32[]{:S(2)}, u32[]{:S(2)}) collective-permute-start(bf16[5,176,128]{2,1,0:T(8,128)(2,1)S(1)} %get-tuple-element.159), channel_id=1, source_target_pairs={{0,2},{2,0},{4,6},{6,4},{8,10},{10,8},{12,14},{14,12},{1,3},{3,1},... | collective-permute-start | bytes 675848 | tf_op jit(solution)/shard_map/ppermute | solution.py:726
  63.7 6.2 %collective-permute-start.27 = (bf16[1,176,128]{2,1,0:T(8,128)(2,1)S(1)}, bf16[1,176,128]{2,1,0:T(8,128)(2,1)S(1)}, u32[]{:S(2)}, u32[]{:S(2)}) collective-permute-start(bf16[1,176,128]{2,1,0:T(8,128)(2,1)S(1)} %get-tuple-element.156), channel_id=1, source_target_pairs={{0,12},{2,14},{4,8},{6,10},{8,4},{10,6},{12,0},{14,2},{1,13},{3,15... | collective-permute-start | bytes 135176 | tf_op jit(solution)/shard_map/ppermute | solution.py:726
  65.5 5.4 %collective-permute-start.28 = (bf16[1,176,128]{2,1,0:T(8,128)(2,1)S(1)}, bf16[1,176,128]{2,1,0:T(8,128)(2,1)S(1)}, u32[]{:S(2)}, u32[]{:S(2)}) collective-permute-start(bf16[1,176,128]{2,1,0:T(8,128)(2,1)S(1)} %get-tuple-element.157), channel_id=1, source_target_pairs={{0,8},{2,10},{4,12},{6,14},{8,0},{10,2},{12,4},{14,6},{1,9},{3,11}... | collective-permute-start | bytes 135176 | tf_op jit(solution)/shard_map/ppermute | solution.py:726
  72.2 8.3 %collective-permute-start.32 = (bf16[1,352,128]{2,1,0:T(8,128)(2,1)S(1)}, bf16[1,352,128]{2,1,0:T(8,128)(2,1)S(1)}, u32[]{:S(2)}, u32[]{:S(2)}) collective-permute-start(bf16[1,352,128]{2,1,0:T(8,128)(2,1)S(1)} %get-tuple-element.163), channel_id=1, source_target_pairs={{0,8},{2,10},{4,12},{6,14},{8,0},{10,2},{12,4},{14,6},{1,9},{3,11}... | collective-permute-start | bytes 270344 | tf_op jit(solution)/shard_map/ppermute | solution.py:726
  73.4 7.1 %collective-permute-start.33 = (bf16[1,352,128]{2,1,0:T(8,128)(2,1)S(1)}, bf16[1,352,128]{2,1,0:T(8,128)(2,1)S(1)}, u32[]{:S(2)}, u32[]{:S(2)}) collective-permute-start(bf16[1,352,128]{2,1,0:T(8,128)(2,1)S(1)} %get-tuple-element.164), channel_id=1, source_target_pairs={{0,12},{2,14},{4,8},{6,10},{8,4},{10,6},{12,0},{14,2},{1,13},{3,15... | collective-permute-start | bytes 270344 | tf_op jit(solution)/shard_map/ppermute | solution.py:726
  80.6 5.6 %collective-permute-start.34 = (bf16[4,176,128]{2,1,0:T(8,128)(2,1)S(1)}, bf16[4,176,128]{2,1,0:T(8,128)(2,1)S(1)}, u32[]{:S(2)}, u32[]{:S(2)}) collective-permute-start(bf16[4,176,128]{2,1,0:T(8,128)(2,1)S(1)} %shard_map.127.refs_0_), channel_id=1, source_target_pairs={{0,2},{2,0},{4,6},{6,4},{8,10},{10,8},{12,14},{14,12},{1,3},{3,1},... | collective-permute-start | bytes 540680 | tf_op jit(solution)/shard_map/ppermute | solution.py:726
  81.4 5.8 %collective-permute-start.35 = (bf16[4,176,128]{2,1,0:T(8,128)(2,1)S(1)}, bf16[4,176,128]{2,1,0:T(8,128)(2,1)S(1)}, u32[]{:S(2)}, u32[]{:S(2)}) collective-permute-start(bf16[4,176,128]{2,1,0:T(8,128)(2,1)S(1)} %shard_map.127.refs_0_), channel_id=1, source_target_pairs={{0,1},{1,0},{2,3},{3,2},{4,5},{5,4},{6,7},{7,6},{8,9},{9,8},{10,11... | collective-permute-start | bytes 540680 | tf_op jit(solution)/shard_map/ppermute | solution.py:721
  (16 other events, 90.4 us)
where the time goes:
time: 91.5 us; the launch traced here: 91.3 us
  waiting for transfers between devices  38.6 us (42%)
  starting transfers between devices  35.3 us (39%)
  Pallas kernels  14.7 us (16%)
  other arithmetic  1.74 us (2%)
    ppermute x24, waiting for transfers between devices, partner_swap(): return lax.ppermute(value, 'latent', [(i, i ^ bits) for i in range(size)])  35.8 us
    ppermute x24, starting transfers between devices, partner_swap(): return lax.ppermute(value, 'latent', [(i, i ^ bits) for i in range(size)])  33.2 us
    pallas_call x27, Pallas kernels, call(): pl.pallas_call(body, out_shape=out_shapes, in_specs=[ONCHIP] * len(operan...  13 us
    ppermute x13, waiting for transfers between devices, swap(): lax.ppermute(value, 'hidden', [(i, (i + 1) % size) for i in range(size)])  2.81 us
    ppermute x13, starting transfers between devices, swap(): lax.ppermute(value, 'hidden', [(i, (i + 1) % size) for i in range(size)])  2.04 us
  transfers between devices with their start and end apart: 37, of which 20 were waited for; matrix products, arithmetic and copies ran while one was open for 1% of the time, Pallas kernels for 8%

commit v1 on v0

--- a/solution.py
+++ b/solution.py
@@ -58,7 +58,7 @@
             )
             self.packed = rows + self.fold_rows
         self.columns = list(range(0, chips, 2))
-        self.doubling = [1 << k for k in reversed(range(1, (chips - 1).bit_length()))]
+        self.doubling = [1 << k for k in range(1, (chips - 1).bit_length())]
         self.doubled = [0]
         for bit in self.doubling:
             self.doubled = self.doubled + [place ^ bit for place in self.doubled]
@@ -527,26 +527,53 @@
 
 def add_with_output_body(plan, count, *refs):
     total = column_total(*refs[:count])
-    first_ref, kept_ref, block_ref, own_ref = refs[count - 1 : count + 3]
+    first_ref, out_ref, block_ref, message_ref, kept_ref = refs[count - 1 : count + 4]
     block_ref[0] = total
-    own_ref[0] = kept_ref[0] + first_ref[1].astype(F32)
-    for place, both_ref in enumerate(refs[count + 3 :], 1):
-        both_ref[0, : plan.chunk, :] = total
-        both_ref[0, plan.chunk :, :] = (
-            kept_ref[place] + first_ref[1 + place].astype(F32)
-        ).astype(BF16)
+    message_ref[0, : plan.chunk, :] = total
+    near = plan.doubling[0]
+    halves = [[], []]
+    for place, column in enumerate(plan.columns):
+        halves[column & near != 0].append(out_ref[place] + first_ref[1 + place].astype(F32))
+    for index, (kept, sent) in enumerate(zip(*halves)):
+        kept_ref[index] = kept
+        start = plan.chunk + index * plan.packed
+        message_ref[0, start : start + plan.packed, :] = sent.astype(BF16)
 
 
 def add_with_output(plan, mine, theirs, got, first, kept):
-    both = shaped(1, plan.chunk + plan.packed, LANES, dtype=BF16)
-    block, out_own, *messages = call(
+    half = len(plan.columns) // 2
+    return call(
         functools.partial(add_with_output_body, plan, 3 + len(got)),
-        [shaped(1, plan.chunk, LANES, dtype=BF16), shaped(1, plan.packed, LANES)]
-        + [both] * (len(plan.columns) - 1),
+        [
+            shaped(1, plan.chunk, LANES, dtype=BF16),
+            shaped(1, plan.chunk + half * plan.packed, LANES, dtype=BF16),
+            shaped(half, plan.packed, LANES),
+        ],
         (mine, theirs, *reversed(got), first, kept),
         moved=mine.size * 12,
     )
-    return block, out_own, messages
+
+
+def halve_body(rows, skip, kept_ref, got_ref, left_ref, sent_ref):
+    half = left_ref.shape[0]
+    for index in range(2 * half):
+        start = skip + index * rows
+        total = kept_ref[index] + got_ref[0, start : start + rows, :].astype(F32)
+        if index < half:
+            left_ref[index] = total
+        else:
+            begin = (index - half) * rows
+            sent_ref[0, begin : begin + rows, :] = total.astype(BF16)
+
+
+def halve(plan, kept, got, skip):
+    half, rows = kept.shape[0] // 2, plan.packed
+    return call(
+        functools.partial(halve_body, rows, skip),
+        [shaped(half, rows, LANES), shaped(1, half * rows, LANES, dtype=BF16)],
+        (kept, got),
+        moved=kept.size * 10,
+    )
 
 
 def stack_body(places, *refs):
@@ -631,19 +658,17 @@
     )
 
 
-def finish_output_body(plan, own_ref, *refs):
-    total = own_ref[0]
-    for ref in refs[:-1]:
-        total = total + ref[0, plan.chunk :, :].astype(F32)
-    refs[-1][...] = unpack_block(plan, total).astype(BF16)
-
-
-def finish_output(plan, own, messages):
+def finish_output_body(plan, kept_ref, got_ref, out_ref):
+    total = kept_ref[0] + got_ref[0].astype(F32)
+    out_ref[...] = unpack_block(plan, total).astype(BF16)
+
+
+def finish_output(plan, kept, got):
     return call(
         functools.partial(finish_output_body, plan),
         shaped(plan.rows, plan.own, dtype=BF16),
-        (own, *reversed(messages)),
-        moved=own.size * 8,
+        (kept, got),
+        moved=kept.size * 8,
     )
 
 
@@ -819,13 +844,18 @@
     sent, sent_first, out_kept = tie(sent, sent_first, out_kept)
     got = to_column(plan, sent)
     first = cross(sent_first)
-    block, out_own, messages = add_with_output(plan, own_kept, kept, got, first, out_kept)
-    got = list(tie(*to_column(plan, messages)))
+    block, message, out_kept = add_with_output(plan, own_kept, kept, got, first, out_kept)
+    got = to_column(plan, [message] + [block] * (len(plan.columns) - 2))
     stack = stack_up(plan, block, got)
-    stack, scaled_late, inputs_late = tie(stack, scaled, inputs)
-    crossed, stack_other = cross(stack), swap(stack)
+    out_kept, out_sent = halve(plan, out_kept, got[0], plan.chunk)
+    stack, scaled_late, inputs_late, out_sent = tie(stack, scaled, inputs, out_sent)
+    stack_other, crossed = swap(stack), cross(stack)
     prepared = prepare(plan, scaled_late, inputs_late, gain, inverse)
-    block_output = finish_output(plan, out_own, got)
+    for bit in reversed(plan.doubling[2:]):
+        out_kept, out_sent = halve(plan, out_kept, partner_swap(out_sent, bit), 0)
+    out_got = partner_swap(out_sent, plan.doubling[1])
+    stack_other, crossed, out_got = tie(stack_other, crossed, out_got)
+    block_output = finish_output(plan, out_kept, out_got)
     grad_own = line_up(plan, stack, crossed)
     grad_other = line_up(plan, stack_other, swap(crossed))
     dictionary_grad = dictionary_step(

time: 91.5 us -> 91.9 us (level)
    ppermute x24 -> x25, starting transfers between devices: 33.2 us -> 34 us  [partner_swap(): return lax.ppermute(value, 'latent', [(i, i ^ bits) for i in range(size)])]
    ppermute x24 -> x25, waiting for transfers between devices: 35.8 us -> 35.4 us  [partner_swap(): return lax.ppermute(value, 'latent', [(i, i ^ bits) for i in range(size)])]
    pallas_call x27 -> x28, Pallas kernels: 13 us -> 13 us  [call(): pl.pallas_call(body, out_shape=out_shapes, in_specs=[ONCHIP] * len(operan...]
  transfers between devices with their start and end apart: 37 -> 38, of which waited for: 20 -> 21; matrix products, arithmetic and copies ran while one was open for 1% -> 1% of each run, Pallas kernels for 8% -> 8%
where the time goes in v1:
time: 91.9 us; the launch traced here: 91.7 us
  waiting for transfers between devices  38.3 us (42%)
  starting transfers between devices  36 us (39%)
  Pallas kernels  14.7 us (16%)
  other arithmetic  1.74 us (2%)
    ppermute x25, waiting for transfers between devices, partner_swap(): return lax.ppermute(value, 'latent', [(i, i ^ bits) for i in range(size)])  35.4 us
    ppermute x25, starting transfers between devices, partner_swap(): return lax.ppermute(value, 'latent', [(i, i ^ bits) for i in range(size)])  34 us
    pallas_call x28, Pallas kernels, call(): pl.pallas_call(body, out_shape=out_shapes, in_specs=[ONCHIP] * len(operan...  13 us
    ppermute x13, waiting for transfers between devices, swap(): lax.ppermute(value, 'hidden', [(i, (i + 1) % size) for i in range(size)])  2.86 us
    ppermute x13, starting transfers between devices, swap(): lax.ppermute(value, 'hidden', [(i, (i + 1) % size) for i in range(size)])  1.97 us
  transfers between devices with their start and end apart: 38, of which 21 were waited for; matrix products, arithmetic and copies ran while one was open for 1% of the time, Pallas kernels for 8%

profile of v1, /device:TPU:0, one launch (start us, length us, event | category | flops | bytes accessed | tf_op | source)
XLA Modules:
  0.0 91.7 jit_solution(12557854082477933149)
XLA Ops:
  1.7 5.1 %collective-permute-start.2 = (bf16[1,176,128]{2,1,0:T(8,128)(2,1)S(1)}, bf16[1,176,128]{2,1,0:T(8,128)(2,1)S(1)}, u32[]{:S(2)}, u32[]{:S(2)}) collective-permute-start(bf16[1,176,128]{2,1,0:T(8,128)(2,1)S(1)} %get-tuple-element.91.refs_0_), channel_id=1, source_target_pairs={{0,12},{2,14},{4,8},{6,10},{8,4},{10,6},{12,0},{14,2},{1,13},{3,15... | collective-permute-start | bytes 135176 | tf_op jit(solution)/shard_map/ppermute | solution.py:751
  8.9 2.9 %collective-permute-done.1.refs_2_ = bf16[1,176,128]{2,1,0:T(8,128)(2,1)S(1)} collective-permute-done((bf16[1,176,128]{2,1,0:T(8,128)(2,1)S(1)}, bf16[1,176,128]{2,1,0:T(8,128)(2,1)S(1)}, u32[]{:S(2)}, u32[]{:S(2)}) %collective-permute-start.1) | collective-permute-done | bytes 45088 | tf_op jit(solution)/shard_map/ppermute | solution.py:751
  13.8 1.7 %shard_map.106 = (bf16[512,2304]{1,0:T(8,128)(2,1)S(1)}, f32[1,512]{1,0:T(1,128)S(1)}, f32[1,2304]{1,0:T(1,128)S(1)}, f32[1,2304]{1,0:T(1,128)S(1)}) custom-call(bf16[512,2304]{1,0:T(8,128)(2,1)} %dict_hbm, f32[1,5120]{1,0:T(1,128)S(1)} %bitcast.3), custom_call_target="tpu_custom_call" | custom-call | bytes 4718592 | tf_op jit(solution)/shard_map/pallas_call | solution.py:246
  15.5 2.0 %collective-permute-done.5.refs_1_ = bf16[1,176,128]{2,1,0:T(8,128)(2,1)S(1)} collective-permute-done((bf16[1,176,128]{2,1,0:T(8,128)(2,1)S(1)}, bf16[1,176,128]{2,1,0:T(8,128)(2,1)S(1)}, u32[]{:S(2)}, u32[]{:S(2)}) %collective-permute-start.5) | collective-permute-done | bytes 45088 | tf_op jit(solution)/shard_map/ppermute | solution.py:751
  19.0 1.7 %shard_map.108 = (bf16[144,2304]{1,0:T(8,128)(2,1)S(1)}, bf16[144,512]{1,0:T(8,128)(2,1)S(1)}, f32[4,176,128]{2,1,0:T(8,128)S(1)}, f32[4,176,128]{2,1,0:T(8,128)S(1)}) custom-call(bf16[4,176,128]{2,1,0:T(8,128)(2,1)S(1)} %shard_map.105.refs_0_, bf16[4,176,128]{2,1,0:T(8,128)(2,1)S(1)} %collective-permute-done.4.refs_1_, ...), custom_call_target="tpu_custom_call" | custom-call | flops 509607936 | bytes 2359296 | tf_op jit(solution)/shard_map/pallas_call | solution.py:113
  23.8 2.0 %collective-permute-start.10 = (bf16[2,176,128]{2,1,0:T(8,128)(2,1)S(1)}, bf16[2,176,128]{2,1,0:T(8,128)(2,1)S(1)}, u32[]{:S(2)}, u32[]{:S(2)}) collective-permute-start(bf16[2,176,128]{2,1,0:T(8,128)(2,1)S(1)} %shard_map.107.here_ref), channel_id=1, source_target_pairs={{0,8},{2,10},{4,12},{6,14},{8,0},{10,2},{12,4},{14,6},{1,9},{3,11}... | collective-permute-start | bytes 270344 | tf_op jit(solution)/shard_map/ppermute | solution.py:751
  25.8 2.3 %collective-permute-done.9.got_ref = bf16[3,176,128]{2,1,0:T(8,128)(2,1)S(1)} collective-permute-done((bf16[3,176,128]{2,1,0:T(8,128)(2,1)S(1)}, bf16[3,176,128]{2,1,0:T(8,128)(2,1)S(1)}, u32[]{:S(2)}, u32[]{:S(2)}) %collective-permute-start.9) | collective-permute-done | bytes 135200 | tf_op jit(solution)/shard_map/ppermute | solution.py:751
  28.2 2.7 %collective-permute-done.10.there_ref = bf16[2,176,128]{2,1,0:T(8,128)(2,1)S(1)} collective-permute-done((bf16[2,176,128]{2,1,0:T(8,128)(2,1)S(1)}, bf16[2,176,128]{2,1,0:T(8,128)(2,1)S(1)}, u32[]{:S(2)}, u32[]{:S(2)}) %collective-permute-start.10) | collective-permute-done | bytes 90144 | tf_op jit(solution)/shard_map/ppermute | solution.py:751
  31.6 2.1 %collective-permute-start.11 = (bf16[1,176,128]{2,1,0:T(8,128)(2,1)S(1)}, bf16[1,176,128]{2,1,0:T(8,128)(2,1)S(1)}, u32[]{:S(2)}, u32[]{:S(2)}) collective-permute-start(bf16[1,176,128]{2,1,0:T(8,128)(2,1)S(1)} %get-tuple-element.120), channel_id=1, source_target_pairs={{0,12},{2,14},{4,8},{6,10},{8,4},{10,6},{12,0},{14,2},{1,13},{3,15... | collective-permute-start | bytes 135176 | tf_op jit(solution)/shard_map/ppermute | solution.py:751
  33.8 2.2 %collective-permute-start.13 = (bf16[1,176,128]{2,1,0:T(8,128)(2,1)S(1)}, bf16[1,176,128]{2,1,0:T(8,128)(2,1)S(1)}, u32[]{:S(2)}, u32[]{:S(2)}) collective-permute-start(bf16[1,176,128]{2,1,0:T(8,128)(2,1)S(1)} %get-tuple-element.122), channel_id=1, source_target_pairs={{0,4},{2,6},{4,0},{6,2},{8,12},{10,14},{12,8},{14,10},{1,5},{3,7},... | collective-permute-start | bytes 135176 | tf_op jit(solution)/shard_map/ppermute | solution.py:751
  36.0 1.6 %collective-permute-done.11.refs_2_ = bf16[1,176,128]{2,1,0:T(8,128)(2,1)S(1)} collective-permute-done((bf16[1,176,128]{2,1,0:T(8,128)(2,1)S(1)}, bf16[1,176,128]{2,1,0:T(8,128)(2,1)S(1)}, u32[]{:S(2)}, u32[]{:S(2)}) %collective-permute-start.11) | collective-permute-done | bytes 45088 | tf_op jit(solution)/shard_map/ppermute | solution.py:751
  38.8 2.2 %collective-permute-start.17 = (bf16[1,176,128]{2,1,0:T(8,128)(2,1)S(1)}, bf16[1,176,128]{2,1,0:T(8,128)(2,1)S(1)}, u32[]{:S(2)}, u32[]{:S(2)}) collective-permute-start(bf16[1,176,128]{2,1,0:T(8,128)(2,1)S(1)} %get-tuple-element.127.refs_0_), channel_id=1, source_target_pairs={{0,12},{2,14},{4,8},{6,10},{8,4},{10,6},{12,0},{14,2},{1,13},{3,15... | collective-permute-start | bytes 135176 | tf_op jit(solution)/shard_map/ppermute | solution.py:751
  41.7 1.6 %collective-permute-start.15 = (bf16[1,176,128]{2,1,0:T(8,128)(2,1)S(1)}, bf16[1,176,128]{2,1,0:T(8,128)(2,1)S(1)}, u32[]{:S(2)}, u32[]{:S(2)}) collective-permute-start(bf16[1,176,128]{2,1,0:T(8,128)(2,1)S(1)} %get-tuple-element.127.refs_0_), channel_id=1, source_target_pairs={{0,4},{2,6},{4,0},{6,2},{8,12},{10,14},{12,8},{14,10},{1,5},{3,7},... | collective-permute-start | bytes 135176 | tf_op jit(solution)/shard_map/ppermute | solution.py:751
  44.7 1.6 %collective-permute-done.16.refs_2_ = bf16[1,176,128]{2,1,0:T(8,128)(2,1)S(1)} collective-permute-done((bf16[1,176,128]{2,1,0:T(8,128)(2,1)S(1)}, bf16[1,176,128]{2,1,0:T(8,128)(2,1)S(1)}, u32[]{:S(2)}, u32[]{:S(2)}) %collective-permute-start.16) | collective-permute-done | bytes 45088 | tf_op jit(solution)/shard_map/ppermute | solution.py:751
  49.0 2.9 %collective-permute-done.19.refs_1_ = bf16[4,176,128]{2,1,0:T(8,128)(2,1)S(1)} collective-permute-done((bf16[4,176,128]{2,1,0:T(8,128)(2,1)S(1)}, bf16[4,176,128]{2,1,0:T(8,128)(2,1)S(1)}, u32[]{:S(2)}, u32[]{:S(2)}) %collective-permute-start.19) | collective-permute-done | bytes 180256 | tf_op jit(solution)/shard_map/ppermute | solution.py:751
  53.4 1.6 %shard_map.119 = (bf16[144,2304]{1,0:T(8,128)(2,1)S(1)}, f32[144,1]{1,0:T(8,128)S(1)}, bf16[144,512]{1,0:T(8,128)(2,1)S(1)}, bf16[144,512]{1,0:T(8,128)(2,1)S(1)...) custom-call(bf16[8,176,128]{2,1,0:T(8,128)(2,1)S(1)} %shard_map.116.other_ref, ...), custom_call_target="tpu_custom_call" | custom-call | flops 1019215872 | bytes 4718592 | tf_op jit(solution)/shard_map/pallas_call | solution.py:113
  58.9 4.5 %collective-permute-done.25.got_ref = bf16[3,176,128]{2,1,0:T(8,128)(2,1)S(1)} collective-permute-done((bf16[3,176,128]{2,1,0:T(8,128)(2,1)S(1)}, bf16[3,176,128]{2,1,0:T(8,128)(2,1)S(1)}, u32[]{:S(2)}, u32[]{:S(2)}) %collective-permute-start.25) | collective-permute-done | bytes 135200 | tf_op jit(solution)/shard_map/ppermute | solution.py:751
  64.9 2.0 %collective-permute-start.27 = (bf16[1,176,128]{2,1,0:T(8,128)(2,1)S(1)}, bf16[1,176,128]{2,1,0:T(8,128)(2,1)S(1)}, u32[]{:S(2)}, u32[]{:S(2)}) collective-permute-start(bf16[1,176,128]{2,1,0:T(8,128)(2,1)S(1)} %get-tuple-element.157), channel_id=1, source_target_pairs={{0,12},{2,14},{4,8},{6,10},{8,4},{10,6},{12,0},{14,2},{1,13},{3,15... | collective-permute-start | bytes 135176 | tf_op jit(solution)/shard_map/ppermute | solution.py:751
  67.4 2.0 %collective-permute-start.29 = (bf16[1,176,128]{2,1,0:T(8,128)(2,1)S(1)}, bf16[1,176,128]{2,1,0:T(8,128)(2,1)S(1)}, u32[]{:S(2)}, u32[]{:S(2)}) collective-permute-start(bf16[1,176,128]{2,1,0:T(8,128)(2,1)S(1)} %get-tuple-element.159), channel_id=1, source_target_pairs={{0,4},{2,6},{4,0},{6,2},{8,12},{10,14},{12,8},{14,10},{1,5},{3,7},... | collective-permute-start | bytes 135176 | tf_op jit(solution)/shard_map/ppermute | solution.py:751
  69.3 1.6 %collective-permute-done.27.refs_2_ = bf16[1,176,128]{2,1,0:T(8,128)(2,1)S(1)} collective-permute-done((bf16[1,176,128]{2,1,0:T(8,128)(2,1)S(1)}, bf16[1,176,128]{2,1,0:T(8,128)(2,1)S(1)}, u32[]{:S(2)}, u32[]{:S(2)}) %collective-permute-start.27) | collective-permute-done | bytes 45088 | tf_op jit(solution)/shard_map/ppermute | solution.py:751
  73.5 2.0 %collective-permute-start.33 = (bf16[1,176,128]{2,1,0:T(8,128)(2,1)S(1)}, bf16[1,176,128]{2,1,0:T(8,128)(2,1)S(1)}, u32[]{:S(2)}, u32[]{:S(2)}) collective-permute-start(bf16[1,176,128]{2,1,0:T(8,128)(2,1)S(1)} %get-tuple-element.165.refs_0_), channel_id=1, source_target_pairs={{0,12},{2,14},{4,8},{6,10},{8,4},{10,6},{12,0},{14,2},{1,13},{3,15... | collective-permute-start | bytes 135176 | tf_op jit(solution)/shard_map/ppermute | solution.py:751
  75.8 2.5 %collective-permute-done.31.got_ref.refs_1_ = bf16[1,528,128]{2,1,0:T(8,128)(2,1)S(1)} collective-permute-done((bf16[1,528,128]{2,1,0:T(8,128)(2,1)S(1)}, bf16[1,528,128]{2,1,0:T(8,128)(2,1)S(1)}, u32[]{:S(2)}, u32[]{:S(2)}) %collective-permute-start.31) | collective-permute-done | bytes 135200 | tf_op jit(solution)/shard_map/ppermute | solution.py:751
  81.7 4.8 %collective-permute-done.36.got_ref = bf16[1,176,128]{2,1,0:T(8,128)(2,1)S(1)} collective-permute-done((bf16[1,176,128]{2,1,0:T(8,128)(2,1)S(1)}, bf16[1,176,128]{2,1,0:T(8,128)(2,1)S(1)}, u32[]{:S(2)}, u32[]{:S(2)}) %collective-permute-start.36) | collective-permute-done | bytes 45088 | tf_op jit(solution)/shard_map/ppermute | solution.py:751
  88.0 3.7 %shard_map.132 = bf16[512,2304]{1,0:T(8,128)(2,1)} custom-call(bf16[8,176,128]{2,1,0:T(8,128)(2,1)S(1)} %shard_map.129.own_ref, bf16[8,176,128]{2,1,0:T(8,128)(2,1)S(1)} %shard_map.130.other_ref, bf16[144,2304]{1,0:T(8,128)(2,1)S(1)} %get-tuple-element.174.scaled_ref, f32[144,2304]{1,0:T(8,128)S(1)} %get-tuple-element.177.factor_ref, ...), custom_call_target="tpu_custom_call" | custom-call | flops 1019215872 | bytes 4718592 | tf_op jit(solution)/shard_map/pallas_call | solution.py:113
  (89 shorter events, 31.6 us)
Async XLA Ops:
  1.7 7.2 %collective-permute-start.2 = (bf16[1,176,128]{2,1,0:T(8,128)(2,1)S(1)}, bf16[1,176,128]{2,1,0:T(8,128)(2,1)S(1)}, u32[]{:S(2)}, u32[]{:S(2)}) collective-permute-start(bf16[1,176,128]{2,1,0:T(8,128)(2,1)S(1)} %get-tuple-element.91.refs_0_), channel_id=1, source_target_pairs={{0,12},{2,14},{4,8},{6,10},{8,4},{10,6},{12,0},{14,2},{1,13},{3,15... | collective-permute-start | bytes 135176 | tf_op jit(solution)/shard_map/ppermute | solution.py:751
  6.9 4.9 %collective-permute-start.1 = (bf16[1,176,128]{2,1,0:T(8,128)(2,1)S(1)}, bf16[1,176,128]{2,1,0:T(8,128)(2,1)S(1)}, u32[]{:S(2)}, u32[]{:S(2)}) collective-permute-start(bf16[1,176,128]{2,1,0:T(8,128)(2,1)S(1)} %get-tuple-element.91.refs_0_), channel_id=1, source_target_pairs={{0,8},{2,10},{4,12},{6,14},{8,0},{10,2},{12,4},{14,6},{1,9},{3,11}... | collective-permute-start | bytes 135176 | tf_op jit(solution)/shard_map/ppermute | solution.py:751
  6.9 4.9 %collective-permute-start = (bf16[1,176,128]{2,1,0:T(8,128)(2,1)S(1)}, bf16[1,176,128]{2,1,0:T(8,128)(2,1)S(1)}, u32[]{:S(2)}, u32[]{:S(2)}) collective-permute-start(bf16[1,176,128]{2,1,0:T(8,128)(2,1)S(1)} %get-tuple-element.91.refs_0_), channel_id=1, source_target_pairs={{0,4},{2,6},{4,0},{6,2},{8,12},{10,14},{12,8},{14,10},{1,5},{3,7},... | collective-permute-start | bytes 135176 | tf_op jit(solution)/shard_map/ppermute | solution.py:751
  11.8 5.6 %collective-permute-start.4 = (bf16[4,176,128]{2,1,0:T(8,128)(2,1)S(1)}, bf16[4,176,128]{2,1,0:T(8,128)(2,1)S(1)}, u32[]{:S(2)}, u32[]{:S(2)}) collective-permute-start(bf16[4,176,128]{2,1,0:T(8,128)(2,1)S(1)} %shard_map.105.refs_0_), channel_id=1, source_target_pairs={{0,2},{2,0},{4,6},{6,4},{8,10},{10,8},{12,14},{14,12},{1,3},{3,1},... | collective-permute-start | bytes 540680 | tf_op jit(solution)/shard_map/ppermute | solution.py:751
  20.8 5.0 %collective-permute-start.7 = (f32[4,176,128]{2,1,0:T(8,128)S(1)}, f32[4,176,128]{2,1,0:T(8,128)S(1)}, u32[]{:S(2)}, u32[]{:S(2)}) collective-permute-start(f32[4,176,128]{2,1,0:T(8,128)S(1)} %get-tuple-element.109), channel_id=1, source_target_pairs={{0,1},{1,0},{2,3},{3,2},{4,5},{5,4},{6,7},{7,6},{8,9},{9,8},{10,11... | collective-permute-start | bytes 1081352 | tf_op jit(solution)/shard_map/ppermute | solution.py:746
  22.4 5.7 %collective-permute-start.9 = (bf16[3,176,128]{2,1,0:T(8,128)(2,1)S(1)}, bf16[3,176,128]{2,1,0:T(8,128)(2,1)S(1)}, u32[]{:S(2)}, u32[]{:S(2)}) collective-permute-start(bf16[3,176,128]{2,1,0:T(8,128)(2,1)S(1)} %get-tuple-element.114), channel_id=1, source_target_pairs={{0,2},{2,0},{4,6},{6,4},{8,10},{10,8},{12,14},{14,12},{1,3},{3,1},... | collective-permute-start | bytes 405512 | tf_op jit(solution)/shard_map/ppermute | solution.py:751
  23.8 7.0 %collective-permute-start.10 = (bf16[2,176,128]{2,1,0:T(8,128)(2,1)S(1)}, bf16[2,176,128]{2,1,0:T(8,128)(2,1)S(1)}, u32[]{:S(2)}, u32[]{:S(2)}) collective-permute-start(bf16[2,176,128]{2,1,0:T(8,128)(2,1)S(1)} %shard_map.107.here_ref), channel_id=1, source_target_pairs={{0,8},{2,10},{4,12},{6,14},{8,0},{10,2},{12,4},{14,6},{1,9},{3,11}... | collective-permute-start | bytes 270344 | tf_op jit(solution)/shard_map/ppermute | solution.py:751
  30.9 7.8 %collective-permute-start.14 = (bf16[5,176,128]{2,1,0:T(8,128)(2,1)S(1)}, bf16[5,176,128]{2,1,0:T(8,128)(2,1)S(1)}, u32[]{:S(2)}, u32[]{:S(2)}) collective-permute-start(bf16[5,176,128]{2,1,0:T(8,128)(2,1)S(1)} %get-tuple-element.126), channel_id=1, source_target_pairs={{0,2},{2,0},{4,6},{6,4},{8,10},{10,8},{12,14},{14,12},{1,3},{3,1},... | collective-permute-start | bytes 675848 | tf_op jit(solution)/shard_map/ppermute | solution.py:751
  31.6 6.0 %collective-permute-start.11 = (bf16[1,176,128]{2,1,0:T(8,128)(2,1)S(1)}, bf16[1,176,128]{2,1,0:T(8,128)(2,1)S(1)}, u32[]{:S(2)}, u32[]{:S(2)}) collective-permute-start(bf16[1,176,128]{2,1,0:T(8,128)(2,1)S(1)} %get-tuple-element.120), channel_id=1, source_target_pairs={{0,12},{2,14},{4,8},{6,10},{8,4},{10,6},{12,0},{14,2},{1,13},{3,15... | collective-permute-start | bytes 135176 | tf_op jit(solution)/shard_map/ppermute | solution.py:751
  33.8 4.9 %collective-permute-start.12 = (bf16[1,176,128]{2,1,0:T(8,128)(2,1)S(1)}, bf16[1,176,128]{2,1,0:T(8,128)(2,1)S(1)}, u32[]{:S(2)}, u32[]{:S(2)}) collective-permute-start(bf16[1,176,128]{2,1,0:T(8,128)(2,1)S(1)} %get-tuple-element.121), channel_id=1, source_target_pairs={{0,8},{2,10},{4,12},{6,14},{8,0},{10,2},{12,4},{14,6},{1,9},{3,11}... | collective-permute-start | bytes 135176 | tf_op jit(solution)/shard_map/ppermute | solution.py:751
  33.8 4.9 %collective-permute-start.13 = (bf16[1,176,128]{2,1,0:T(8,128)(2,1)S(1)}, bf16[1,176,128]{2,1,0:T(8,128)(2,1)S(1)}, u32[]{:S(2)}, u32[]{:S(2)}) collective-permute-start(bf16[1,176,128]{2,1,0:T(8,128)(2,1)S(1)} %get-tuple-element.122), channel_id=1, source_target_pairs={{0,4},{2,6},{4,0},{6,2},{8,12},{10,14},{12,8},{14,10},{1,5},{3,7},... | collective-permute-start | bytes 135176 | tf_op jit(solution)/shard_map/ppermute | solution.py:751
  38.8 5.9 %collective-permute-start.17 = (bf16[1,176,128]{2,1,0:T(8,128)(2,1)S(1)}, bf16[1,176,128]{2,1,0:T(8,128)(2,1)S(1)}, u32[]{:S(2)}, u32[]{:S(2)}) collective-permute-start(bf16[1,176,128]{2,1,0:T(8,128)(2,1)S(1)} %get-tuple-element.127.refs_0_), channel_id=1, source_target_pairs={{0,12},{2,14},{4,8},{6,10},{8,4},{10,6},{12,0},{14,2},{1,13},{3,15... | collective-permute-start | bytes 135176 | tf_op jit(solution)/shard_map/ppermute | solution.py:751
  41.0 5.3 %collective-permute-start.16 = (bf16[1,176,128]{2,1,0:T(8,128)(2,1)S(1)}, bf16[1,176,128]{2,1,0:T(8,128)(2,1)S(1)}, u32[]{:S(2)}, u32[]{:S(2)}) collective-permute-start(bf16[1,176,128]{2,1,0:T(8,128)(2,1)S(1)} %get-tuple-element.127.refs_0_), channel_id=1, source_target_pairs={{0,8},{2,10},{4,12},{6,14},{8,0},{10,2},{12,4},{14,6},{1,9},{3,11}... | collective-permute-start | bytes 135176 | tf_op jit(solution)/shard_map/ppermute | solution.py:751
  46.3 5.6 %collective-permute-start.19 = (bf16[4,176,128]{2,1,0:T(8,128)(2,1)S(1)}, bf16[4,176,128]{2,1,0:T(8,128)(2,1)S(1)}, u32[]{:S(2)}, u32[]{:S(2)}) collective-permute-start(bf16[4,176,128]{2,1,0:T(8,128)(2,1)S(1)} %shard_map.114.refs_0_), channel_id=1, source_target_pairs={{0,2},{2,0},{4,6},{6,4},{8,10},{10,8},{12,14},{14,12},{1,3},{3,1},... | collective-permute-start | bytes 540680 | tf_op jit(solution)/shard_map/ppermute | solution.py:751
  57.3 6.1 %collective-permute-start.26 = (bf16[8,176,128]{2,1,0:T(8,128)(2,1)S(1)}, bf16[8,176,128]{2,1,0:T(8,128)(2,1)S(1)}, u32[]{:S(2)}, u32[]{:S(2)}) collective-permute-start(bf16[8,176,128]{2,1,0:T(8,128)(2,1)S(1)} %get-tuple-element.154), channel_id=1, source_target_pairs={{0,1},{1,0},{2,3},{3,2},{4,5},{5,4},{6,7},{7,6},{8,9},{9,8},{10,11... | collective-permute-start | bytes 1081352 | tf_op jit(solution)/shard_map/ppermute | solution.py:746
  57.5 5.8 %collective-permute-start.25 = (bf16[3,176,128]{2,1,0:T(8,128)(2,1)S(1)}, bf16[3,176,128]{2,1,0:T(8,128)(2,1)S(1)}, u32[]{:S(2)}, u32[]{:S(2)}) collective-permute-start(bf16[3,176,128]{2,1,0:T(8,128)(2,1)S(1)} %get-tuple-element.148), channel_id=1, source_target_pairs={{0,2},{2,0},{4,6},{6,4},{8,10},{10,8},{12,14},{14,12},{1,3},{3,1},... | collective-permute-start | bytes 405512 | tf_op jit(solution)/shard_map/ppermute | solution.py:751
  63.5 8.7 %collective-permute-start.30 = (bf16[5,176,128]{2,1,0:T(8,128)(2,1)S(1)}, bf16[5,176,128]{2,1,0:T(8,128)(2,1)S(1)}, u32[]{:S(2)}, u32[]{:S(2)}) collective-permute-start(bf16[5,176,128]{2,1,0:T(8,128)(2,1)S(1)} %get-tuple-element.160), channel_id=1, source_target_pairs={{0,2},{2,0},{4,6},{6,4},{8,10},{10,8},{12,14},{14,12},{1,3},{3,1},... | collective-permute-start | bytes 675848 | tf_op jit(solution)/shard_map/ppermute | solution.py:751
  64.9 6.0 %collective-permute-start.27 = (bf16[1,176,128]{2,1,0:T(8,128)(2,1)S(1)}, bf16[1,176,128]{2,1,0:T(8,128)(2,1)S(1)}, u32[]{:S(2)}, u32[]{:S(2)}) collective-permute-start(bf16[1,176,128]{2,1,0:T(8,128)(2,1)S(1)} %get-tuple-element.157), channel_id=1, source_target_pairs={{0,12},{2,14},{4,8},{6,10},{8,4},{10,6},{12,0},{14,2},{1,13},{3,15... | collective-permute-start | bytes 135176 | tf_op jit(solution)/shard_map/ppermute | solution.py:751
  66.9 5.2 %collective-permute-start.28 = (bf16[1,176,128]{2,1,0:T(8,128)(2,1)S(1)}, bf16[1,176,128]{2,1,0:T(8,128)(2,1)S(1)}, u32[]{:S(2)}, u32[]{:S(2)}) collective-permute-start(bf16[1,176,128]{2,1,0:T(8,128)(2,1)S(1)} %get-tuple-element.158), channel_id=1, source_target_pairs={{0,8},{2,10},{4,12},{6,14},{8,0},{10,2},{12,4},{14,6},{1,9},{3,11}... | collective-permute-start | bytes 135176 | tf_op jit(solution)/shard_map/ppermute | solution.py:751
  72.3 6.0 %collective-permute-start.31 = (bf16[1,528,128]{2,1,0:T(8,128)(2,1)S(1)}, bf16[1,528,128]{2,1,0:T(8,128)(2,1)S(1)}, u32[]{:S(2)}, u32[]{:S(2)}) collective-permute-start(bf16[1,528,128]{2,1,0:T(8,128)(2,1)S(1)} %get-tuple-element.163), channel_id=1, source_target_pairs={{0,4},{2,6},{4,0},{6,2},{8,12},{10,14},{12,8},{14,10},{1,5},{3,7},... | collective-permute-start | bytes 405512 | tf_op jit(solution)/shard_map/ppermute | solution.py:751
  73.5 5.8 %collective-permute-start.33 = (bf16[1,176,128]{2,1,0:T(8,128)(2,1)S(1)}, bf16[1,176,128]{2,1,0:T(8,128)(2,1)S(1)}, u32[]{:S(2)}, u32[]{:S(2)}) collective-permute-start(bf16[1,176,128]{2,1,0:T(8,128)(2,1)S(1)} %get-tuple-element.165.refs_0_), channel_id=1, source_target_pairs={{0,12},{2,14},{4,8},{6,10},{8,4},{10,6},{12,0},{14,2},{1,13},{3,15... | collective-permute-start | bytes 135176 | tf_op jit(solution)/shard_map/ppermute | solution.py:751
  80.5 6.1 %collective-permute-start.35 = (bf16[4,176,128]{2,1,0:T(8,128)(2,1)S(1)}, bf16[4,176,128]{2,1,0:T(8,128)(2,1)S(1)}, u32[]{:S(2)}, u32[]{:S(2)}) collective-permute-start(bf16[4,176,128]{2,1,0:T(8,128)(2,1)S(1)} %shard_map.127.refs_0_), channel_id=1, source_target_pairs={{0,2},{2,0},{4,6},{6,4},{8,10},{10,8},{12,14},{14,12},{1,3},{3,1},... | collective-permute-start | bytes 540680 | tf_op jit(solution)/shard_map/ppermute | solution.py:751
  81.2 5.3 %collective-permute-start.34 = (bf16[4,176,128]{2,1,0:T(8,128)(2,1)S(1)}, bf16[4,176,128]{2,1,0:T(8,128)(2,1)S(1)}, u32[]{:S(2)}, u32[]{:S(2)}) collective-permute-start(bf16[4,176,128]{2,1,0:T(8,128)(2,1)S(1)} %shard_map.127.refs_0_), channel_id=1, source_target_pairs={{0,1},{1,0},{2,3},{3,2},{4,5},{5,4},{6,7},{7,6},{8,9},{9,8},{10,11... | collective-permute-start | bytes 540680 | tf_op jit(solution)/shard_map/ppermute | solution.py:746
  81.2 5.3 %collective-permute-start.36 = (bf16[1,176,128]{2,1,0:T(8,128)(2,1)S(1)}, bf16[1,176,128]{2,1,0:T(8,128)(2,1)S(1)}, u32[]{:S(2)}, u32[]{:S(2)}) collective-permute-start(bf16[1,176,128]{2,1,0:T(8,128)(2,1)S(1)} %get-tuple-element.170), channel_id=1, source_target_pairs={{0,8},{2,10},{4,12},{6,14},{8,0},{10,2},{12,4},{14,6},{1,9},{3,11}... | collective-permute-start | bytes 135176 | tf_op jit(solution)/shard_map/ppermute | solution.py:751
  (17 other events, 100.6 us)

commit v2 on v1

--- a/solution.py
+++ b/solution.py
@@ -60,7 +60,7 @@
         self.columns = list(range(0, chips, 2))
         self.doubling = [1 << k for k in range(1, (chips - 1).bit_length())]
         self.doubled = [0]
-        for bit in self.doubling:
+        for bit in reversed(self.doubling):
             self.doubled = self.doubled + [place ^ bit for place in self.doubled]
 
     def side_blocks(self, refs):
@@ -424,29 +424,49 @@
     )
 
 
-def project_body(plan, hidden_ref, down_ref, mine_ref, theirs_ref, both):
-    core = lax.axis_index("hidden")
-    terms = jnp.dot(hidden_ref[...], down_ref[...], preferred_element_type=F32).astype(BF16)
-    for chip in range(plan.chips):
-        for side in range(plan.cores):
-            start = (chip * plan.cores + side) * plan.own
-            main, tail = pack_block(plan, terms[:, start : start + plan.own])
-            both[side, chip, : plan.rows, :] = main
-            both[side, chip, plan.rows :, :] = tail
-    mine_ref[...] = both[core]
-    theirs_ref[...] = both[1 - core]
+def pack_side(plan, terms_ref, side, out_ref):
+    for core in range(plan.cores):
+
+        @pl.when(side == core)
+        def _():
+            for chip in range(plan.chips):
+                start = (chip * plan.cores + core) * plan.own
+                main, tail = pack_block(plan, terms_ref[:, start : start + plan.own])
+                out_ref[chip, : plan.rows, :] = main
+                out_ref[chip, plan.rows :, :] = tail
+
+
+def project_body(plan, hidden_ref, down_ref, terms_ref, theirs_ref):
+    terms_ref[...] = jnp.dot(
+        hidden_ref[...], down_ref[...], preferred_element_type=F32
+    ).astype(BF16)
+    pack_side(plan, terms_ref, 1 - lax.axis_index("hidden"), theirs_ref)
 
 
 def project(plan, hidden, down_weight):
     units = down_weight.shape[0]
-    shape = (plan.chips, plan.packed, LANES)
     return call(
         functools.partial(project_body, plan),
-        [shaped(*shape, dtype=BF16)] * 2,
+        [
+            shaped(plan.rows, plan.width, dtype=BF16),
+            shaped(plan.chips, plan.packed, LANES, dtype=BF16),
+        ],
         (hidden, down_weight),
-        [both_scratch(plan)],
         flops=2 * plan.rows * plan.width * units,
         moved=down_weight.size * 2,
+    )
+
+
+def pack_own_body(plan, terms_ref, mine_ref):
+    pack_side(plan, terms_ref, lax.axis_index("hidden"), mine_ref)
+
+
+def pack_own(plan, terms):
+    return call(
+        functools.partial(pack_own_body, plan),
+        shaped(plan.chips, plan.packed, LANES, dtype=BF16),
+        (terms,),
+        moved=terms.size * 4,
     )
 
 
@@ -803,7 +823,7 @@
     stack, vectors, late_dictionary, cotangent = tie(stack, vectors, dictionary, cotangent)
     stack_other, crossed = swap(stack), cross(stack)
     encoder = bring_encoder(plan, late_dictionary, vectors)
-    cotangent = double(plan, cotangent, plan.doubling[0])
+    cotangent = double(plan, cotangent, plan.doubling[-1])
     stack_other, crossed, encoder, cotangent = tie(stack_other, crossed, encoder, cotangent)
     brought, bias, decoder, gain = encoder
     inputs, latents, kept, sent = encode(
@@ -813,9 +833,9 @@
     own_kept, own_sent = decode_own(plan, latents, brought, decoder, gain)
     sent_first, sent_rest = add_sent(plan, own_sent, sent)
     sent_rest, cotangent = tie(sent_rest, cotangent)
-    for bit in plan.doubling[1:-1]:
+    for bit in reversed(plan.doubling[1:-1]):
         cotangent = double(plan, cotangent, bit)
-    there = partner_swap(cotangent, plan.doubling[-1])
+    there = partner_swap(cotangent, plan.doubling[0])
     sent = add_across(plan, own_kept, kept, cross(sent_rest))
     sent, sent_first, cotangent, there = tie(sent, sent_first, cotangent, there)
     cotangent, sent_first = add_message(plan, sent_first, cotangent, there)
@@ -835,11 +855,14 @@
     )
     sent, kept = swap(sent), swap(kept)
     own_kept, own_sent = mlp_own(plan, gate_grad, up_grad, gate_weight, up_weight)
-    out_mine, out_theirs = project(plan, hidden, down_weight)
+    out_terms, out_theirs = project(plan, hidden, down_weight)
     sent_first, sent_rest = add_sent(plan, own_sent, sent)
-    sent_first, sent_rest, out_mine, out_theirs = tie(sent_first, sent_rest, out_mine, out_theirs)
+    sent_first, sent_rest, out_terms, out_theirs = tie(
+        sent_first, sent_rest, out_terms, out_theirs
+    )
     crossed = cross(sent_rest)
-    out_kept, sent_first = add_pair(plan, sent_first, out_mine, swap(out_theirs))
+    out_theirs = swap(out_theirs)
+    out_kept, sent_first = add_pair(plan, sent_first, pack_own(plan, out_terms), out_theirs)
     sent = add_across(plan, own_kept, kept, crossed)
     sent, sent_first, out_kept = tie(sent, sent_first, out_kept)
     got = to_column(plan, sent)

time: 91.9 us -> 90.8 us (0.988)
  starting transfers between devices: 36 us -> 35 us
    ppermute x25, starting transfers between devices: 34 us -> 32.9 us  [partner_swap(): return lax.ppermute(value, 'latent', [(i, i ^ bits) for i in range(size)])]
    pallas_call x28 -> x29, Pallas kernels: 13 us -> 13.6 us  [call(): pl.pallas_call(body, out_shape=out_shapes, in_specs=[ONCHIP] * len(operan...]
  transfers between devices with their start and end apart: 38 -> 38, of which waited for: 21 -> 21; matrix products, arithmetic and copies ran while one was open for 1% -> 1% of each run, Pallas kernels for 8% -> 9%
where the time goes in v2:
time: 90.8 us; the launch traced here: 90.6 us
  waiting for transfers between devices  37.5 us (41%)
  starting transfers between devices  35 us (39%)
  Pallas kernels  15.3 us (17%)
  other arithmetic  1.74 us (2%)
  between operations  1.03 us (1%)
    ppermute x25, waiting for transfers between devices, partner_swap(): return lax.ppermute(value, 'latent', [(i, i ^ bits) for i in range(size)])  34.7 us
    ppermute x25, starting transfers between devices, partner_swap(): return lax.ppermute(value, 'latent', [(i, i ^ bits) for i in range(size)])  32.9 us
    pallas_call x29, Pallas kernels, call(): pl.pallas_call(body, out_shape=out_shapes, in_specs=[ONCHIP] * len(operan...  13.6 us
    ppermute x13, waiting for transfers between devices, swap(): lax.ppermute(value, 'hidden', [(i, (i + 1) % size) for i in range(size)])  2.77 us
    ppermute x13, starting transfers between devices, swap(): lax.ppermute(value, 'hidden', [(i, (i + 1) % size) for i in range(size)])  2.12 us
  transfers between devices with their start and end apart: 38, of which 21 were waited for; matrix products, arithmetic and copies ran while one was open for 1% of the time, Pallas kernels for 9%

profile of v2, /device:TPU:0, one launch (start us, length us, event | category | flops | bytes accessed | tf_op | source)
XLA Modules:
  0.0 90.6 jit_solution(5120462621185587625)
XLA Ops:
  1.7 5.1 %collective-permute-start.2 = (bf16[1,176,128]{2,1,0:T(8,128)(2,1)S(1)}, bf16[1,176,128]{2,1,0:T(8,128)(2,1)S(1)}, u32[]{:S(2)}, u32[]{:S(2)}) collective-permute-start(bf16[1,176,128]{2,1,0:T(8,128)(2,1)S(1)} %get-tuple-element.91.refs_0_), channel_id=1, source_target_pairs={{0,12},{2,14},{4,8},{6,10},{8,4},{10,6},{12,0},{14,2},{1,13},{3,15... | collective-permute-start | bytes 135176 | tf_op jit(solution)/shard_map/ppermute | solution.py:771
  8.9 2.9 %collective-permute-done.1.refs_2_ = bf16[1,176,128]{2,1,0:T(8,128)(2,1)S(1)} collective-permute-done((bf16[1,176,128]{2,1,0:T(8,128)(2,1)S(1)}, bf16[1,176,128]{2,1,0:T(8,128)(2,1)S(1)}, u32[]{:S(2)}, u32[]{:S(2)}) %collective-permute-start.1) | collective-permute-done | bytes 45088 | tf_op jit(solution)/shard_map/ppermute | solution.py:771
  11.8 1.6 %collective-permute-start.4 = (bf16[4,176,128]{2,1,0:T(8,128)(2,1)S(1)}, bf16[4,176,128]{2,1,0:T(8,128)(2,1)S(1)}, u32[]{:S(2)}, u32[]{:S(2)}) collective-permute-start(bf16[4,176,128]{2,1,0:T(8,128)(2,1)S(1)} %shard_map.105.refs_0_), channel_id=1, source_target_pairs={{0,2},{2,0},{4,6},{6,4},{8,10},{10,8},{12,14},{14,12},{1,3},{3,1},... | collective-permute-start | bytes 540680 | tf_op jit(solution)/shard_map/ppermute | solution.py:771
  13.4 2.0 %collective-permute-start.5 = (bf16[1,176,128]{2,1,0:T(8,128)(2,1)S(1)}, bf16[1,176,128]{2,1,0:T(8,128)(2,1)S(1)}, u32[]{:S(2)}, u32[]{:S(2)}) collective-permute-start(bf16[1,176,128]{2,1,0:T(8,128)(2,1)S(1)} %get-tuple-element.100.refs_0_), channel_id=1, source_target_pairs={{0,8},{2,10},{4,12},{6,14},{8,0},{10,2},{12,4},{14,6},{1,9},{3,11}... | collective-permute-start | bytes 135176 | tf_op jit(solution)/shard_map/ppermute | solution.py:771
  15.4 1.7 %shard_map.106 = (bf16[512,2304]{1,0:T(8,128)(2,1)S(1)}, f32[1,512]{1,0:T(1,128)S(1)}, f32[1,2304]{1,0:T(1,128)S(1)}, f32[1,2304]{1,0:T(1,128)S(1)}) custom-call(bf16[512,2304]{1,0:T(8,128)(2,1)} %dict_hbm, f32[1,5120]{1,0:T(1,128)S(1)} %bitcast.3), custom_call_target="tpu_custom_call" | custom-call | bytes 4718592 | tf_op jit(solution)/shard_map/pallas_call | solution.py:246
  17.1 2.0 %collective-permute-done.5.refs_1_ = bf16[1,176,128]{2,1,0:T(8,128)(2,1)S(1)} collective-permute-done((bf16[1,176,128]{2,1,0:T(8,128)(2,1)S(1)}, bf16[1,176,128]{2,1,0:T(8,128)(2,1)S(1)}, u32[]{:S(2)}, u32[]{:S(2)}) %collective-permute-start.5) | collective-permute-done | bytes 45088 | tf_op jit(solution)/shard_map/ppermute | solution.py:771
  19.3 1.3 %collective-permute-done.6.refs_3_ = bf16[4,176,128]{2,1,0:T(8,128)(2,1)S(1)} collective-permute-done((bf16[4,176,128]{2,1,0:T(8,128)(2,1)S(1)}, bf16[4,176,128]{2,1,0:T(8,128)(2,1)S(1)}, u32[]{:S(2)}, u32[]{:S(2)}) %collective-permute-start.6) | collective-permute-done | bytes 180256 | tf_op jit(solution)/shard_map/ppermute | solution.py:766
  20.6 1.7 %shard_map.108 = (bf16[144,2304]{1,0:T(8,128)(2,1)S(1)}, bf16[144,512]{1,0:T(8,128)(2,1)S(1)}, f32[4,176,128]{2,1,0:T(8,128)S(1)}, f32[4,176,128]{2,1,0:T(8,128)S(1)}) custom-call(bf16[4,176,128]{2,1,0:T(8,128)(2,1)S(1)} %shard_map.105.refs_0_, bf16[4,176,128]{2,1,0:T(8,128)(2,1)S(1)} %collective-permute-done.4.refs_1_, ...), custom_call_target="tpu_custom_call" | custom-call | flops 509607936 | bytes 2359296 | tf_op jit(solution)/shard_map/pallas_call | solution.py:113
  24.7 5.1 %collective-permute-done.9.got_ref = bf16[3,176,128]{2,1,0:T(8,128)(2,1)S(1)} collective-permute-done((bf16[3,176,128]{2,1,0:T(8,128)(2,1)S(1)}, bf16[3,176,128]{2,1,0:T(8,128)(2,1)S(1)}, u32[]{:S(2)}, u32[]{:S(2)}) %collective-permute-start.9) | collective-permute-done | bytes 135200 | tf_op jit(solution)/shard_map/ppermute | solution.py:771
  32.4 2.8 %collective-permute-start.13 = (bf16[1,176,128]{2,1,0:T(8,128)(2,1)S(1)}, bf16[1,176,128]{2,1,0:T(8,128)(2,1)S(1)}, u32[]{:S(2)}, u32[]{:S(2)}) collective-permute-start(bf16[1,176,128]{2,1,0:T(8,128)(2,1)S(1)} %get-tuple-element.122), channel_id=1, source_target_pairs={{0,4},{2,6},{4,0},{6,2},{8,12},{10,14},{12,8},{14,10},{1,5},{3,7},... | collective-permute-start | bytes 135176 | tf_op jit(solution)/shard_map/ppermute | solution.py:771
  35.2 1.5 %collective-permute-done.11.refs_2_ = bf16[1,176,128]{2,1,0:T(8,128)(2,1)S(1)} collective-permute-done((bf16[1,176,128]{2,1,0:T(8,128)(2,1)S(1)}, bf16[1,176,128]{2,1,0:T(8,128)(2,1)S(1)}, u32[]{:S(2)}, u32[]{:S(2)}) %collective-permute-start.11) | collective-permute-done | bytes 45088 | tf_op jit(solution)/shard_map/ppermute | solution.py:771
  37.8 2.0 %collective-permute-start.17 = (bf16[1,176,128]{2,1,0:T(8,128)(2,1)S(1)}, bf16[1,176,128]{2,1,0:T(8,128)(2,1)S(1)}, u32[]{:S(2)}, u32[]{:S(2)}) collective-permute-start(bf16[1,176,128]{2,1,0:T(8,128)(2,1)S(1)} %get-tuple-element.127.refs_0_), channel_id=1, source_target_pairs={{0,12},{2,14},{4,8},{6,10},{8,4},{10,6},{12,0},{14,2},{1,13},{3,15... | collective-permute-start | bytes 135176 | tf_op jit(solution)/shard_map/ppermute | solution.py:771
  40.9 1.4 %collective-permute-start.15 = (bf16[1,176,128]{2,1,0:T(8,128)(2,1)S(1)}, bf16[1,176,128]{2,1,0:T(8,128)(2,1)S(1)}, u32[]{:S(2)}, u32[]{:S(2)}) collective-permute-start(bf16[1,176,128]{2,1,0:T(8,128)(2,1)S(1)} %get-tuple-element.127.refs_0_), channel_id=1, source_target_pairs={{0,4},{2,6},{4,0},{6,2},{8,12},{10,14},{12,8},{14,10},{1,5},{3,7},... | collective-permute-start | bytes 135176 | tf_op jit(solution)/shard_map/ppermute | solution.py:771
  47.8 3.0 %collective-permute-done.19.refs_1_ = bf16[4,176,128]{2,1,0:T(8,128)(2,1)S(1)} collective-permute-done((bf16[4,176,128]{2,1,0:T(8,128)(2,1)S(1)}, bf16[4,176,128]{2,1,0:T(8,128)(2,1)S(1)}, u32[]{:S(2)}, u32[]{:S(2)}) %collective-permute-start.19) | collective-permute-done | bytes 180256 | tf_op jit(solution)/shard_map/ppermute | solution.py:771
  52.2 1.6 %shard_map.119 = (bf16[144,2304]{1,0:T(8,128)(2,1)S(1)}, f32[144,1]{1,0:T(8,128)S(1)}, bf16[144,512]{1,0:T(8,128)(2,1)S(1)}, bf16[144,512]{1,0:T(8,128)(2,1)S(1)...) custom-call(bf16[8,176,128]{2,1,0:T(8,128)(2,1)S(1)} %shard_map.116.other_ref, ...), custom_call_target="tpu_custom_call" | custom-call | flops 1019215872 | bytes 4718592 | tf_op jit(solution)/shard_map/pallas_call | solution.py:113
  58.2 4.0 %collective-permute-done.25.got_ref = bf16[3,176,128]{2,1,0:T(8,128)(2,1)S(1)} collective-permute-done((bf16[3,176,128]{2,1,0:T(8,128)(2,1)S(1)}, bf16[3,176,128]{2,1,0:T(8,128)(2,1)S(1)}, u32[]{:S(2)}, u32[]{:S(2)}) %collective-permute-start.25) | collective-permute-done | bytes 135200 | tf_op jit(solution)/shard_map/ppermute | solution.py:771
  62.3 1.3 %collective-permute-start.30 = (bf16[5,176,128]{2,1,0:T(8,128)(2,1)S(1)}, bf16[5,176,128]{2,1,0:T(8,128)(2,1)S(1)}, u32[]{:S(2)}, u32[]{:S(2)}) collective-permute-start(bf16[5,176,128]{2,1,0:T(8,128)(2,1)S(1)} %get-tuple-element.160), channel_id=1, source_target_pairs={{0,2},{2,0},{4,6},{6,4},{8,10},{10,8},{12,14},{14,12},{1,3},{3,1},... | collective-permute-start | bytes 675848 | tf_op jit(solution)/shard_map/ppermute | solution.py:771
  63.6 1.9 %collective-permute-start.27 = (bf16[1,176,128]{2,1,0:T(8,128)(2,1)S(1)}, bf16[1,176,128]{2,1,0:T(8,128)(2,1)S(1)}, u32[]{:S(2)}, u32[]{:S(2)}) collective-permute-start(bf16[1,176,128]{2,1,0:T(8,128)(2,1)S(1)} %get-tuple-element.157), channel_id=1, source_target_pairs={{0,12},{2,14},{4,8},{6,10},{8,4},{10,6},{12,0},{14,2},{1,13},{3,15... | collective-permute-start | bytes 135176 | tf_op jit(solution)/shard_map/ppermute | solution.py:771
  66.1 1.9 %collective-permute-start.29 = (bf16[1,176,128]{2,1,0:T(8,128)(2,1)S(1)}, bf16[1,176,128]{2,1,0:T(8,128)(2,1)S(1)}, u32[]{:S(2)}, u32[]{:S(2)}) collective-permute-start(bf16[1,176,128]{2,1,0:T(8,128)(2,1)S(1)} %get-tuple-element.159), channel_id=1, source_target_pairs={{0,4},{2,6},{4,0},{6,2},{8,12},{10,14},{12,8},{14,10},{1,5},{3,7},... | collective-permute-start | bytes 135176 | tf_op jit(solution)/shard_map/ppermute | solution.py:771
  68.0 1.8 %collective-permute-done.27.refs_2_ = bf16[1,176,128]{2,1,0:T(8,128)(2,1)S(1)} collective-permute-done((bf16[1,176,128]{2,1,0:T(8,128)(2,1)S(1)}, bf16[1,176,128]{2,1,0:T(8,128)(2,1)S(1)}, u32[]{:S(2)}, u32[]{:S(2)}) %collective-permute-start.27) | collective-permute-done | bytes 45088 | tf_op jit(solution)/shard_map/ppermute | solution.py:771
  72.2 1.9 %collective-permute-start.33 = (bf16[1,176,128]{2,1,0:T(8,128)(2,1)S(1)}, bf16[1,176,128]{2,1,0:T(8,128)(2,1)S(1)}, u32[]{:S(2)}, u32[]{:S(2)}) collective-permute-start(bf16[1,176,128]{2,1,0:T(8,128)(2,1)S(1)} %get-tuple-element.165.refs_0_), channel_id=1, source_target_pairs={{0,12},{2,14},{4,8},{6,10},{8,4},{10,6},{12,0},{14,2},{1,13},{3,15... | collective-permute-start | bytes 135176 | tf_op jit(solution)/shard_map/ppermute | solution.py:771
  74.4 2.5 %collective-permute-done.31.got_ref.refs_1_ = bf16[1,528,128]{2,1,0:T(8,128)(2,1)S(1)} collective-permute-done((bf16[1,528,128]{2,1,0:T(8,128)(2,1)S(1)}, bf16[1,528,128]{2,1,0:T(8,128)(2,1)S(1)}, u32[]{:S(2)}, u32[]{:S(2)}) %collective-permute-start.31) | collective-permute-done | bytes 135200 | tf_op jit(solution)/shard_map/ppermute | solution.py:771
  80.4 4.9 %collective-permute-done.36.got_ref = bf16[1,176,128]{2,1,0:T(8,128)(2,1)S(1)} collective-permute-done((bf16[1,176,128]{2,1,0:T(8,128)(2,1)S(1)}, bf16[1,176,128]{2,1,0:T(8,128)(2,1)S(1)}, u32[]{:S(2)}, u32[]{:S(2)}) %collective-permute-start.36) | collective-permute-done | bytes 45088 | tf_op jit(solution)/shard_map/ppermute | solution.py:771
  86.8 3.7 %shard_map.133 = bf16[512,2304]{1,0:T(8,128)(2,1)} custom-call(bf16[8,176,128]{2,1,0:T(8,128)(2,1)S(1)} %shard_map.130.own_ref, bf16[8,176,128]{2,1,0:T(8,128)(2,1)S(1)} %shard_map.131.other_ref, bf16[144,2304]{1,0:T(8,128)(2,1)S(1)} %get-tuple-element.174.scaled_ref, f32[144,2304]{1,0:T(8,128)S(1)} %get-tuple-element.177.factor_ref, ...), custom_call_target="tpu_custom_call" | custom-call | flops 1019215872 | bytes 4718592 | tf_op jit(solution)/shard_map/pallas_call | solution.py:113
  (90 shorter events, 30.2 us)
Async XLA Ops:
  1.7 7.2 %collective-permute-start.2 = (bf16[1,176,128]{2,1,0:T(8,128)(2,1)S(1)}, bf16[1,176,128]{2,1,0:T(8,128)(2,1)S(1)}, u32[]{:S(2)}, u32[]{:S(2)}) collective-permute-start(bf16[1,176,128]{2,1,0:T(8,128)(2,1)S(1)} %get-tuple-element.91.refs_0_), channel_id=1, source_target_pairs={{0,12},{2,14},{4,8},{6,10},{8,4},{10,6},{12,0},{14,2},{1,13},{3,15... | collective-permute-start | bytes 135176 | tf_op jit(solution)/shard_map/ppermute | solution.py:771
  11.8 7.3 %collective-permute-start.4 = (bf16[4,176,128]{2,1,0:T(8,128)(2,1)S(1)}, bf16[4,176,128]{2,1,0:T(8,128)(2,1)S(1)}, u32[]{:S(2)}, u32[]{:S(2)}) collective-permute-start(bf16[4,176,128]{2,1,0:T(8,128)(2,1)S(1)} %shard_map.105.refs_0_), channel_id=1, source_target_pairs={{0,2},{2,0},{4,6},{6,4},{8,10},{10,8},{12,14},{14,12},{1,3},{3,1},... | collective-permute-start | bytes 540680 | tf_op jit(solution)/shard_map/ppermute | solution.py:771
  13.4 5.8 %collective-permute-start.3 = (bf16[4,176,128]{2,1,0:T(8,128)(2,1)S(1)}, bf16[4,176,128]{2,1,0:T(8,128)(2,1)S(1)}, u32[]{:S(2)}, u32[]{:S(2)}) collective-permute-start(bf16[4,176,128]{2,1,0:T(8,128)(2,1)S(1)} %shard_map.105.refs_0_), channel_id=1, source_target_pairs={{0,1},{1,0},{2,3},{3,2},{4,5},{5,4},{6,7},{7,6},{8,9},{9,8},{10,11... | collective-permute-start | bytes 540680 | tf_op jit(solution)/shard_map/ppermute | solution.py:766
  13.4 5.7 %collective-permute-start.5 = (bf16[1,176,128]{2,1,0:T(8,128)(2,1)S(1)}, bf16[1,176,128]{2,1,0:T(8,128)(2,1)S(1)}, u32[]{:S(2)}, u32[]{:S(2)}) collective-permute-start(bf16[1,176,128]{2,1,0:T(8,128)(2,1)S(1)} %get-tuple-element.100.refs_0_), channel_id=1, source_target_pairs={{0,8},{2,10},{4,12},{6,14},{8,0},{10,2},{12,4},{14,6},{1,9},{3,11}... | collective-permute-start | bytes 135176 | tf_op jit(solution)/shard_map/ppermute | solution.py:771
  24.1 5.7 %collective-permute-start.9 = (bf16[3,176,128]{2,1,0:T(8,128)(2,1)S(1)}, bf16[3,176,128]{2,1,0:T(8,128)(2,1)S(1)}, u32[]{:S(2)}, u32[]{:S(2)}) collective-permute-start(bf16[3,176,128]{2,1,0:T(8,128)(2,1)S(1)} %get-tuple-element.114), channel_id=1, source_target_pairs={{0,2},{2,0},{4,6},{6,4},{8,10},{10,8},{12,14},{14,12},{1,3},{3,1},... | collective-permute-start | bytes 405512 | tf_op jit(solution)/shard_map/ppermute | solution.py:771
  24.7 5.1 %collective-permute-start.10 = (bf16[2,176,128]{2,1,0:T(8,128)(2,1)S(1)}, bf16[2,176,128]{2,1,0:T(8,128)(2,1)S(1)}, u32[]{:S(2)}, u32[]{:S(2)}) collective-permute-start(bf16[2,176,128]{2,1,0:T(8,128)(2,1)S(1)} %shard_map.107.here_ref), channel_id=1, source_target_pairs={{0,4},{2,6},{4,0},{6,2},{8,12},{10,14},{12,8},{14,10},{1,5},{3,7},... | collective-permute-start | bytes 270344 | tf_op jit(solution)/shard_map/ppermute | solution.py:771
  29.9 7.8 %collective-permute-start.14 = (bf16[5,176,128]{2,1,0:T(8,128)(2,1)S(1)}, bf16[5,176,128]{2,1,0:T(8,128)(2,1)S(1)}, u32[]{:S(2)}, u32[]{:S(2)}) collective-permute-start(bf16[5,176,128]{2,1,0:T(8,128)(2,1)S(1)} %get-tuple-element.126), channel_id=1, source_target_pairs={{0,2},{2,0},{4,6},{6,4},{8,10},{10,8},{12,14},{14,12},{1,3},{3,1},... | collective-permute-start | bytes 675848 | tf_op jit(solution)/shard_map/ppermute | solution.py:771
  30.8 5.9 %collective-permute-start.11 = (bf16[1,176,128]{2,1,0:T(8,128)(2,1)S(1)}, bf16[1,176,128]{2,1,0:T(8,128)(2,1)S(1)}, u32[]{:S(2)}, u32[]{:S(2)}) collective-permute-start(bf16[1,176,128]{2,1,0:T(8,128)(2,1)S(1)} %get-tuple-element.120), channel_id=1, source_target_pairs={{0,12},{2,14},{4,8},{6,10},{8,4},{10,6},{12,0},{14,2},{1,13},{3,15... | collective-permute-start | bytes 135176 | tf_op jit(solution)/shard_map/ppermute | solution.py:771
  31.9 5.8 %collective-permute-start.12 = (bf16[1,176,128]{2,1,0:T(8,128)(2,1)S(1)}, bf16[1,176,128]{2,1,0:T(8,128)(2,1)S(1)}, u32[]{:S(2)}, u32[]{:S(2)}) collective-permute-start(bf16[1,176,128]{2,1,0:T(8,128)(2,1)S(1)} %get-tuple-element.121), channel_id=1, source_target_pairs={{0,8},{2,10},{4,12},{6,14},{8,0},{10,2},{12,4},{14,6},{1,9},{3,11}... | collective-permute-start | bytes 135176 | tf_op jit(solution)/shard_map/ppermute | solution.py:771
  32.4 5.3 %collective-permute-start.13 = (bf16[1,176,128]{2,1,0:T(8,128)(2,1)S(1)}, bf16[1,176,128]{2,1,0:T(8,128)(2,1)S(1)}, u32[]{:S(2)}, u32[]{:S(2)}) collective-permute-start(bf16[1,176,128]{2,1,0:T(8,128)(2,1)S(1)} %get-tuple-element.122), channel_id=1, source_target_pairs={{0,4},{2,6},{4,0},{6,2},{8,12},{10,14},{12,8},{14,10},{1,5},{3,7},... | collective-permute-start | bytes 135176 | tf_op jit(solution)/shard_map/ppermute | solution.py:771
  37.8 5.9 %collective-permute-start.17 = (bf16[1,176,128]{2,1,0:T(8,128)(2,1)S(1)}, bf16[1,176,128]{2,1,0:T(8,128)(2,1)S(1)}, u32[]{:S(2)}, u32[]{:S(2)}) collective-permute-start(bf16[1,176,128]{2,1,0:T(8,128)(2,1)S(1)} %get-tuple-element.127.refs_0_), channel_id=1, source_target_pairs={{0,12},{2,14},{4,8},{6,10},{8,4},{10,6},{12,0},{14,2},{1,13},{3,15... | collective-permute-start | bytes 135176 | tf_op jit(solution)/shard_map/ppermute | solution.py:771
  39.8 5.0 %collective-permute-start.16 = (bf16[1,176,128]{2,1,0:T(8,128)(2,1)S(1)}, bf16[1,176,128]{2,1,0:T(8,128)(2,1)S(1)}, u32[]{:S(2)}, u32[]{:S(2)}) collective-permute-start(bf16[1,176,128]{2,1,0:T(8,128)(2,1)S(1)} %get-tuple-element.127.refs_0_), channel_id=1, source_target_pairs={{0,8},{2,10},{4,12},{6,14},{8,0},{10,2},{12,4},{14,6},{1,9},{3,11}... | collective-permute-start | bytes 135176 | tf_op jit(solution)/shard_map/ppermute | solution.py:771
  45.2 5.6 %collective-permute-start.19 = (bf16[4,176,128]{2,1,0:T(8,128)(2,1)S(1)}, bf16[4,176,128]{2,1,0:T(8,128)(2,1)S(1)}, u32[]{:S(2)}, u32[]{:S(2)}) collective-permute-start(bf16[4,176,128]{2,1,0:T(8,128)(2,1)S(1)} %shard_map.114.refs_0_), channel_id=1, source_target_pairs={{0,2},{2,0},{4,6},{6,4},{8,10},{10,8},{12,14},{14,12},{1,3},{3,1},... | collective-permute-start | bytes 540680 | tf_op jit(solution)/shard_map/ppermute | solution.py:771
  56.1 6.1 %collective-permute-start.26 = (bf16[8,176,128]{2,1,0:T(8,128)(2,1)S(1)}, bf16[8,176,128]{2,1,0:T(8,128)(2,1)S(1)}, u32[]{:S(2)}, u32[]{:S(2)}) collective-permute-start(bf16[8,176,128]{2,1,0:T(8,128)(2,1)S(1)} %get-tuple-element.154), channel_id=1, source_target_pairs={{0,1},{1,0},{2,3},{3,2},{4,5},{5,4},{6,7},{7,6},{8,9},{9,8},{10,11... | collective-permute-start | bytes 1081352 | tf_op jit(solution)/shard_map/ppermute | solution.py:766
  56.3 5.8 %collective-permute-start.25 = (bf16[3,176,128]{2,1,0:T(8,128)(2,1)S(1)}, bf16[3,176,128]{2,1,0:T(8,128)(2,1)S(1)}, u32[]{:S(2)}, u32[]{:S(2)}) collective-permute-start(bf16[3,176,128]{2,1,0:T(8,128)(2,1)S(1)} %get-tuple-element.148), channel_id=1, source_target_pairs={{0,2},{2,0},{4,6},{6,4},{8,10},{10,8},{12,14},{14,12},{1,3},{3,1},... | collective-permute-start | bytes 405512 | tf_op jit(solution)/shard_map/ppermute | solution.py:771
  62.3 8.5 %collective-permute-start.30 = (bf16[5,176,128]{2,1,0:T(8,128)(2,1)S(1)}, bf16[5,176,128]{2,1,0:T(8,128)(2,1)S(1)}, u32[]{:S(2)}, u32[]{:S(2)}) collective-permute-start(bf16[5,176,128]{2,1,0:T(8,128)(2,1)S(1)} %get-tuple-element.160), channel_id=1, source_target_pairs={{0,2},{2,0},{4,6},{6,4},{8,10},{10,8},{12,14},{14,12},{1,3},{3,1},... | collective-permute-start | bytes 675848 | tf_op jit(solution)/shard_map/ppermute | solution.py:771
  63.6 6.2 %collective-permute-start.27 = (bf16[1,176,128]{2,1,0:T(8,128)(2,1)S(1)}, bf16[1,176,128]{2,1,0:T(8,128)(2,1)S(1)}, u32[]{:S(2)}, u32[]{:S(2)}) collective-permute-start(bf16[1,176,128]{2,1,0:T(8,128)(2,1)S(1)} %get-tuple-element.157), channel_id=1, source_target_pairs={{0,12},{2,14},{4,8},{6,10},{8,4},{10,6},{12,0},{14,2},{1,13},{3,15... | collective-permute-start | bytes 135176 | tf_op jit(solution)/shard_map/ppermute | solution.py:771
  65.4 5.4 %collective-permute-start.28 = (bf16[1,176,128]{2,1,0:T(8,128)(2,1)S(1)}, bf16[1,176,128]{2,1,0:T(8,128)(2,1)S(1)}, u32[]{:S(2)}, u32[]{:S(2)}) collective-permute-start(bf16[1,176,128]{2,1,0:T(8,128)(2,1)S(1)} %get-tuple-element.158), channel_id=1, source_target_pairs={{0,8},{2,10},{4,12},{6,14},{8,0},{10,2},{12,4},{14,6},{1,9},{3,11}... | collective-permute-start | bytes 135176 | tf_op jit(solution)/shard_map/ppermute | solution.py:771
  70.9 6.0 %collective-permute-start.31 = (bf16[1,528,128]{2,1,0:T(8,128)(2,1)S(1)}, bf16[1,528,128]{2,1,0:T(8,128)(2,1)S(1)}, u32[]{:S(2)}, u32[]{:S(2)}) collective-permute-start(bf16[1,528,128]{2,1,0:T(8,128)(2,1)S(1)} %get-tuple-element.163), channel_id=1, source_target_pairs={{0,4},{2,6},{4,0},{6,2},{8,12},{10,14},{12,8},{14,10},{1,5},{3,7},... | collective-permute-start | bytes 405512 | tf_op jit(solution)/shard_map/ppermute | solution.py:771
  72.2 5.8 %collective-permute-start.33 = (bf16[1,176,128]{2,1,0:T(8,128)(2,1)S(1)}, bf16[1,176,128]{2,1,0:T(8,128)(2,1)S(1)}, u32[]{:S(2)}, u32[]{:S(2)}) collective-permute-start(bf16[1,176,128]{2,1,0:T(8,128)(2,1)S(1)} %get-tuple-element.165.refs_0_), channel_id=1, source_target_pairs={{0,12},{2,14},{4,8},{6,10},{8,4},{10,6},{12,0},{14,2},{1,13},{3,15... | collective-permute-start | bytes 135176 | tf_op jit(solution)/shard_map/ppermute | solution.py:771
  74.0 5.0 %collective-permute-start.32 = (bf16[1,176,128]{2,1,0:T(8,128)(2,1)S(1)}, bf16[1,176,128]{2,1,0:T(8,128)(2,1)S(1)}, u32[]{:S(2)}, u32[]{:S(2)}) collective-permute-start(bf16[1,176,128]{2,1,0:T(8,128)(2,1)S(1)} %get-tuple-element.165.refs_0_), channel_id=1, source_target_pairs={{0,8},{2,10},{4,12},{6,14},{8,0},{10,2},{12,4},{14,6},{1,9},{3,11}... | collective-permute-start | bytes 135176 | tf_op jit(solution)/shard_map/ppermute | solution.py:771
  79.0 6.3 %collective-permute-start.35 = (bf16[4,176,128]{2,1,0:T(8,128)(2,1)S(1)}, bf16[4,176,128]{2,1,0:T(8,128)(2,1)S(1)}, u32[]{:S(2)}, u32[]{:S(2)}) collective-permute-start(bf16[4,176,128]{2,1,0:T(8,128)(2,1)S(1)} %shard_map.128.refs_0_), channel_id=1, source_target_pairs={{0,2},{2,0},{4,6},{6,4},{8,10},{10,8},{12,14},{14,12},{1,3},{3,1},... | collective-permute-start | bytes 540680 | tf_op jit(solution)/shard_map/ppermute | solution.py:771
  79.9 5.4 %collective-permute-start.34 = (bf16[4,176,128]{2,1,0:T(8,128)(2,1)S(1)}, bf16[4,176,128]{2,1,0:T(8,128)(2,1)S(1)}, u32[]{:S(2)}, u32[]{:S(2)}) collective-permute-start(bf16[4,176,128]{2,1,0:T(8,128)(2,1)S(1)} %shard_map.128.refs_0_), channel_id=1, source_target_pairs={{0,1},{1,0},{2,3},{3,2},{4,5},{5,4},{6,7},{7,6},{8,9},{9,8},{10,11... | collective-permute-start | bytes 540680 | tf_op jit(solution)/shard_map/ppermute | solution.py:766
  79.9 5.4 %collective-permute-start.36 = (bf16[1,176,128]{2,1,0:T(8,128)(2,1)S(1)}, bf16[1,176,128]{2,1,0:T(8,128)(2,1)S(1)}, u32[]{:S(2)}, u32[]{:S(2)}) collective-permute-start(bf16[1,176,128]{2,1,0:T(8,128)(2,1)S(1)} %get-tuple-element.170), channel_id=1, source_target_pairs={{0,8},{2,10},{4,12},{6,14},{8,0},{10,2},{12,4},{14,6},{1,9},{3,11}... | collective-permute-start | bytes 135176 | tf_op jit(solution)/shard_map/ppermute | solution.py:771
  (17 other events, 96.0 us)

commit v3 on v2

--- a/solution.py
+++ b/solution.py
@@ -869,6 +869,8 @@
     first = cross(sent_first)
     block, message, out_kept = add_with_output(plan, own_kept, kept, got, first, out_kept)
     got = to_column(plan, [message] + [block] * (len(plan.columns) - 2))
+    got = list(tie(got[-1], *got[:-1]))
+    got = got[1:] + got[:1]
     stack = stack_up(plan, block, got)
     out_kept, out_sent = halve(plan, out_kept, got[0], plan.chunk)
     stack, scaled_late, inputs_late, out_sent = tie(stack, scaled, inputs, out_sent)

time: 90.8 us -> 90.9 us (level)
  transfers between devices with their start and end apart: 38 -> 38, of which waited for: 21 -> 20; matrix products, arithmetic and copies ran while one was open for 1% -> 1% of each run, Pallas kernels for 9% -> 9%
where the time goes in v3:
time: 90.9 us; the launch traced here: 90.7 us
  waiting for transfers between devices  37 us (41%)
  starting transfers between devices  35.6 us (39%)
  Pallas kernels  15.3 us (17%)
  other arithmetic  1.74 us (2%)
  between operations  1.05 us (1%)
    ppermute x25, waiting for transfers between devices, partner_swap(): return lax.ppermute(value, 'latent', [(i, i ^ bits) for i in range(size)])  34.2 us
    ppermute x25, starting transfers between devices, partner_swap(): return lax.ppermute(value, 'latent', [(i, i ^ bits) for i in range(size)])  33.5 us
    pallas_call x29, Pallas kernels, call(): pl.pallas_call(body, out_shape=out_shapes, in_specs=[ONCHIP] * len(operan...  13.6 us
    ppermute x13, waiting for transfers between devices, swap(): lax.ppermute(value, 'hidden', [(i, (i + 1) % size) for i in range(size)])  2.82 us
    ppermute x13, starting transfers between devices, swap(): lax.ppermute(value, 'hidden', [(i, (i + 1) % size) for i in range(size)])  2.06 us
  transfers between devices with their start and end apart: 38, of which 20 were waited for; matrix products, arithmetic and copies ran while one was open for 1% of the time, Pallas kernels for 9%

profile of v3, /device:TPU:0, one launch (start us, length us, event | category | flops | bytes accessed | tf_op | source)
XLA Modules:
  0.0 90.7 jit_solution(11519320064799297233)
XLA Ops:
  1.7 5.1 %collective-permute-start.2 = (bf16[1,176,128]{2,1,0:T(8,128)(2,1)S(1)}, bf16[1,176,128]{2,1,0:T(8,128)(2,1)S(1)}, u32[]{:S(2)}, u32[]{:S(2)}) collective-permute-start(bf16[1,176,128]{2,1,0:T(8,128)(2,1)S(1)} %get-tuple-element.94.refs_0_), channel_id=1, source_target_pairs={{0,12},{2,14},{4,8},{6,10},{8,4},{10,6},{12,0},{14,2},{1,13},{3,15... | collective-permute-start | bytes 135176 | tf_op jit(solution)/shard_map/ppermute | solution.py:771
  8.9 2.9 %collective-permute-done.1.refs_2_ = bf16[1,176,128]{2,1,0:T(8,128)(2,1)S(1)} collective-permute-done((bf16[1,176,128]{2,1,0:T(8,128)(2,1)S(1)}, bf16[1,176,128]{2,1,0:T(8,128)(2,1)S(1)}, u32[]{:S(2)}, u32[]{:S(2)}) %collective-permute-start.1) | collective-permute-done | bytes 45088 | tf_op jit(solution)/shard_map/ppermute | solution.py:771
  11.8 1.6 %collective-permute-start.4 = (bf16[4,176,128]{2,1,0:T(8,128)(2,1)S(1)}, bf16[4,176,128]{2,1,0:T(8,128)(2,1)S(1)}, u32[]{:S(2)}, u32[]{:S(2)}) collective-permute-start(bf16[4,176,128]{2,1,0:T(8,128)(2,1)S(1)} %shard_map.105.refs_0_), channel_id=1, source_target_pairs={{0,2},{2,0},{4,6},{6,4},{8,10},{10,8},{12,14},{14,12},{1,3},{3,1},... | collective-permute-start | bytes 540680 | tf_op jit(solution)/shard_map/ppermute | solution.py:771
  13.4 2.0 %collective-permute-start.5 = (bf16[1,176,128]{2,1,0:T(8,128)(2,1)S(1)}, bf16[1,176,128]{2,1,0:T(8,128)(2,1)S(1)}, u32[]{:S(2)}, u32[]{:S(2)}) collective-permute-start(bf16[1,176,128]{2,1,0:T(8,128)(2,1)S(1)} %get-tuple-element.103.refs_0_), channel_id=1, source_target_pairs={{0,8},{2,10},{4,12},{6,14},{8,0},{10,2},{12,4},{14,6},{1,9},{3,11}... | collective-permute-start | bytes 135176 | tf_op jit(solution)/shard_map/ppermute | solution.py:771
  15.4 1.7 %shard_map.106 = (bf16[512,2304]{1,0:T(8,128)(2,1)S(1)}, f32[1,512]{1,0:T(1,128)S(1)}, f32[1,2304]{1,0:T(1,128)S(1)}, f32[1,2304]{1,0:T(1,128)S(1)}) custom-call(bf16[512,2304]{1,0:T(8,128)(2,1)} %dict_hbm, f32[1,5120]{1,0:T(1,128)S(1)} %bitcast.3), custom_call_target="tpu_custom_call" | custom-call | bytes 4718592 | tf_op jit(solution)/shard_map/pallas_call | solution.py:246
  17.1 2.0 %collective-permute-done.5.refs_1_ = bf16[1,176,128]{2,1,0:T(8,128)(2,1)S(1)} collective-permute-done((bf16[1,176,128]{2,1,0:T(8,128)(2,1)S(1)}, bf16[1,176,128]{2,1,0:T(8,128)(2,1)S(1)}, u32[]{:S(2)}, u32[]{:S(2)}) %collective-permute-start.5) | collective-permute-done | bytes 45088 | tf_op jit(solution)/shard_map/ppermute | solution.py:771
  19.3 1.3 %collective-permute-done.6.refs_3_ = bf16[4,176,128]{2,1,0:T(8,128)(2,1)S(1)} collective-permute-done((bf16[4,176,128]{2,1,0:T(8,128)(2,1)S(1)}, bf16[4,176,128]{2,1,0:T(8,128)(2,1)S(1)}, u32[]{:S(2)}, u32[]{:S(2)}) %collective-permute-start.6) | collective-permute-done | bytes 180256 | tf_op jit(solution)/shard_map/ppermute | solution.py:766
  20.6 1.7 %shard_map.108 = (bf16[144,2304]{1,0:T(8,128)(2,1)S(1)}, bf16[144,512]{1,0:T(8,128)(2,1)S(1)}, f32[4,176,128]{2,1,0:T(8,128)S(1)}, f32[4,176,128]{2,1,0:T(8,128)S(1)}) custom-call(bf16[4,176,128]{2,1,0:T(8,128)(2,1)S(1)} %shard_map.105.refs_0_, bf16[4,176,128]{2,1,0:T(8,128)(2,1)S(1)} %collective-permute-done.4.refs_1_, ...), custom_call_target="tpu_custom_call" | custom-call | flops 509607936 | bytes 2359296 | tf_op jit(solution)/shard_map/pallas_call | solution.py:113
  24.7 5.1 %collective-permute-done.9.got_ref = bf16[3,176,128]{2,1,0:T(8,128)(2,1)S(1)} collective-permute-done((bf16[3,176,128]{2,1,0:T(8,128)(2,1)S(1)}, bf16[3,176,128]{2,1,0:T(8,128)(2,1)S(1)}, u32[]{:S(2)}, u32[]{:S(2)}) %collective-permute-start.9) | collective-permute-done | bytes 135200 | tf_op jit(solution)/shard_map/ppermute | solution.py:771
  32.4 2.8 %collective-permute-start.13 = (bf16[1,176,128]{2,1,0:T(8,128)(2,1)S(1)}, bf16[1,176,128]{2,1,0:T(8,128)(2,1)S(1)}, u32[]{:S(2)}, u32[]{:S(2)}) collective-permute-start(bf16[1,176,128]{2,1,0:T(8,128)(2,1)S(1)} %get-tuple-element.125), channel_id=1, source_target_pairs={{0,4},{2,6},{4,0},{6,2},{8,12},{10,14},{12,8},{14,10},{1,5},{3,7},... | collective-permute-start | bytes 135176 | tf_op jit(solution)/shard_map/ppermute | solution.py:771
  35.2 1.5 %collective-permute-done.11.refs_2_ = bf16[1,176,128]{2,1,0:T(8,128)(2,1)S(1)} collective-permute-done((bf16[1,176,128]{2,1,0:T(8,128)(2,1)S(1)}, bf16[1,176,128]{2,1,0:T(8,128)(2,1)S(1)}, u32[]{:S(2)}, u32[]{:S(2)}) %collective-permute-start.11) | collective-permute-done | bytes 45088 | tf_op jit(solution)/shard_map/ppermute | solution.py:771
  37.8 2.0 %collective-permute-start.17 = (bf16[1,176,128]{2,1,0:T(8,128)(2,1)S(1)}, bf16[1,176,128]{2,1,0:T(8,128)(2,1)S(1)}, u32[]{:S(2)}, u32[]{:S(2)}) collective-permute-start(bf16[1,176,128]{2,1,0:T(8,128)(2,1)S(1)} %get-tuple-element.130.refs_0_), channel_id=1, source_target_pairs={{0,12},{2,14},{4,8},{6,10},{8,4},{10,6},{12,0},{14,2},{1,13},{3,15... | collective-permute-start | bytes 135176 | tf_op jit(solution)/shard_map/ppermute | solution.py:771
  40.9 1.4 %collective-permute-start.15 = (bf16[1,176,128]{2,1,0:T(8,128)(2,1)S(1)}, bf16[1,176,128]{2,1,0:T(8,128)(2,1)S(1)}, u32[]{:S(2)}, u32[]{:S(2)}) collective-permute-start(bf16[1,176,128]{2,1,0:T(8,128)(2,1)S(1)} %get-tuple-element.130.refs_0_), channel_id=1, source_target_pairs={{0,4},{2,6},{4,0},{6,2},{8,12},{10,14},{12,8},{14,10},{1,5},{3,7},... | collective-permute-start | bytes 135176 | tf_op jit(solution)/shard_map/ppermute | solution.py:771
  47.8 3.0 %collective-permute-done.19.refs_1_ = bf16[4,176,128]{2,1,0:T(8,128)(2,1)S(1)} collective-permute-done((bf16[4,176,128]{2,1,0:T(8,128)(2,1)S(1)}, bf16[4,176,128]{2,1,0:T(8,128)(2,1)S(1)}, u32[]{:S(2)}, u32[]{:S(2)}) %collective-permute-start.19) | collective-permute-done | bytes 180256 | tf_op jit(solution)/shard_map/ppermute | solution.py:771
  52.2 1.6 %shard_map.119 = (bf16[144,2304]{1,0:T(8,128)(2,1)S(1)}, f32[144,1]{1,0:T(8,128)S(1)}, bf16[144,512]{1,0:T(8,128)(2,1)S(1)}, bf16[144,512]{1,0:T(8,128)(2,1)S(1)...) custom-call(bf16[8,176,128]{2,1,0:T(8,128)(2,1)S(1)} %shard_map.116.other_ref, ...), custom_call_target="tpu_custom_call" | custom-call | flops 1019215872 | bytes 4718592 | tf_op jit(solution)/shard_map/pallas_call | solution.py:113
  58.2 4.0 %collective-permute-done.25.got_ref = bf16[3,176,128]{2,1,0:T(8,128)(2,1)S(1)} collective-permute-done((bf16[3,176,128]{2,1,0:T(8,128)(2,1)S(1)}, bf16[3,176,128]{2,1,0:T(8,128)(2,1)S(1)}, u32[]{:S(2)}, u32[]{:S(2)}) %collective-permute-start.25) | collective-permute-done | bytes 135200 | tf_op jit(solution)/shard_map/ppermute | solution.py:771
  63.6 1.9 %collective-permute-start.27 = (bf16[1,176,128]{2,1,0:T(8,128)(2,1)S(1)}, bf16[1,176,128]{2,1,0:T(8,128)(2,1)S(1)}, u32[]{:S(2)}, u32[]{:S(2)}) collective-permute-start(bf16[1,176,128]{2,1,0:T(8,128)(2,1)S(1)} %get-tuple-element.160), channel_id=1, source_target_pairs={{0,12},{2,14},{4,8},{6,10},{8,4},{10,6},{12,0},{14,2},{1,13},{3,15... | collective-permute-start | bytes 135176 | tf_op jit(solution)/shard_map/ppermute | solution.py:771
  66.1 1.9 %collective-permute-start.29 = (bf16[1,176,128]{2,1,0:T(8,128)(2,1)S(1)}, bf16[1,176,128]{2,1,0:T(8,128)(2,1)S(1)}, u32[]{:S(2)}, u32[]{:S(2)}) collective-permute-start(bf16[1,176,128]{2,1,0:T(8,128)(2,1)S(1)} %get-tuple-element.162), channel_id=1, source_target_pairs={{0,4},{2,6},{4,0},{6,2},{8,12},{10,14},{12,8},{14,10},{1,5},{3,7},... | collective-permute-start | bytes 135176 | tf_op jit(solution)/shard_map/ppermute | solution.py:771
  68.0 1.8 %collective-permute-done.27.refs_2_ = bf16[1,176,128]{2,1,0:T(8,128)(2,1)S(1)} collective-permute-done((bf16[1,176,128]{2,1,0:T(8,128)(2,1)S(1)}, bf16[1,176,128]{2,1,0:T(8,128)(2,1)S(1)}, u32[]{:S(2)}, u32[]{:S(2)}) %collective-permute-start.27) | collective-permute-done | bytes 45088 | tf_op jit(solution)/shard_map/ppermute | solution.py:771
  73.4 2.0 %collective-permute-start.31 = (bf16[1,176,128]{2,1,0:T(8,128)(2,1)S(1)}, bf16[1,176,128]{2,1,0:T(8,128)(2,1)S(1)}, u32[]{:S(2)}, u32[]{:S(2)}) collective-permute-start(bf16[1,176,128]{2,1,0:T(8,128)(2,1)S(1)} %get-tuple-element.166.refs_0_), channel_id=1, source_target_pairs={{0,12},{2,14},{4,8},{6,10},{8,4},{10,6},{12,0},{14,2},{1,13},{3,15... | collective-permute-start | bytes 135176 | tf_op jit(solution)/shard_map/ppermute | solution.py:771
  75.3 1.9 %collective-permute-done.33.refs_2_ = bf16[1,176,128]{2,1,0:T(8,128)(2,1)S(1)} collective-permute-done((bf16[1,176,128]{2,1,0:T(8,128)(2,1)S(1)}, bf16[1,176,128]{2,1,0:T(8,128)(2,1)S(1)}, u32[]{:S(2)}, u32[]{:S(2)}) %collective-permute-start.33) | collective-permute-done | bytes 45088 | tf_op jit(solution)/shard_map/ppermute | solution.py:771
  77.3 1.9 %collective-permute-done.31.refs_3_ = bf16[1,176,128]{2,1,0:T(8,128)(2,1)S(1)} collective-permute-done((bf16[1,176,128]{2,1,0:T(8,128)(2,1)S(1)}, bf16[1,176,128]{2,1,0:T(8,128)(2,1)S(1)}, u32[]{:S(2)}, u32[]{:S(2)}) %collective-permute-start.31) | collective-permute-done | bytes 45088 | tf_op jit(solution)/shard_map/ppermute | solution.py:771
  80.4 4.9 %collective-permute-done.36.got_ref = bf16[1,176,128]{2,1,0:T(8,128)(2,1)S(1)} collective-permute-done((bf16[1,176,128]{2,1,0:T(8,128)(2,1)S(1)}, bf16[1,176,128]{2,1,0:T(8,128)(2,1)S(1)}, u32[]{:S(2)}, u32[]{:S(2)}) %collective-permute-start.36) | collective-permute-done | bytes 45088 | tf_op jit(solution)/shard_map/ppermute | solution.py:771
  86.8 3.7 %shard_map.133 = bf16[512,2304]{1,0:T(8,128)(2,1)} custom-call(bf16[8,176,128]{2,1,0:T(8,128)(2,1)S(1)} %shard_map.130.own_ref, bf16[8,176,128]{2,1,0:T(8,128)(2,1)S(1)} %shard_map.131.other_ref, bf16[144,2304]{1,0:T(8,128)(2,1)S(1)} %get-tuple-element.180.scaled_ref, f32[144,2304]{1,0:T(8,128)S(1)} %get-tuple-element.183.factor_ref, ...), custom_call_target="tpu_custom_call" | custom-call | flops 1019215872 | bytes 4718592 | tf_op jit(solution)/shard_map/pallas_call | solution.py:113
  (90 shorter events, 30.1 us)
Async XLA Ops:
  1.7 7.2 %collective-permute-start.2 = (bf16[1,176,128]{2,1,0:T(8,128)(2,1)S(1)}, bf16[1,176,128]{2,1,0:T(8,128)(2,1)S(1)}, u32[]{:S(2)}, u32[]{:S(2)}) collective-permute-start(bf16[1,176,128]{2,1,0:T(8,128)(2,1)S(1)} %get-tuple-element.94.refs_0_), channel_id=1, source_target_pairs={{0,12},{2,14},{4,8},{6,10},{8,4},{10,6},{12,0},{14,2},{1,13},{3,15... | collective-permute-start | bytes 135176 | tf_op jit(solution)/shard_map/ppermute | solution.py:771
  11.8 7.3 %collective-permute-start.4 = (bf16[4,176,128]{2,1,0:T(8,128)(2,1)S(1)}, bf16[4,176,128]{2,1,0:T(8,128)(2,1)S(1)}, u32[]{:S(2)}, u32[]{:S(2)}) collective-permute-start(bf16[4,176,128]{2,1,0:T(8,128)(2,1)S(1)} %shard_map.105.refs_0_), channel_id=1, source_target_pairs={{0,2},{2,0},{4,6},{6,4},{8,10},{10,8},{12,14},{14,12},{1,3},{3,1},... | collective-permute-start | bytes 540680 | tf_op jit(solution)/shard_map/ppermute | solution.py:771
  13.4 5.8 %collective-permute-start.3 = (bf16[4,176,128]{2,1,0:T(8,128)(2,1)S(1)}, bf16[4,176,128]{2,1,0:T(8,128)(2,1)S(1)}, u32[]{:S(2)}, u32[]{:S(2)}) collective-permute-start(bf16[4,176,128]{2,1,0:T(8,128)(2,1)S(1)} %shard_map.105.refs_0_), channel_id=1, source_target_pairs={{0,1},{1,0},{2,3},{3,2},{4,5},{5,4},{6,7},{7,6},{8,9},{9,8},{10,11... | collective-permute-start | bytes 540680 | tf_op jit(solution)/shard_map/ppermute | solution.py:766
  13.4 5.7 %collective-permute-start.5 = (bf16[1,176,128]{2,1,0:T(8,128)(2,1)S(1)}, bf16[1,176,128]{2,1,0:T(8,128)(2,1)S(1)}, u32[]{:S(2)}, u32[]{:S(2)}) collective-permute-start(bf16[1,176,128]{2,1,0:T(8,128)(2,1)S(1)} %get-tuple-element.103.refs_0_), channel_id=1, source_target_pairs={{0,8},{2,10},{4,12},{6,14},{8,0},{10,2},{12,4},{14,6},{1,9},{3,11}... | collective-permute-start | bytes 135176 | tf_op jit(solution)/shard_map/ppermute | solution.py:771
  24.1 5.7 %collective-permute-start.9 = (bf16[3,176,128]{2,1,0:T(8,128)(2,1)S(1)}, bf16[3,176,128]{2,1,0:T(8,128)(2,1)S(1)}, u32[]{:S(2)}, u32[]{:S(2)}) collective-permute-start(bf16[3,176,128]{2,1,0:T(8,128)(2,1)S(1)} %get-tuple-element.117), channel_id=1, source_target_pairs={{0,2},{2,0},{4,6},{6,4},{8,10},{10,8},{12,14},{14,12},{1,3},{3,1},... | collective-permute-start | bytes 405512 | tf_op jit(solution)/shard_map/ppermute | solution.py:771
  24.7 5.1 %collective-permute-start.10 = (bf16[2,176,128]{2,1,0:T(8,128)(2,1)S(1)}, bf16[2,176,128]{2,1,0:T(8,128)(2,1)S(1)}, u32[]{:S(2)}, u32[]{:S(2)}) collective-permute-start(bf16[2,176,128]{2,1,0:T(8,128)(2,1)S(1)} %shard_map.107.here_ref), channel_id=1, source_target_pairs={{0,4},{2,6},{4,0},{6,2},{8,12},{10,14},{12,8},{14,10},{1,5},{3,7},... | collective-permute-start | bytes 270344 | tf_op jit(solution)/shard_map/ppermute | solution.py:771
  29.9 7.8 %collective-permute-start.14 = (bf16[5,176,128]{2,1,0:T(8,128)(2,1)S(1)}, bf16[5,176,128]{2,1,0:T(8,128)(2,1)S(1)}, u32[]{:S(2)}, u32[]{:S(2)}) collective-permute-start(bf16[5,176,128]{2,1,0:T(8,128)(2,1)S(1)} %get-tuple-element.129), channel_id=1, source_target_pairs={{0,2},{2,0},{4,6},{6,4},{8,10},{10,8},{12,14},{14,12},{1,3},{3,1},... | collective-permute-start | bytes 675848 | tf_op jit(solution)/shard_map/ppermute | solution.py:771
  30.8 5.9 %collective-permute-start.11 = (bf16[1,176,128]{2,1,0:T(8,128)(2,1)S(1)}, bf16[1,176,128]{2,1,0:T(8,128)(2,1)S(1)}, u32[]{:S(2)}, u32[]{:S(2)}) collective-permute-start(bf16[1,176,128]{2,1,0:T(8,128)(2,1)S(1)} %get-tuple-element.123), channel_id=1, source_target_pairs={{0,12},{2,14},{4,8},{6,10},{8,4},{10,6},{12,0},{14,2},{1,13},{3,15... | collective-permute-start | bytes 135176 | tf_op jit(solution)/shard_map/ppermute | solution.py:771
  31.9 5.8 %collective-permute-start.12 = (bf16[1,176,128]{2,1,0:T(8,128)(2,1)S(1)}, bf16[1,176,128]{2,1,0:T(8,128)(2,1)S(1)}, u32[]{:S(2)}, u32[]{:S(2)}) collective-permute-start(bf16[1,176,128]{2,1,0:T(8,128)(2,1)S(1)} %get-tuple-element.124), channel_id=1, source_target_pairs={{0,8},{2,10},{4,12},{6,14},{8,0},{10,2},{12,4},{14,6},{1,9},{3,11}... | collective-permute-start | bytes 135176 | tf_op jit(solution)/shard_map/ppermute | solution.py:771
  32.4 5.3 %collective-permute-start.13 = (bf16[1,176,128]{2,1,0:T(8,128)(2,1)S(1)}, bf16[1,176,128]{2,1,0:T(8,128)(2,1)S(1)}, u32[]{:S(2)}, u32[]{:S(2)}) collective-permute-start(bf16[1,176,128]{2,1,0:T(8,128)(2,1)S(1)} %get-tuple-element.125), channel_id=1, source_target_pairs={{0,4},{2,6},{4,0},{6,2},{8,12},{10,14},{12,8},{14,10},{1,5},{3,7},... | collective-permute-start | bytes 135176 | tf_op jit(solution)/shard_map/ppermute | solution.py:771
  37.8 5.9 %collective-permute-start.17 = (bf16[1,176,128]{2,1,0:T(8,128)(2,1)S(1)}, bf16[1,176,128]{2,1,0:T(8,128)(2,1)S(1)}, u32[]{:S(2)}, u32[]{:S(2)}) collective-permute-start(bf16[1,176,128]{2,1,0:T(8,128)(2,1)S(1)} %get-tuple-element.130.refs_0_), channel_id=1, source_target_pairs={{0,12},{2,14},{4,8},{6,10},{8,4},{10,6},{12,0},{14,2},{1,13},{3,15... | collective-permute-start | bytes 135176 | tf_op jit(solution)/shard_map/ppermute | solution.py:771
  39.8 5.0 %collective-permute-start.16 = (bf16[1,176,128]{2,1,0:T(8,128)(2,1)S(1)}, bf16[1,176,128]{2,1,0:T(8,128)(2,1)S(1)}, u32[]{:S(2)}, u32[]{:S(2)}) collective-permute-start(bf16[1,176,128]{2,1,0:T(8,128)(2,1)S(1)} %get-tuple-element.130.refs_0_), channel_id=1, source_target_pairs={{0,8},{2,10},{4,12},{6,14},{8,0},{10,2},{12,4},{14,6},{1,9},{3,11}... | collective-permute-start | bytes 135176 | tf_op jit(solution)/shard_map/ppermute | solution.py:771
  45.2 5.6 %collective-permute-start.19 = (bf16[4,176,128]{2,1,0:T(8,128)(2,1)S(1)}, bf16[4,176,128]{2,1,0:T(8,128)(2,1)S(1)}, u32[]{:S(2)}, u32[]{:S(2)}) collective-permute-start(bf16[4,176,128]{2,1,0:T(8,128)(2,1)S(1)} %shard_map.114.refs_0_), channel_id=1, source_target_pairs={{0,2},{2,0},{4,6},{6,4},{8,10},{10,8},{12,14},{14,12},{1,3},{3,1},... | collective-permute-start | bytes 540680 | tf_op jit(solution)/shard_map/ppermute | solution.py:771
  56.1 6.1 %collective-permute-start.26 = (bf16[8,176,128]{2,1,0:T(8,128)(2,1)S(1)}, bf16[8,176,128]{2,1,0:T(8,128)(2,1)S(1)}, u32[]{:S(2)}, u32[]{:S(2)}) collective-permute-start(bf16[8,176,128]{2,1,0:T(8,128)(2,1)S(1)} %get-tuple-element.157), channel_id=1, source_target_pairs={{0,1},{1,0},{2,3},{3,2},{4,5},{5,4},{6,7},{7,6},{8,9},{9,8},{10,11... | collective-permute-start | bytes 1081352 | tf_op jit(solution)/shard_map/ppermute | solution.py:766
  56.3 5.8 %collective-permute-start.25 = (bf16[3,176,128]{2,1,0:T(8,128)(2,1)S(1)}, bf16[3,176,128]{2,1,0:T(8,128)(2,1)S(1)}, u32[]{:S(2)}, u32[]{:S(2)}) collective-permute-start(bf16[3,176,128]{2,1,0:T(8,128)(2,1)S(1)} %get-tuple-element.151), channel_id=1, source_target_pairs={{0,2},{2,0},{4,6},{6,4},{8,10},{10,8},{12,14},{14,12},{1,3},{3,1},... | collective-permute-start | bytes 405512 | tf_op jit(solution)/shard_map/ppermute | solution.py:771
  62.3 8.5 %collective-permute-start.30 = (bf16[5,176,128]{2,1,0:T(8,128)(2,1)S(1)}, bf16[5,176,128]{2,1,0:T(8,128)(2,1)S(1)}, u32[]{:S(2)}, u32[]{:S(2)}) collective-permute-start(bf16[5,176,128]{2,1,0:T(8,128)(2,1)S(1)} %get-tuple-element.163), channel_id=1, source_target_pairs={{0,2},{2,0},{4,6},{6,4},{8,10},{10,8},{12,14},{14,12},{1,3},{3,1},... | collective-permute-start | bytes 675848 | tf_op jit(solution)/shard_map/ppermute | solution.py:771
  63.6 6.2 %collective-permute-start.27 = (bf16[1,176,128]{2,1,0:T(8,128)(2,1)S(1)}, bf16[1,176,128]{2,1,0:T(8,128)(2,1)S(1)}, u32[]{:S(2)}, u32[]{:S(2)}) collective-permute-start(bf16[1,176,128]{2,1,0:T(8,128)(2,1)S(1)} %get-tuple-element.160), channel_id=1, source_target_pairs={{0,12},{2,14},{4,8},{6,10},{8,4},{10,6},{12,0},{14,2},{1,13},{3,15... | collective-permute-start | bytes 135176 | tf_op jit(solution)/shard_map/ppermute | solution.py:771
  65.4 5.4 %collective-permute-start.28 = (bf16[1,176,128]{2,1,0:T(8,128)(2,1)S(1)}, bf16[1,176,128]{2,1,0:T(8,128)(2,1)S(1)}, u32[]{:S(2)}, u32[]{:S(2)}) collective-permute-start(bf16[1,176,128]{2,1,0:T(8,128)(2,1)S(1)} %get-tuple-element.161), channel_id=1, source_target_pairs={{0,8},{2,10},{4,12},{6,14},{8,0},{10,2},{12,4},{14,6},{1,9},{3,11}... | collective-permute-start | bytes 135176 | tf_op jit(solution)/shard_map/ppermute | solution.py:771
  70.9 8.3 %collective-permute-start.32 = (bf16[1,528,128]{2,1,0:T(8,128)(2,1)S(1)}, bf16[1,528,128]{2,1,0:T(8,128)(2,1)S(1)}, u32[]{:S(2)}, u32[]{:S(2)}) collective-permute-start(bf16[1,528,128]{2,1,0:T(8,128)(2,1)S(1)} %get-tuple-element.167), channel_id=1, source_target_pairs={{0,4},{2,6},{4,0},{6,2},{8,12},{10,14},{12,8},{14,10},{1,5},{3,7},... | collective-permute-start | bytes 405512 | tf_op jit(solution)/shard_map/ppermute | solution.py:771
  72.2 5.1 %collective-permute-start.33 = (bf16[1,176,128]{2,1,0:T(8,128)(2,1)S(1)}, bf16[1,176,128]{2,1,0:T(8,128)(2,1)S(1)}, u32[]{:S(2)}, u32[]{:S(2)}) collective-permute-start(bf16[1,176,128]{2,1,0:T(8,128)(2,1)S(1)} %get-tuple-element.166.refs_0_), channel_id=1, source_target_pairs={{0,8},{2,10},{4,12},{6,14},{8,0},{10,2},{12,4},{14,6},{1,9},{3,11}... | collective-permute-start | bytes 135176 | tf_op jit(solution)/shard_map/ppermute | solution.py:771
  73.4 5.8 %collective-permute-start.31 = (bf16[1,176,128]{2,1,0:T(8,128)(2,1)S(1)}, bf16[1,176,128]{2,1,0:T(8,128)(2,1)S(1)}, u32[]{:S(2)}, u32[]{:S(2)}) collective-permute-start(bf16[1,176,128]{2,1,0:T(8,128)(2,1)S(1)} %get-tuple-element.166.refs_0_), channel_id=1, source_target_pairs={{0,12},{2,14},{4,8},{6,10},{8,4},{10,6},{12,0},{14,2},{1,13},{3,15... | collective-permute-start | bytes 135176 | tf_op jit(solution)/shard_map/ppermute | solution.py:771
  79.3 6.1 %collective-permute-start.35 = (bf16[4,176,128]{2,1,0:T(8,128)(2,1)S(1)}, bf16[4,176,128]{2,1,0:T(8,128)(2,1)S(1)}, u32[]{:S(2)}, u32[]{:S(2)}) collective-permute-start(bf16[4,176,128]{2,1,0:T(8,128)(2,1)S(1)} %shard_map.128.refs_0_), channel_id=1, source_target_pairs={{0,2},{2,0},{4,6},{6,4},{8,10},{10,8},{12,14},{14,12},{1,3},{3,1},... | collective-permute-start | bytes 540680 | tf_op jit(solution)/shard_map/ppermute | solution.py:771
  80.2 5.2 %collective-permute-start.34 = (bf16[4,176,128]{2,1,0:T(8,128)(2,1)S(1)}, bf16[4,176,128]{2,1,0:T(8,128)(2,1)S(1)}, u32[]{:S(2)}, u32[]{:S(2)}) collective-permute-start(bf16[4,176,128]{2,1,0:T(8,128)(2,1)S(1)} %shard_map.128.refs_0_), channel_id=1, source_target_pairs={{0,1},{1,0},{2,3},{3,2},{4,5},{5,4},{6,7},{7,6},{8,9},{9,8},{10,11... | collective-permute-start | bytes 540680 | tf_op jit(solution)/shard_map/ppermute | solution.py:766
  80.2 5.2 %collective-permute-start.36 = (bf16[1,176,128]{2,1,0:T(8,128)(2,1)S(1)}, bf16[1,176,128]{2,1,0:T(8,128)(2,1)S(1)}, u32[]{:S(2)}, u32[]{:S(2)}) collective-permute-start(bf16[1,176,128]{2,1,0:T(8,128)(2,1)S(1)} %get-tuple-element.176), channel_id=1, source_target_pairs={{0,8},{2,10},{4,12},{6,14},{8,0},{10,2},{12,4},{14,6},{1,9},{3,11}... | collective-permute-start | bytes 135176 | tf_op jit(solution)/shard_map/ppermute | solution.py:771
  (17 other events, 96.0 us)

commit v4 on v3

--- a/solution.py
+++ b/solution.py
@@ -196,8 +196,9 @@
     return pltpu.VMEM((plan.chips, plan.chunk, LANES), F32)
 
 
-def side_shapes(plan, dtype=F32):
-    return [shaped(len(plan.columns), plan.chunk, LANES, dtype=dtype)] * 2
+def side_shapes(plan, sent_as=F32):
+    dims = (len(plan.columns), plan.chunk, LANES)
+    return [shaped(*dims), shaped(*dims, dtype=sent_as)]
 
 
 def half_product(plan, pairs, side, kept_ref, sent_ref, target, gain_ref=None, bias_ref=None):
@@ -222,7 +223,7 @@
     me = lax.axis_index("latent")
     for place, column in enumerate(plan.columns):
         kept_ref[place] = target[me ^ column]
-        sent_ref[place] = target[me ^ column ^ 1]
+        sent_ref[place] = target[me ^ column ^ 1].astype(sent_ref.dtype)
 
 
 def bring_encoder_body(dict_hbm, vectors_hbm, dict_ref, bias_ref, decoder_ref, gain_ref, sems):
@@ -279,7 +280,7 @@
         [
             shaped(plan.rows, plan.width, dtype=BF16),
             shaped(plan.rows, latents, dtype=BF16),
-            *side_shapes(plan),
+            *side_shapes(plan, BF16),
         ],
         (*own, *other, dictionary, encoder_bias, gain),
         [both_scratch(plan), chunk_scratch(plan)],
@@ -492,7 +493,7 @@
 
 
 def add_sent_body(mine_ref, theirs_ref, first_ref, rest_ref):
-    total = (mine_ref[...] + theirs_ref[...]).astype(BF16)
+    total = (mine_ref[...] + theirs_ref[...].astype(F32)).astype(BF16)
     first_ref[...] = total[:1]
     rest_ref[...] = total[1:]
 

time: 90.9 us -> 91.1 us (level)
  no operation moved by 1% of the time
where the time goes in v4:
time: 91.1 us; the launch traced here: 90.9 us
  waiting for transfers between devices  37.2 us (41%)
  starting transfers between devices  35.6 us (39%)
  Pallas kernels  15.2 us (17%)
  other arithmetic  1.74 us (2%)
  between operations  1.05 us (1%)
    ppermute x25, waiting for transfers between devices, partner_swap(): return lax.ppermute(value, 'latent', [(i, i ^ bits) for i in range(size)])  34.2 us
    ppermute x25, starting transfers between devices, partner_swap(): return lax.ppermute(value, 'latent', [(i, i ^ bits) for i in range(size)])  33.6 us
    pallas_call x29, Pallas kernels, call(): pl.pallas_call(body, out_shape=out_shapes, in_specs=[ONCHIP] * len(operan...  13.5 us
    ppermute x13, waiting for transfers between devices, swap(): lax.ppermute(value, 'hidden', [(i, (i + 1) % size) for i in range(size)])  3.08 us
    ppermute x13, starting transfers between devices, swap(): lax.ppermute(value, 'hidden', [(i, (i + 1) % size) for i in range(size)])  2.06 us
  transfers between devices with their start and end apart: 38, of which 20 were waited for; matrix products, arithmetic and copies ran while one was open for 1% of the time, Pallas kernels for 9%

profile of v4, /device:TPU:0, one launch (start us, length us, event | category | flops | bytes accessed | tf_op | source)
XLA Modules:
  0.0 90.9 jit_solution(6205161234990544185)
XLA Ops:
  1.7 5.1 %collective-permute-start.2 = (bf16[1,176,128]{2,1,0:T(8,128)(2,1)S(1)}, bf16[1,176,128]{2,1,0:T(8,128)(2,1)S(1)}, u32[]{:S(2)}, u32[]{:S(2)}) collective-permute-start(bf16[1,176,128]{2,1,0:T(8,128)(2,1)S(1)} %get-tuple-element.94.refs_0_), channel_id=1, source_target_pairs={{0,12},{2,14},{4,8},{6,10},{8,4},{10,6},{12,0},{14,2},{1,13},{3,15... | collective-permute-start | bytes 135176 | tf_op jit(solution)/shard_map/ppermute | solution.py:772
  8.9 2.9 %collective-permute-done.1.refs_2_ = bf16[1,176,128]{2,1,0:T(8,128)(2,1)S(1)} collective-permute-done((bf16[1,176,128]{2,1,0:T(8,128)(2,1)S(1)}, bf16[1,176,128]{2,1,0:T(8,128)(2,1)S(1)}, u32[]{:S(2)}, u32[]{:S(2)}) %collective-permute-start.1) | collective-permute-done | bytes 45088 | tf_op jit(solution)/shard_map/ppermute | solution.py:772
  11.8 1.6 %collective-permute-start.4 = (bf16[4,176,128]{2,1,0:T(8,128)(2,1)S(1)}, bf16[4,176,128]{2,1,0:T(8,128)(2,1)S(1)}, u32[]{:S(2)}, u32[]{:S(2)}) collective-permute-start(bf16[4,176,128]{2,1,0:T(8,128)(2,1)S(1)} %shard_map.105.refs_0_), channel_id=1, source_target_pairs={{0,2},{2,0},{4,6},{6,4},{8,10},{10,8},{12,14},{14,12},{1,3},{3,1},... | collective-permute-start | bytes 540680 | tf_op jit(solution)/shard_map/ppermute | solution.py:772
  13.4 2.0 %collective-permute-start.5 = (bf16[1,176,128]{2,1,0:T(8,128)(2,1)S(1)}, bf16[1,176,128]{2,1,0:T(8,128)(2,1)S(1)}, u32[]{:S(2)}, u32[]{:S(2)}) collective-permute-start(bf16[1,176,128]{2,1,0:T(8,128)(2,1)S(1)} %get-tuple-element.103.refs_0_), channel_id=1, source_target_pairs={{0,8},{2,10},{4,12},{6,14},{8,0},{10,2},{12,4},{14,6},{1,9},{3,11}... | collective-permute-start | bytes 135176 | tf_op jit(solution)/shard_map/ppermute | solution.py:772
  15.4 1.7 %shard_map.106 = (bf16[512,2304]{1,0:T(8,128)(2,1)S(1)}, f32[1,512]{1,0:T(1,128)S(1)}, f32[1,2304]{1,0:T(1,128)S(1)}, f32[1,2304]{1,0:T(1,128)S(1)}) custom-call(bf16[512,2304]{1,0:T(8,128)(2,1)} %dict_hbm, f32[1,5120]{1,0:T(1,128)S(1)} %bitcast.3), custom_call_target="tpu_custom_call" | custom-call | bytes 4718592 | tf_op jit(solution)/shard_map/pallas_call | solution.py:247
  17.1 2.0 %collective-permute-done.5.refs_1_ = bf16[1,176,128]{2,1,0:T(8,128)(2,1)S(1)} collective-permute-done((bf16[1,176,128]{2,1,0:T(8,128)(2,1)S(1)}, bf16[1,176,128]{2,1,0:T(8,128)(2,1)S(1)}, u32[]{:S(2)}, u32[]{:S(2)}) %collective-permute-start.5) | collective-permute-done | bytes 45088 | tf_op jit(solution)/shard_map/ppermute | solution.py:772
  19.3 1.3 %collective-permute-done.6.refs_3_ = bf16[4,176,128]{2,1,0:T(8,128)(2,1)S(1)} collective-permute-done((bf16[4,176,128]{2,1,0:T(8,128)(2,1)S(1)}, bf16[4,176,128]{2,1,0:T(8,128)(2,1)S(1)}, u32[]{:S(2)}, u32[]{:S(2)}) %collective-permute-start.6) | collective-permute-done | bytes 180256 | tf_op jit(solution)/shard_map/ppermute | solution.py:767
  20.6 1.7 %shard_map.108 = (bf16[144,2304]{1,0:T(8,128)(2,1)S(1)}, bf16[144,512]{1,0:T(8,128)(2,1)S(1)}, f32[4,176,128]{2,1,0:T(8,128)S(1)}, bf16[4,176,128]{2,1,0:T(8,128)(2,1)S(1)}) custom-call(bf16[4,176,128]{2,1,0:T(8,128)(2,1)S(1)} %shard_map.105.refs_0_, bf16[4,176,128]{2,1,0:T(8,128)(2,1)S(1)} %collective-permute-done.4.refs_1_, ...), custom_call_target="tpu_custom_call" | custom-call | flops 509607936 | bytes 2359296 | tf_op jit(solution)/shard_map/pallas_call | solution.py:113
  24.9 5.1 %collective-permute-done.9.got_ref = bf16[3,176,128]{2,1,0:T(8,128)(2,1)S(1)} collective-permute-done((bf16[3,176,128]{2,1,0:T(8,128)(2,1)S(1)}, bf16[3,176,128]{2,1,0:T(8,128)(2,1)S(1)}, u32[]{:S(2)}, u32[]{:S(2)}) %collective-permute-start.9) | collective-permute-done | bytes 135200 | tf_op jit(solution)/shard_map/ppermute | solution.py:772
  32.7 2.8 %collective-permute-start.13 = (bf16[1,176,128]{2,1,0:T(8,128)(2,1)S(1)}, bf16[1,176,128]{2,1,0:T(8,128)(2,1)S(1)}, u32[]{:S(2)}, u32[]{:S(2)}) collective-permute-start(bf16[1,176,128]{2,1,0:T(8,128)(2,1)S(1)} %get-tuple-element.125), channel_id=1, source_target_pairs={{0,4},{2,6},{4,0},{6,2},{8,12},{10,14},{12,8},{14,10},{1,5},{3,7},... | collective-permute-start | bytes 135176 | tf_op jit(solution)/shard_map/ppermute | solution.py:772
  35.5 1.5 %collective-permute-done.11.refs_2_ = bf16[1,176,128]{2,1,0:T(8,128)(2,1)S(1)} collective-permute-done((bf16[1,176,128]{2,1,0:T(8,128)(2,1)S(1)}, bf16[1,176,128]{2,1,0:T(8,128)(2,1)S(1)}, u32[]{:S(2)}, u32[]{:S(2)}) %collective-permute-start.11) | collective-permute-done | bytes 45088 | tf_op jit(solution)/shard_map/ppermute | solution.py:772
  38.0 2.0 %collective-permute-start.17 = (bf16[1,176,128]{2,1,0:T(8,128)(2,1)S(1)}, bf16[1,176,128]{2,1,0:T(8,128)(2,1)S(1)}, u32[]{:S(2)}, u32[]{:S(2)}) collective-permute-start(bf16[1,176,128]{2,1,0:T(8,128)(2,1)S(1)} %get-tuple-element.130.refs_0_), channel_id=1, source_target_pairs={{0,12},{2,14},{4,8},{6,10},{8,4},{10,6},{12,0},{14,2},{1,13},{3,15... | collective-permute-start | bytes 135176 | tf_op jit(solution)/shard_map/ppermute | solution.py:772
  41.1 1.4 %collective-permute-start.15 = (bf16[1,176,128]{2,1,0:T(8,128)(2,1)S(1)}, bf16[1,176,128]{2,1,0:T(8,128)(2,1)S(1)}, u32[]{:S(2)}, u32[]{:S(2)}) collective-permute-start(bf16[1,176,128]{2,1,0:T(8,128)(2,1)S(1)} %get-tuple-element.130.refs_0_), channel_id=1, source_target_pairs={{0,4},{2,6},{4,0},{6,2},{8,12},{10,14},{12,8},{14,10},{1,5},{3,7},... | collective-permute-start | bytes 135176 | tf_op jit(solution)/shard_map/ppermute | solution.py:772
  48.0 3.0 %collective-permute-done.19.refs_1_ = bf16[4,176,128]{2,1,0:T(8,128)(2,1)S(1)} collective-permute-done((bf16[4,176,128]{2,1,0:T(8,128)(2,1)S(1)}, bf16[4,176,128]{2,1,0:T(8,128)(2,1)S(1)}, u32[]{:S(2)}, u32[]{:S(2)}) %collective-permute-start.19) | collective-permute-done | bytes 180256 | tf_op jit(solution)/shard_map/ppermute | solution.py:772
  52.4 1.6 %shard_map.119 = (bf16[144,2304]{1,0:T(8,128)(2,1)S(1)}, f32[144,1]{1,0:T(8,128)S(1)}, bf16[144,512]{1,0:T(8,128)(2,1)S(1)}, bf16[144,512]{1,0:T(8,128)(2,1)S(1)...) custom-call(bf16[8,176,128]{2,1,0:T(8,128)(2,1)S(1)} %shard_map.116.other_ref, ...), custom_call_target="tpu_custom_call" | custom-call | flops 1019215872 | bytes 4718592 | tf_op jit(solution)/shard_map/pallas_call | solution.py:113
  58.4 4.0 %collective-permute-done.25.got_ref = bf16[3,176,128]{2,1,0:T(8,128)(2,1)S(1)} collective-permute-done((bf16[3,176,128]{2,1,0:T(8,128)(2,1)S(1)}, bf16[3,176,128]{2,1,0:T(8,128)(2,1)S(1)}, u32[]{:S(2)}, u32[]{:S(2)}) %collective-permute-start.25) | collective-permute-done | bytes 135200 | tf_op jit(solution)/shard_map/ppermute | solution.py:772
  63.8 1.9 %collective-permute-start.27 = (bf16[1,176,128]{2,1,0:T(8,128)(2,1)S(1)}, bf16[1,176,128]{2,1,0:T(8,128)(2,1)S(1)}, u32[]{:S(2)}, u32[]{:S(2)}) collective-permute-start(bf16[1,176,128]{2,1,0:T(8,128)(2,1)S(1)} %get-tuple-element.160), channel_id=1, source_target_pairs={{0,12},{2,14},{4,8},{6,10},{8,4},{10,6},{12,0},{14,2},{1,13},{3,15... | collective-permute-start | bytes 135176 | tf_op jit(solution)/shard_map/ppermute | solution.py:772
  66.3 1.9 %collective-permute-start.29 = (bf16[1,176,128]{2,1,0:T(8,128)(2,1)S(1)}, bf16[1,176,128]{2,1,0:T(8,128)(2,1)S(1)}, u32[]{:S(2)}, u32[]{:S(2)}) collective-permute-start(bf16[1,176,128]{2,1,0:T(8,128)(2,1)S(1)} %get-tuple-element.162), channel_id=1, source_target_pairs={{0,4},{2,6},{4,0},{6,2},{8,12},{10,14},{12,8},{14,10},{1,5},{3,7},... | collective-permute-start | bytes 135176 | tf_op jit(solution)/shard_map/ppermute | solution.py:772
  68.2 1.8 %collective-permute-done.27.refs_2_ = bf16[1,176,128]{2,1,0:T(8,128)(2,1)S(1)} collective-permute-done((bf16[1,176,128]{2,1,0:T(8,128)(2,1)S(1)}, bf16[1,176,128]{2,1,0:T(8,128)(2,1)S(1)}, u32[]{:S(2)}, u32[]{:S(2)}) %collective-permute-start.27) | collective-permute-done | bytes 45088 | tf_op jit(solution)/shard_map/ppermute | solution.py:772
  73.6 2.0 %collective-permute-start.31 = (bf16[1,176,128]{2,1,0:T(8,128)(2,1)S(1)}, bf16[1,176,128]{2,1,0:T(8,128)(2,1)S(1)}, u32[]{:S(2)}, u32[]{:S(2)}) collective-permute-start(bf16[1,176,128]{2,1,0:T(8,128)(2,1)S(1)} %get-tuple-element.166.refs_0_), channel_id=1, source_target_pairs={{0,12},{2,14},{4,8},{6,10},{8,4},{10,6},{12,0},{14,2},{1,13},{3,15... | collective-permute-start | bytes 135176 | tf_op jit(solution)/shard_map/ppermute | solution.py:772
  75.6 2.0 %collective-permute-done.33.refs_2_ = bf16[1,176,128]{2,1,0:T(8,128)(2,1)S(1)} collective-permute-done((bf16[1,176,128]{2,1,0:T(8,128)(2,1)S(1)}, bf16[1,176,128]{2,1,0:T(8,128)(2,1)S(1)}, u32[]{:S(2)}, u32[]{:S(2)}) %collective-permute-start.33) | collective-permute-done | bytes 45088 | tf_op jit(solution)/shard_map/ppermute | solution.py:772
  77.5 1.9 %collective-permute-done.31.refs_3_ = bf16[1,176,128]{2,1,0:T(8,128)(2,1)S(1)} collective-permute-done((bf16[1,176,128]{2,1,0:T(8,128)(2,1)S(1)}, bf16[1,176,128]{2,1,0:T(8,128)(2,1)S(1)}, u32[]{:S(2)}, u32[]{:S(2)}) %collective-permute-start.31) | collective-permute-done | bytes 45088 | tf_op jit(solution)/shard_map/ppermute | solution.py:772
  80.7 5.0 %collective-permute-done.36.got_ref = bf16[1,176,128]{2,1,0:T(8,128)(2,1)S(1)} collective-permute-done((bf16[1,176,128]{2,1,0:T(8,128)(2,1)S(1)}, bf16[1,176,128]{2,1,0:T(8,128)(2,1)S(1)}, u32[]{:S(2)}, u32[]{:S(2)}) %collective-permute-start.36) | collective-permute-done | bytes 45088 | tf_op jit(solution)/shard_map/ppermute | solution.py:772
  87.1 3.7 %shard_map.133 = bf16[512,2304]{1,0:T(8,128)(2,1)} custom-call(bf16[8,176,128]{2,1,0:T(8,128)(2,1)S(1)} %shard_map.130.own_ref, bf16[8,176,128]{2,1,0:T(8,128)(2,1)S(1)} %shard_map.131.other_ref, bf16[144,2304]{1,0:T(8,128)(2,1)S(1)} %get-tuple-element.180.scaled_ref, f32[144,2304]{1,0:T(8,128)S(1)} %get-tuple-element.183.factor_ref, ...), custom_call_target="tpu_custom_call" | custom-call | flops 1019215872 | bytes 4718592 | tf_op jit(solution)/shard_map/pallas_call | solution.py:113
  (90 shorter events, 30.3 us)
Async XLA Ops:
  1.7 7.2 %collective-permute-start.2 = (bf16[1,176,128]{2,1,0:T(8,128)(2,1)S(1)}, bf16[1,176,128]{2,1,0:T(8,128)(2,1)S(1)}, u32[]{:S(2)}, u32[]{:S(2)}) collective-permute-start(bf16[1,176,128]{2,1,0:T(8,128)(2,1)S(1)} %get-tuple-element.94.refs_0_), channel_id=1, source_target_pairs={{0,12},{2,14},{4,8},{6,10},{8,4},{10,6},{12,0},{14,2},{1,13},{3,15... | collective-permute-start | bytes 135176 | tf_op jit(solution)/shard_map/ppermute | solution.py:772
  11.8 7.3 %collective-permute-start.4 = (bf16[4,176,128]{2,1,0:T(8,128)(2,1)S(1)}, bf16[4,176,128]{2,1,0:T(8,128)(2,1)S(1)}, u32[]{:S(2)}, u32[]{:S(2)}) collective-permute-start(bf16[4,176,128]{2,1,0:T(8,128)(2,1)S(1)} %shard_map.105.refs_0_), channel_id=1, source_target_pairs={{0,2},{2,0},{4,6},{6,4},{8,10},{10,8},{12,14},{14,12},{1,3},{3,1},... | collective-permute-start | bytes 540680 | tf_op jit(solution)/shard_map/ppermute | solution.py:772
  13.4 5.8 %collective-permute-start.3 = (bf16[4,176,128]{2,1,0:T(8,128)(2,1)S(1)}, bf16[4,176,128]{2,1,0:T(8,128)(2,1)S(1)}, u32[]{:S(2)}, u32[]{:S(2)}) collective-permute-start(bf16[4,176,128]{2,1,0:T(8,128)(2,1)S(1)} %shard_map.105.refs_0_), channel_id=1, source_target_pairs={{0,1},{1,0},{2,3},{3,2},{4,5},{5,4},{6,7},{7,6},{8,9},{9,8},{10,11... | collective-permute-start | bytes 540680 | tf_op jit(solution)/shard_map/ppermute | solution.py:767
  13.4 5.7 %collective-permute-start.5 = (bf16[1,176,128]{2,1,0:T(8,128)(2,1)S(1)}, bf16[1,176,128]{2,1,0:T(8,128)(2,1)S(1)}, u32[]{:S(2)}, u32[]{:S(2)}) collective-permute-start(bf16[1,176,128]{2,1,0:T(8,128)(2,1)S(1)} %get-tuple-element.103.refs_0_), channel_id=1, source_target_pairs={{0,8},{2,10},{4,12},{6,14},{8,0},{10,2},{12,4},{14,6},{1,9},{3,11}... | collective-permute-start | bytes 135176 | tf_op jit(solution)/shard_map/ppermute | solution.py:772
  22.3 7.7 %collective-permute-start.7 = (f32[4,176,128]{2,1,0:T(8,128)S(1)}, f32[4,176,128]{2,1,0:T(8,128)S(1)}, u32[]{:S(2)}, u32[]{:S(2)}) collective-permute-start(f32[4,176,128]{2,1,0:T(8,128)S(1)} %get-tuple-element.112), channel_id=1, source_target_pairs={{0,1},{1,0},{2,3},{3,2},{4,5},{5,4},{6,7},{7,6},{8,9},{9,8},{10,11... | collective-permute-start | bytes 1081352 | tf_op jit(solution)/shard_map/ppermute | solution.py:767
  24.3 5.7 %collective-permute-start.9 = (bf16[3,176,128]{2,1,0:T(8,128)(2,1)S(1)}, bf16[3,176,128]{2,1,0:T(8,128)(2,1)S(1)}, u32[]{:S(2)}, u32[]{:S(2)}) collective-permute-start(bf16[3,176,128]{2,1,0:T(8,128)(2,1)S(1)} %get-tuple-element.117), channel_id=1, source_target_pairs={{0,2},{2,0},{4,6},{6,4},{8,10},{10,8},{12,14},{14,12},{1,3},{3,1},... | collective-permute-start | bytes 405512 | tf_op jit(solution)/shard_map/ppermute | solution.py:772
  24.9 5.2 %collective-permute-start.10 = (bf16[2,176,128]{2,1,0:T(8,128)(2,1)S(1)}, bf16[2,176,128]{2,1,0:T(8,128)(2,1)S(1)}, u32[]{:S(2)}, u32[]{:S(2)}) collective-permute-start(bf16[2,176,128]{2,1,0:T(8,128)(2,1)S(1)} %shard_map.107.here_ref), channel_id=1, source_target_pairs={{0,4},{2,6},{4,0},{6,2},{8,12},{10,14},{12,8},{14,10},{1,5},{3,7},... | collective-permute-start | bytes 270344 | tf_op jit(solution)/shard_map/ppermute | solution.py:772
  30.2 7.8 %collective-permute-start.14 = (bf16[5,176,128]{2,1,0:T(8,128)(2,1)S(1)}, bf16[5,176,128]{2,1,0:T(8,128)(2,1)S(1)}, u32[]{:S(2)}, u32[]{:S(2)}) collective-permute-start(bf16[5,176,128]{2,1,0:T(8,128)(2,1)S(1)} %get-tuple-element.129), channel_id=1, source_target_pairs={{0,2},{2,0},{4,6},{6,4},{8,10},{10,8},{12,14},{14,12},{1,3},{3,1},... | collective-permute-start | bytes 675848 | tf_op jit(solution)/shard_map/ppermute | solution.py:772
  31.1 5.9 %collective-permute-start.11 = (bf16[1,176,128]{2,1,0:T(8,128)(2,1)S(1)}, bf16[1,176,128]{2,1,0:T(8,128)(2,1)S(1)}, u32[]{:S(2)}, u32[]{:S(2)}) collective-permute-start(bf16[1,176,128]{2,1,0:T(8,128)(2,1)S(1)} %get-tuple-element.123), channel_id=1, source_target_pairs={{0,12},{2,14},{4,8},{6,10},{8,4},{10,6},{12,0},{14,2},{1,13},{3,15... | collective-permute-start | bytes 135176 | tf_op jit(solution)/shard_map/ppermute | solution.py:772
  32.1 5.8 %collective-permute-start.12 = (bf16[1,176,128]{2,1,0:T(8,128)(2,1)S(1)}, bf16[1,176,128]{2,1,0:T(8,128)(2,1)S(1)}, u32[]{:S(2)}, u32[]{:S(2)}) collective-permute-start(bf16[1,176,128]{2,1,0:T(8,128)(2,1)S(1)} %get-tuple-element.124), channel_id=1, source_target_pairs={{0,8},{2,10},{4,12},{6,14},{8,0},{10,2},{12,4},{14,6},{1,9},{3,11}... | collective-permute-start | bytes 135176 | tf_op jit(solution)/shard_map/ppermute | solution.py:772
  32.7 5.3 %collective-permute-start.13 = (bf16[1,176,128]{2,1,0:T(8,128)(2,1)S(1)}, bf16[1,176,128]{2,1,0:T(8,128)(2,1)S(1)}, u32[]{:S(2)}, u32[]{:S(2)}) collective-permute-start(bf16[1,176,128]{2,1,0:T(8,128)(2,1)S(1)} %get-tuple-element.125), channel_id=1, source_target_pairs={{0,4},{2,6},{4,0},{6,2},{8,12},{10,14},{12,8},{14,10},{1,5},{3,7},... | collective-permute-start | bytes 135176 | tf_op jit(solution)/shard_map/ppermute | solution.py:772
  38.0 5.9 %collective-permute-start.17 = (bf16[1,176,128]{2,1,0:T(8,128)(2,1)S(1)}, bf16[1,176,128]{2,1,0:T(8,128)(2,1)S(1)}, u32[]{:S(2)}, u32[]{:S(2)}) collective-permute-start(bf16[1,176,128]{2,1,0:T(8,128)(2,1)S(1)} %get-tuple-element.130.refs_0_), channel_id=1, source_target_pairs={{0,12},{2,14},{4,8},{6,10},{8,4},{10,6},{12,0},{14,2},{1,13},{3,15... | collective-permute-start | bytes 135176 | tf_op jit(solution)/shard_map/ppermute | solution.py:772
  45.4 5.6 %collective-permute-start.19 = (bf16[4,176,128]{2,1,0:T(8,128)(2,1)S(1)}, bf16[4,176,128]{2,1,0:T(8,128)(2,1)S(1)}, u32[]{:S(2)}, u32[]{:S(2)}) collective-permute-start(bf16[4,176,128]{2,1,0:T(8,128)(2,1)S(1)} %shard_map.114.refs_0_), channel_id=1, source_target_pairs={{0,2},{2,0},{4,6},{6,4},{8,10},{10,8},{12,14},{14,12},{1,3},{3,1},... | collective-permute-start | bytes 540680 | tf_op jit(solution)/shard_map/ppermute | solution.py:772
  56.3 6.1 %collective-permute-start.26 = (bf16[8,176,128]{2,1,0:T(8,128)(2,1)S(1)}, bf16[8,176,128]{2,1,0:T(8,128)(2,1)S(1)}, u32[]{:S(2)}, u32[]{:S(2)}) collective-permute-start(bf16[8,176,128]{2,1,0:T(8,128)(2,1)S(1)} %get-tuple-element.157), channel_id=1, source_target_pairs={{0,1},{1,0},{2,3},{3,2},{4,5},{5,4},{6,7},{7,6},{8,9},{9,8},{10,11... | collective-permute-start | bytes 1081352 | tf_op jit(solution)/shard_map/ppermute | solution.py:767
  56.5 5.8 %collective-permute-start.25 = (bf16[3,176,128]{2,1,0:T(8,128)(2,1)S(1)}, bf16[3,176,128]{2,1,0:T(8,128)(2,1)S(1)}, u32[]{:S(2)}, u32[]{:S(2)}) collective-permute-start(bf16[3,176,128]{2,1,0:T(8,128)(2,1)S(1)} %get-tuple-element.151), channel_id=1, source_target_pairs={{0,2},{2,0},{4,6},{6,4},{8,10},{10,8},{12,14},{14,12},{1,3},{3,1},... | collective-permute-start | bytes 405512 | tf_op jit(solution)/shard_map/ppermute | solution.py:772
  62.5 8.5 %collective-permute-start.30 = (bf16[5,176,128]{2,1,0:T(8,128)(2,1)S(1)}, bf16[5,176,128]{2,1,0:T(8,128)(2,1)S(1)}, u32[]{:S(2)}, u32[]{:S(2)}) collective-permute-start(bf16[5,176,128]{2,1,0:T(8,128)(2,1)S(1)} %get-tuple-element.163), channel_id=1, source_target_pairs={{0,2},{2,0},{4,6},{6,4},{8,10},{10,8},{12,14},{14,12},{1,3},{3,1},... | collective-permute-start | bytes 675848 | tf_op jit(solution)/shard_map/ppermute | solution.py:772
  63.8 6.2 %collective-permute-start.27 = (bf16[1,176,128]{2,1,0:T(8,128)(2,1)S(1)}, bf16[1,176,128]{2,1,0:T(8,128)(2,1)S(1)}, u32[]{:S(2)}, u32[]{:S(2)}) collective-permute-start(bf16[1,176,128]{2,1,0:T(8,128)(2,1)S(1)} %get-tuple-element.160), channel_id=1, source_target_pairs={{0,12},{2,14},{4,8},{6,10},{8,4},{10,6},{12,0},{14,2},{1,13},{3,15... | collective-permute-start | bytes 135176 | tf_op jit(solution)/shard_map/ppermute | solution.py:772
  65.7 5.4 %collective-permute-start.28 = (bf16[1,176,128]{2,1,0:T(8,128)(2,1)S(1)}, bf16[1,176,128]{2,1,0:T(8,128)(2,1)S(1)}, u32[]{:S(2)}, u32[]{:S(2)}) collective-permute-start(bf16[1,176,128]{2,1,0:T(8,128)(2,1)S(1)} %get-tuple-element.161), channel_id=1, source_target_pairs={{0,8},{2,10},{4,12},{6,14},{8,0},{10,2},{12,4},{14,6},{1,9},{3,11}... | collective-permute-start | bytes 135176 | tf_op jit(solution)/shard_map/ppermute | solution.py:772
  71.1 8.3 %collective-permute-start.32 = (bf16[1,528,128]{2,1,0:T(8,128)(2,1)S(1)}, bf16[1,528,128]{2,1,0:T(8,128)(2,1)S(1)}, u32[]{:S(2)}, u32[]{:S(2)}) collective-permute-start(bf16[1,528,128]{2,1,0:T(8,128)(2,1)S(1)} %get-tuple-element.167), channel_id=1, source_target_pairs={{0,4},{2,6},{4,0},{6,2},{8,12},{10,14},{12,8},{14,10},{1,5},{3,7},... | collective-permute-start | bytes 405512 | tf_op jit(solution)/shard_map/ppermute | solution.py:772
  72.4 5.1 %collective-permute-start.33 = (bf16[1,176,128]{2,1,0:T(8,128)(2,1)S(1)}, bf16[1,176,128]{2,1,0:T(8,128)(2,1)S(1)}, u32[]{:S(2)}, u32[]{:S(2)}) collective-permute-start(bf16[1,176,128]{2,1,0:T(8,128)(2,1)S(1)} %get-tuple-element.166.refs_0_), channel_id=1, source_target_pairs={{0,8},{2,10},{4,12},{6,14},{8,0},{10,2},{12,4},{14,6},{1,9},{3,11}... | collective-permute-start | bytes 135176 | tf_op jit(solution)/shard_map/ppermute | solution.py:772
  73.6 5.8 %collective-permute-start.31 = (bf16[1,176,128]{2,1,0:T(8,128)(2,1)S(1)}, bf16[1,176,128]{2,1,0:T(8,128)(2,1)S(1)}, u32[]{:S(2)}, u32[]{:S(2)}) collective-permute-start(bf16[1,176,128]{2,1,0:T(8,128)(2,1)S(1)} %get-tuple-element.166.refs_0_), channel_id=1, source_target_pairs={{0,12},{2,14},{4,8},{6,10},{8,4},{10,6},{12,0},{14,2},{1,13},{3,15... | collective-permute-start | bytes 135176 | tf_op jit(solution)/shard_map/ppermute | solution.py:772
  79.5 6.1 %collective-permute-start.35 = (bf16[4,176,128]{2,1,0:T(8,128)(2,1)S(1)}, bf16[4,176,128]{2,1,0:T(8,128)(2,1)S(1)}, u32[]{:S(2)}, u32[]{:S(2)}) collective-permute-start(bf16[4,176,128]{2,1,0:T(8,128)(2,1)S(1)} %shard_map.128.refs_0_), channel_id=1, source_target_pairs={{0,2},{2,0},{4,6},{6,4},{8,10},{10,8},{12,14},{14,12},{1,3},{3,1},... | collective-permute-start | bytes 540680 | tf_op jit(solution)/shard_map/ppermute | solution.py:772
  80.4 5.2 %collective-permute-start.34 = (bf16[4,176,128]{2,1,0:T(8,128)(2,1)S(1)}, bf16[4,176,128]{2,1,0:T(8,128)(2,1)S(1)}, u32[]{:S(2)}, u32[]{:S(2)}) collective-permute-start(bf16[4,176,128]{2,1,0:T(8,128)(2,1)S(1)} %shard_map.128.refs_0_), channel_id=1, source_target_pairs={{0,1},{1,0},{2,3},{3,2},{4,5},{5,4},{6,7},{7,6},{8,9},{9,8},{10,11... | collective-permute-start | bytes 540680 | tf_op jit(solution)/shard_map/ppermute | solution.py:767
  80.4 5.2 %collective-permute-start.36 = (bf16[1,176,128]{2,1,0:T(8,128)(2,1)S(1)}, bf16[1,176,128]{2,1,0:T(8,128)(2,1)S(1)}, u32[]{:S(2)}, u32[]{:S(2)}) collective-permute-start(bf16[1,176,128]{2,1,0:T(8,128)(2,1)S(1)} %get-tuple-element.176), channel_id=1, source_target_pairs={{0,8},{2,10},{4,12},{6,14},{8,0},{10,2},{12,4},{14,6},{1,9},{3,11}... | collective-permute-start | bytes 135176 | tf_op jit(solution)/shard_map/ppermute | solution.py:772
  (17 other events, 99.1 us)
